TPU v7x, 256 devices: a whole 4x4x8 slice. The times are simulated.
256 devices in a mesh: row: 16 (over y, x), col: 16 (over z, core).
Axes of the slice: x: 4, y: 4, z: 8, core: 2. Of those that a mesh axis runs over, the one named last changes fastest.
Arguments:
- queries: bfloat16 [2, 256, 256, 2240], P(None, 'row', 'col'), may hold values from -6 to 6
- key_rows_per_head: bfloat16 [2, 256, 256, 2240], P(None, 'row', 'col'), may hold values from -1000 to 1000
- value_rows_per_head: bfloat16 [2, 256, 256, 2240], P(None, 'row', 'col'), may hold values from -13 to 13
- latent_projection_weight: bfloat16 [2240, 32], replicated, may hold values from -0.125 to 0.125
- entry_conv_weight: bfloat16 [3, 3, 32, 512], replicated, may hold values from -0.375 to 0.375
- residual_norm_gain: float32 [512], replicated, may hold values from 0.1 to 1.9
- residual_conv_weight: bfloat16 [3, 3, 512, 512], replicated, may hold values from -0.09375 to 0.09375
- upscale_conv_weight: bfloat16 [3, 3, 512, 512], replicated, may hold values from -0.09375 to 0.09375
Outputs:
- decoded_image: bfloat16 [2, 512, 512, 512], P(None, 'row', 'col')
All inputs are finite; a program needn't handle non-finite values.
Results may differ from a plain program's by a relative error of at most 0.017.
Values may be sent and summed in bfloat16 or wider, within the bound.
No kernel may reach another device: no remote copies, remote signals or barrier semaphores. Data moves between devices by JAX's collectives and lax.ppermute only.
A program may use at most 128 MiB of HBM per device.

v0:
```python
import functools

import jax
import jax.numpy as jnp
from jax import lax
from jax.experimental import pallas as pl
from jax.experimental.pallas import tpu as pltpu
from jax.sharding import PartitionSpec as P

HEAD = 32
NORM_EPS = 1e-06
LANES = 128
PACK = 2560
KS_AT = 2304


def sums_kernel(scale, _, k_ref, v_ref, out_ref):
    tokens, width = k_ref.shape[1:]
    ones = jnp.ones((tokens, LANES), jnp.bfloat16)
    lane = lax.broadcasted_iota(jnp.int32, (HEAD, LANES), 1)
    parts = []
    key_sums = jnp.zeros((HEAD, LANES), jnp.float32)
    for start in range(0, width, LANES):
        size = min(LANES, width - start)
        keys = jnp.maximum(k_ref[0, :, start : start + size], 0)
        values = jnp.concatenate([v_ref[0, :, start : start + size], ones], axis=1)
        product = lax.dot_general(
            keys, values, (((0,), (0,)), ((), ())), preferred_element_type=jnp.float32
        )
        packed = jnp.zeros((HEAD, size), jnp.float32)
        for h in range(size // HEAD):
            rows = product[h * HEAD : (h + 1) * HEAD]
            packed = jnp.where(lane[:, :size] // HEAD == h, rows[:, :size], packed)
            key_sums = jnp.where(lane == start // HEAD + h, rows[:, size:], key_sums)
        parts.append(packed)
    parts.append(jnp.zeros((HEAD, KS_AT - width), jnp.float32))
    parts.append(key_sums)
    parts.append(jnp.zeros((HEAD, PACK - KS_AT - LANES), jnp.float32))
    total = (jnp.concatenate(parts, axis=1) * scale).astype(jnp.bfloat16)
    half = PACK // 2
    for r in range(2):
        for c in range(2):
            out_ref[2 * r + c] = total[16 * r : 16 * r + 16, half * c : half * (c + 1)]


def image_sums(keys, values, image, scale):
    images, tokens, width = keys.shape
    spec = pl.BlockSpec((1, tokens, width), lambda i, at: (at[0], 0, 0))
    return pl.pallas_call(
        functools.partial(sums_kernel, scale),
        out_shape=jax.ShapeDtypeStruct((4, 16, PACK // 2), jnp.bfloat16),
        grid_spec=pltpu.PrefetchScalarGridSpec(
            num_scalar_prefetch=1,
            grid=(1,),
            in_specs=[spec, spec],
            out_specs=pl.BlockSpec((4, 16, PACK // 2), lambda i, at: (0, 0, 0)),
        ),
        compiler_params=pltpu.CompilerParams(vmem_limit_bytes=32 << 20),
        cost_estimate=pl.CostEstimate(flops=2 * tokens * width * 256, bytes_accessed=4 * tokens * width, transcendentals=0),
        name="image_sums",
    )(image.reshape(1), keys, values)


def attend_kernel(q_ref, kv_ref, w_ref, out_ref):
    tokens, width = q_ref.shape[1:]
    group = 2 * LANES
    same = (
        lax.broadcasted_iota(jnp.int32, (group, group), 0) // HEAD
        == lax.broadcasted_iota(jnp.int32, (group, group), 1) // HEAD
    )
    kv = jnp.concatenate(
        [jnp.concatenate([kv_ref[0, 2 * r + c] for c in range(2)], axis=1) for r in range(2)], axis=0
    )
    key_means = kv[:, KS_AT : KS_AT + LANES]
    head_of = lax.broadcasted_iota(jnp.int32, (LANES, group), 0)
    lane_head = lax.broadcasted_iota(jnp.int32, (LANES, group), 1) // HEAD
    squares = jnp.zeros((tokens, 1), jnp.float32)
    latent = jnp.zeros((tokens, w_ref.shape[1]), jnp.float32)
    for start in range(0, width, group):
        size = min(group, width - start)
        spread = (head_of == lane_head + start // HEAD).astype(jnp.bfloat16)[:, :size]
        means = jnp.dot(key_means, spread, preferred_element_type=jnp.float32).astype(jnp.bfloat16)
        here = same[:size, :size]
        zero = jnp.zeros((size, size), jnp.bfloat16)
        numerator_weights = jnp.where(
            here, jnp.concatenate([kv[:, start : start + size]] * (size // HEAD), axis=0), zero
        )
        denominator_weights = jnp.where(
            here, jnp.concatenate([means] * (size // HEAD), axis=0), zero
        )
        query = jnp.maximum(q_ref[0, :, start : start + size], 0)
        numerator = jnp.dot(query, numerator_weights, preferred_element_type=jnp.float32)
        denominator = jnp.dot(query, denominator_weights, preferred_element_type=jnp.float32)
        bound = jnp.maximum(denominator, 1.0)
        inverse = pl.reciprocal(bound, approx=True)
        attended = numerator * (inverse * (2.0 - bound * inverse))
        squares += jnp.sum(attended * attended, axis=1, keepdims=True)
        latent += jnp.dot(
            attended.astype(jnp.bfloat16),
            w_ref[start : start + size],
            preferred_element_type=jnp.float32,
        )
    out_ref[0] = (latent * lax.rsqrt(squares / width + NORM_EPS)).astype(jnp.bfloat16)


def attend(queries, kv, weight):
    images, tokens, width = queries.shape
    channels = weight.shape[1]
    return pl.pallas_call(
        attend_kernel,
        out_shape=jax.ShapeDtypeStruct((images, tokens, channels), jnp.bfloat16),
        grid=(images,),
        in_specs=[
            pl.BlockSpec((1, tokens, width), lambda i: (i, 0, 0)),
            pl.BlockSpec((1, 4, 16, PACK // 2), lambda i: (i, 0, 0, 0)),
            pl.BlockSpec((width, channels), lambda i: (0, 0)),
        ],
        out_specs=pl.BlockSpec((1, tokens, channels), lambda i: (i, 0, 0)),
        compiler_params=pltpu.CompilerParams(vmem_limit_bytes=32 << 20),
        cost_estimate=pl.CostEstimate(flops=2 * images * tokens * width * 512, bytes_accessed=2 * images * tokens * width, transcendentals=0),
        name="attend",
    )(queries, kv, weight)


def xor_pairs(distance):
    return [(i, i ^ distance) for i in range(16)]


def exchange_group(value, axis, distances):
    arrived = [lax.ppermute(value, axis, xor_pairs(d)) for d in distances]
    total = value.astype(jnp.float32)
    for part in arrived:
        total = total + part.astype(jnp.float32)
    return total.astype(jnp.bfloat16)


def sum_over_mesh(mine, other):
    at_x = lax.axis_index("row") % 4
    core = lax.axis_index("col") % 2
    arrived = lax.ppermute(other, "col", xor_pairs(1))
    image = mine.astype(jnp.float32) + arrived.astype(jnp.float32)
    parts = [
        lax.ppermute(
            lax.dynamic_index_in_dim(image, at_x ^ d, 0, False).astype(jnp.bfloat16), "row", xor_pairs(d)
        )
        for d in (1, 3, 2)
    ]
    total = lax.dynamic_index_in_dim(image, at_x, 0, False)
    for part in parts:
        total = total + part.astype(jnp.float32)
    chunk = exchange_group(total.astype(jnp.bfloat16), "row", (4, 12, 8))
    chunk = exchange_group(chunk, "col", (2,))
    chunk = exchange_group(chunk, "col", (4, 12, 10))
    twin = lax.ppermute(chunk, "col", xor_pairs(1))
    both = jnp.where(core == 0, jnp.stack([chunk, twin]), jnp.stack([twin, chunk]))
    gathered = jnp.stack([both] + [lax.ppermute(both, "row", xor_pairs(d)) for d in (1, 2, 3)])
    return jnp.stack(
        [lax.dynamic_index_in_dim(gathered, at_x ^ c, 0, False) for c in range(4)], axis=1
    )


def extended(value, sides, width):
    for axis, dim in sides:
        devices, length = (lax.axis_size(axis), value.shape[dim])
        up = [(i, (i + 1) % devices) for i in range(devices - 1)]
        down = [(j, i) for i, j in up]
        last = lax.slice_in_dim(value, length - width, length, axis=dim)
        initial = lax.slice_in_dim(value, 0, width, axis=dim)
        before = lax.ppermute(last, axis, up)
        after = lax.ppermute(initial, axis, down)
        value = jnp.concatenate([before, value, after], axis=dim)
    return value


def read(ref, at):
    return jnp.concatenate([ref[c, at, :] for c in range(ref.shape[0])], axis=1)


def write(ref, at, value):
    for c in range(ref.shape[0]):
        ref[c, at, :] = value[:, LANES * c : LANES * (c + 1)]


def decode_kernel(
    tiles, at_ref, lat_ref, entry_ref, gain_ref, residual_ref, upscale_ref, out_ref,
    wide, dec, hid, taps, ref, centre, slope, mix,
):
    tile = 16
    channels = out_ref.shape[-1]
    pitch = 24
    f32, bf16 = jnp.float32, jnp.bfloat16
    rows = tile + 4
    spot = lax.broadcasted_iota(jnp.int32, (2 * pitch, 1), 0) % pitch

    def real(at, axis):
        return (at >= 0) & (at < tile * tiles[axis])

    for i in range(2 * (tile + 6)):
        block = [lat_ref[i, dx : dx + pitch, :] for dx in range(3)]
        wide[pitch * i : pitch * (i + 1)] = jnp.concatenate(block, axis=1).astype(bf16)

    across = real(at_ref[1] * tile - 2 + spot, 1)
    gain = gain_ref[...]
    for y in range(rows):
        at = 2 * pitch * y
        value = jnp.dot(wide[at : at + 2 * pitch], entry_ref[0], preferred_element_type=f32)
        for dy in (1, 2):
            start = at + 2 * pitch * dy
            value += jnp.dot(wide[start : start + 2 * pitch], entry_ref[dy], preferred_element_type=f32)
        value = value.astype(bf16).astype(f32)
        write(dec, pl.ds(at, 2 * pitch), value)
        mean = jnp.mean(value * value, axis=1, keepdims=True)
        scaled = value * lax.rsqrt(mean + NORM_EPS) * gain
        active = 0.5 * scaled * (1.0 + jnp.tanh(0.5 * scaled))
        keep = across & real(at_ref[0] * tile - 2 + y, 0)
        write(hid, pl.ds(at, 2 * pitch), jnp.where(keep, active, 0.0))
    spare = jnp.zeros((8 * pitch, channels), f32)
    write(hid, pl.ds(2 * pitch * rows, 8 * pitch), spare)
    write(dec, pl.ds(2 * pitch * rows, 8 * pitch), spare)

    inner = 2 * (tile + 2)
    main = inner * tile
    edge = 40
    for i in range(2 * rows):
        for dx in range(3):
            piece = read(hid, pl.ds(pitch * i + dx, tile)).astype(bf16)
            for dy in range(3):
                j = i - 2 * dy
                if 0 <= j < inner:
                    tap = (3 * dy + dx) * channels
                    taps[tile * j : tile * (j + 1), tap : tap + channels] = piece
    for dy in range(3):
        for x in range(tile, tile + 4):
            piece = read(hid, pl.ds(2 * pitch * dy + x, edge, stride=pitch)).astype(bf16)
            for e in range(2):
                dx = x - tile - e
                if 0 <= dx < 3:
                    tap = (3 * dy + dx) * channels
                    taps[main + edge * e : main + edge * (e + 1), tap : tap + channels] = piece

    conv = jnp.dot(taps[...], residual_ref[...], preferred_element_type=f32)
    column = real(at_ref[1] * tile - 1 + lax.broadcasted_iota(jnp.int32, (tile, 1), 0), 1)
    for i in range(inner):
        value = conv[tile * i : tile * (i + 1)] + read(dec, pl.ds(pitch * (i + 2) + 1, tile))
        keep = column & real(at_ref[0] * tile - 1 + i // 2, 0)
        write(ref, pl.ds(pitch * i, tile), jnp.where(keep, value, 0.0).astype(bf16).astype(f32))
    line = real(at_ref[0] * tile - 1 + lax.broadcasted_iota(jnp.int32, (edge, 1), 0) // 2, 0)
    for e in range(2):
        value = conv[main + edge * e : main + edge * (e + 1)]
        value += read(dec, pl.ds(2 * pitch + tile + 1 + e, edge, stride=pitch))
        keep = line & real(at_ref[1] * tile - 1 + tile + e, 1)
        value = jnp.where(keep, value, 0.0).astype(bf16).astype(f32)
        write(ref, pl.ds(tile + e, edge, stride=pitch), value)

    def column_parts(i):
        left, here, right = (read(ref, pl.ds(pitch * i + d, tile)) for d in range(3))
        return left - here, here, right - here

    for image in range(2):
        before = column_parts(image)
        for y in range(tile + 1):
            after = column_parts(2 * (y + 1) + image)
            at = tile * (2 * y + image)
            for q in range(3):
                slope[q, at : at + tile] = (before[q] - after[q]).astype(bf16)
                if y < tile:
                    centre[q, at : at + tile] = after[q].astype(bf16)
            before = after

    total = 2 * tile * tile

    def product(p, q):
        source = centre[q] if p == 1 else slope[q, tile * p : tile * p + total]
        return jnp.dot(source, upscale_ref[3 * p + q], preferred_element_type=f32)

    middle = product(1, 1)
    shared = (middle + product(1, 0), middle + product(1, 2))
    for a in range(2):
        between = product(2 * a, 1)
        for b in range(2):
            value = shared[b] + between + product(2 * a, 2 * b)
            write(mix.at[a], pl.ds(b, total, stride=2), value)
    for y in range(tile):
        for image in range(2):
            at = 2 * tile * (2 * y + image)
            for a in range(2):
                out_ref[image, 2 * y + a] = read(mix.at[a], pl.ds(at, 2 * tile)).astype(bf16)


def phases_kernel(w_ref, out_ref):
    wide = [w_ref[t].astype(jnp.float32) for t in range(9)]
    down = [
        [wide[q], wide[q] + wide[3 + q] + wide[6 + q], -wide[6 + q]] for q in range(3)
    ]
    for p in range(3):
        parts = [down[q][p] for q in range(3)]
        out_ref[3 * p] = parts[0].astype(jnp.bfloat16)
        out_ref[3 * p + 1] = (parts[0] + parts[1] + parts[2]).astype(jnp.bfloat16)
        out_ref[3 * p + 2] = parts[2].astype(jnp.bfloat16)


def phases(upscale):
    deep, channels = upscale.shape[2:]
    block = pl.BlockSpec((9, deep // 4, channels), lambda i: (0, i, 0))
    return pl.pallas_call(
        phases_kernel,
        out_shape=jax.ShapeDtypeStruct((9, deep, channels), jnp.bfloat16),
        grid=(4,),
        in_specs=[block],
        out_specs=block,
        compiler_params=pltpu.CompilerParams(vmem_limit_bytes=24 << 20),
        cost_estimate=pl.CostEstimate(flops=10 * deep * channels, bytes_accessed=36 * deep * channels, transcendentals=0),
        name="phases",
    )(upscale.reshape(9, deep, channels))


def decode(at, latent, entry, gain, residual, u, tiles):
    images, tile = latent.shape[0], 16
    channels = entry.shape[-1]
    pitch = 24
    padded = jnp.pad(latent, ((0, 0), (0, 0), (0, 10), (0, 0))).astype(jnp.float32)
    padded = padded.transpose(1, 0, 2, 3).reshape(images * (tile + 6), 32, latent.shape[-1])
    rows = images * (tile + 4) + 8
    inner = images * (tile + 2)
    total = images * tile * tile
    f32, bf16 = jnp.float32, jnp.bfloat16
    vmem = pl.BlockSpec(memory_space=pltpu.VMEM)
    return pl.pallas_call(
        functools.partial(decode_kernel, tiles),
        out_shape=jax.ShapeDtypeStruct((images, 2 * tile, 2 * tile, channels), bf16),
        in_specs=[pl.BlockSpec(memory_space=pltpu.SMEM)] + [vmem] * 5,
        out_specs=vmem,
        scratch_shapes=[
            pltpu.VMEM((images * (tile + 6) * pitch, 3 * latent.shape[-1]), bf16),
            pltpu.VMEM((channels // LANES, rows * pitch, LANES), f32),
            pltpu.VMEM((channels // LANES, rows * pitch, LANES), f32),
            pltpu.VMEM((inner * tile + 80, 9 * channels), bf16),
            pltpu.VMEM((channels // LANES, (inner + 4) * pitch, LANES), f32),
            pltpu.VMEM((3, total, channels), bf16),
            pltpu.VMEM((3, total + images * tile, channels), bf16),
            pltpu.VMEM((2, channels // LANES, 2 * total, LANES), f32),
        ],
        compiler_params=pltpu.CompilerParams(vmem_limit_bytes=44 << 20),
        cost_estimate=pl.CostEstimate(flops=8 * 10**9, bytes_accessed=12 << 20, transcendentals=0),
        name="decode",
    )(
        at,
        padded,
        entry.reshape(3, 3 * entry.shape[2], channels),
        gain.reshape(1, channels),
        residual.reshape(9 * channels, channels),
        u,
    )


def local(
    queries,
    key_rows_per_head,
    value_rows_per_head,
    latent_projection_weight,
    entry_conv_weight,
    residual_norm_gain,
    residual_conv_weight,
    upscale_conv_weight,
):
    images, tile, _, width = queries.shape
    scale = 1.0 / (tile * lax.axis_size("row") * tile * lax.axis_size("col"))
    flat = (images, tile * tile, width)
    keys, values = key_rows_per_head.reshape(flat), value_rows_per_head.reshape(flat)
    core = (lax.axis_index("col") % 2).astype(jnp.int32)
    other = image_sums(keys, values, 1 - core, scale)
    mine = image_sums(keys, values, core, scale)
    kv = sum_over_mesh(mine, other)
    latent = attend(queries.reshape(flat), kv, latent_projection_weight)
    latent = latent.reshape(images, tile, tile, latent.shape[-1])
    widened = extended(latent, (("row", 1), ("col", 2)), 3)
    at = jnp.stack([lax.axis_index("row"), lax.axis_index("col")]).astype(jnp.int32)
    tiles = (lax.axis_size("row"), lax.axis_size("col"))
    return decode(
        at,
        widened,
        entry_conv_weight,
        residual_norm_gain,
        residual_conv_weight,
        phases(upscale_conv_weight),
        tiles,
    )


def solution(mesh):
    placed = (
        P(None, "row", "col", None),
        P(None, "row", "col", None),
        P(None, "row", "col", None),
        P(),
        P(),
        P(),
        P(),
        P(),
    )
    return jax.shard_map(
        local, mesh=mesh, in_specs=placed, out_specs=P(None, "row", "col", None), check_vma=False
    )
```

profile of v0, /device:TPU:23, one launch (start us, length us, event | category | flops | bytes accessed | tf_op | source)
XLA Modules:
  0.0 87.8 jit_solution(8294864782163089695)
XLA Ops:
  0.0 1.7 %copy-done = bf16[2,16,16,2240]{3,2,1,0:T(8,128)(2,1)S(1)} copy-done((bf16[2,16,16,2240]{3,2,1,0:T(8,128)(2,1)S(1)}, bf16[2,16,16,2240]{3,2,1,0:T(8,128)(2,1)}, u32[]{:S(2)}) %copy-start) | copy-done | bytes 2293784
  1.7 1.7 %copy-done.2 = bf16[2,16,16,2240]{3,2,1,0:T(8,128)(2,1)S(1)} copy-done((bf16[2,16,16,2240]{3,2,1,0:T(8,128)(2,1)S(1)}, bf16[2,16,16,2240]{3,2,1,0:T(8,128)(2,1)}, u32[]{:S(2)}) %copy-start.2) | copy-done | bytes 2293784
  3.3 0.6 image_sums.3
  3.9 0.8 collective-permute-start
  5.0 1.7 %copy-done.3 = bf16[2,16,16,2240]{3,2,1,0:T(8,128)(2,1)S(1)} copy-done((bf16[2,16,16,2240]{3,2,1,0:T(8,128)(2,1)S(1)}, bf16[2,16,16,2240]{3,2,1,0:T(8,128)(2,1)}, u32[]{:S(2)}) %copy-start.3) | copy-done | bytes 2293784
  7.3 0.6 collective-permute-start.1
  8.0 0.8 collective-permute-start.3
  8.8 2.5 %collective-permute-start.2 = (bf16[16,1280]{1,0:T(8,128)(2,1)S(1)}, bf16[16,1280]{1,0:T(8,128)(2,1)S(1)}, u32[]{:S(2)}, u32[]{:S(2)}) collective-permute-start(bf16[16,1280]{1,0:T(8,128)(2,1)S(1)} %get-tuple-element.11), channel_id=1, source_target_pairs={{0,48},{16,32},{32,16},{48,0},{64,112},{80,96},{96,80},{112,64},{1... | collective-permute-start | bytes 122888 | tf_op jit(solution)/shard_map/ppermute | solution.py:143
  11.3 1.0 %collective-permute-done.3 = bf16[16,1280]{1,0:T(8,128)(2,1)S(1)} collective-permute-done((bf16[16,1280]{1,0:T(8,128)(2,1)S(1)}, bf16[16,1280]{1,0:T(8,128)(2,1)S(1)}, u32[]{:S(2)}, u32[]{:S(2)}) %collective-permute-start.3) | collective-permute-done | bytes 40992 | tf_op jit(solution)/shard_map/ppermute | solution.py:143
  12.9 1.5 %collective-permute-start.6 = (bf16[16,1280]{1,0:T(8,128)(2,1)S(1)}, bf16[16,1280]{1,0:T(8,128)(2,1)S(1)}, u32[]{:S(2)}, u32[]{:S(2)}) collective-permute-start(bf16[16,1280]{1,0:T(8,128)(2,1)S(1)} %fusion.8), channel_id=1, source_target_pairs={{0,128},{16,144},{32,160},{48,176},{64,192},{80,208},{96,224},{112... | collective-permute-start | bytes 122888 | tf_op jit(solution)/shard_map/ppermute | solution.py:130
  14.4 0.7 collective-permute-start.5
  15.2 1.7 %collective-permute-start.4 = (bf16[16,1280]{1,0:T(8,128)(2,1)S(1)}, bf16[16,1280]{1,0:T(8,128)(2,1)S(1)}, u32[]{:S(2)}, u32[]{:S(2)}) collective-permute-start(bf16[16,1280]{1,0:T(8,128)(2,1)S(1)} %fusion.8), channel_id=1, source_target_pairs={{0,64},{16,80},{32,96},{48,112},{64,0},{80,16},{96,32},{112,48},{1... | collective-permute-start | bytes 122888 | tf_op jit(solution)/shard_map/ppermute | solution.py:130
  16.8 0.6 collective-permute-done.6
  18.3 1.7 %collective-permute-start.7 = (bf16[16,1280]{1,0:T(8,128)(2,1)S(1)}, bf16[16,1280]{1,0:T(8,128)(2,1)S(1)}, u32[]{:S(2)}, u32[]{:S(2)}) collective-permute-start(bf16[16,1280]{1,0:T(8,128)(2,1)S(1)} %add_convert_fusion.2), channel_id=1, source_target_pairs={{0,2},{1,3},{2,0},{3,1},{4,6},{5,7},{6,4},{7,5},{8,10},{9,11},{10,... | collective-permute-start | bytes 122888 | tf_op jit(solution)/shard_map/ppermute | solution.py:130
  20.0 1.7 %collective-permute-done.7 = bf16[16,1280]{1,0:T(8,128)(2,1)S(1)} collective-permute-done((bf16[16,1280]{1,0:T(8,128)(2,1)S(1)}, bf16[16,1280]{1,0:T(8,128)(2,1)S(1)}, u32[]{:S(2)}, u32[]{:S(2)}) %collective-permute-start.7) | collective-permute-done | bytes 40992 | tf_op jit(solution)/shard_map/ppermute | solution.py:130
  21.7 6.4 %collective-permute-start.10 = (bf16[16,1280]{1,0:T(8,128)(2,1)S(1)}, bf16[16,1280]{1,0:T(8,128)(2,1)S(1)}, u32[]{:S(2)}, u32[]{:S(2)}) collective-permute-start(bf16[16,1280]{1,0:T(8,128)(2,1)S(1)} %add_convert_fusion.1), channel_id=1, source_target_pairs={{0,10},{1,11},{2,8},{3,9},{4,14},{5,15},{6,12},{7,13},{8,2},{9,3},... | collective-permute-start | bytes 122888 | tf_op jit(solution)/shard_map/ppermute | solution.py:130
  28.3 0.9 %collective-permute-start.8 = (bf16[16,1280]{1,0:T(8,128)(2,1)S(1)}, bf16[16,1280]{1,0:T(8,128)(2,1)S(1)}, u32[]{:S(2)}, u32[]{:S(2)}) collective-permute-start(bf16[16,1280]{1,0:T(8,128)(2,1)S(1)} %add_convert_fusion.1), channel_id=1, source_target_pairs={{0,4},{1,5},{2,6},{3,7},{4,0},{5,1},{6,2},{7,3},{8,12},{9,13},{10,... | collective-permute-start | bytes 122888 | tf_op jit(solution)/shard_map/ppermute | solution.py:130
  29.4 3.6 %collective-permute-done.9 = bf16[16,1280]{1,0:T(8,128)(2,1)S(1)} collective-permute-done((bf16[16,1280]{1,0:T(8,128)(2,1)S(1)}, bf16[16,1280]{1,0:T(8,128)(2,1)S(1)}, u32[]{:S(2)}, u32[]{:S(2)}) %collective-permute-start.9) | collective-permute-done | bytes 40992 | tf_op jit(solution)/shard_map/ppermute | solution.py:130
  33.1 6.3 %collective-permute-start.11 = (bf16[16,1280]{1,0:T(8,128)(2,1)S(1)}, bf16[16,1280]{1,0:T(8,128)(2,1)S(1)}, u32[]{:S(2)}, u32[]{:S(2)}) collective-permute-start(bf16[16,1280]{1,0:T(8,128)(2,1)S(1)} %add_convert_fusion), channel_id=1, source_target_pairs={{0,1},{1,0},{2,3},{3,2},{4,5},{5,4},{6,7},{7,6},{8,9},{9,8},{10,11... | collective-permute-start | bytes 122888 | tf_op jit(solution)/shard_map/ppermute | solution.py:154
  40.2 2.6 %collective-permute-start.14 = (bf16[2,16,1280]{2,1,0:T(8,128)(2,1)S(1)}, bf16[2,16,1280]{2,1,0:T(8,128)(2,1)S(1)}, u32[]{:S(2)}, u32[]{:S(2)}) collective-permute-start(bf16[2,16,1280]{2,1,0:T(8,128)(2,1)S(1)} %maximum_select_fusion.1), channel_id=1, source_target_pairs={{0,48},{16,32},{32,16},{48,0},{64,112},{80,96},{96,80},{112,64},{1... | collective-permute-start | bytes 245768 | tf_op jit(solution)/shard_map/ppermute | solution.py:156
  42.8 0.8 collective-permute-start.12
  43.5 1.8 %collective-permute-done.14 = bf16[2,16,1280]{2,1,0:T(8,128)(2,1)S(1)} collective-permute-done((bf16[2,16,1280]{2,1,0:T(8,128)(2,1)S(1)}, bf16[2,16,1280]{2,1,0:T(8,128)(2,1)S(1)}, u32[]{:S(2)}, u32[]{:S(2)}) %collective-permute-start.14) | collective-permute-done | bytes 81952 | tf_op jit(solution)/shard_map/ppermute | solution.py:156
  45.3 2.2 %collective-permute-done.13 = bf16[2,16,1280]{2,1,0:T(8,128)(2,1)S(1)} collective-permute-done((bf16[2,16,1280]{2,1,0:T(8,128)(2,1)S(1)}, bf16[2,16,1280]{2,1,0:T(8,128)(2,1)S(1)}, u32[]{:S(2)}, u32[]{:S(2)}) %collective-permute-start.13) | collective-permute-done | bytes 81952 | tf_op jit(solution)/shard_map/ppermute | solution.py:156
  47.7 4.9 %attend.1 = bf16[2,256,32]{2,1,0:T(8,128)(2,1)S(1)} custom-call(bf16[2,256,2240]{2,1,0:T(8,128)(2,1)S(1)} %bitcast.55, bf16[2,4,16,1280]{3,2,1,0:T(8,128)(2,1)S(1)} %pad_maximum_fusion.1.kv_ref, bf16[2240,32]{1,0:T(8,128)(2,1)S(1)} %copy.9.w_ref), custom_call_target="tpu_custom_call" | custom-call | flops 1174405120 | bytes 2293760 | tf_op jit(solution)/shard_map/attend/pallas_call | solution.py:109
  52.7 5.4 %collective-permute-start.15 = (bf16[2,3,16,32]{3,2,0,1:T(8,128)(2,1)S(1)}, bf16[2,3,16,32]{3,2,0,1:T(8,128)(2,1)S(1)}, u32[]{:S(2)}, u32[]{:S(2)}) collective-permute-start(bf16[2,3,16,32]{3,2,0,1:T(8,128)(2,1)S(1)} %copy.14), channel_id=1, source_target_pairs={{0,16},{16,32},{32,48},{48,64},{64,80},{80,96},{96,112},{112,128},... | collective-permute-start | bytes 18440 | tf_op jit(solution)/shard_map/ppermute | solution.py:169
  58.1 1.9 %collective-permute-start.16 = (bf16[2,3,16,32]{3,2,0,1:T(8,128)(2,1)S(1)}, bf16[2,3,16,32]{3,2,0,1:T(8,128)(2,1)S(1)}, u32[]{:S(2)}, u32[]{:S(2)}) collective-permute-start(bf16[2,3,16,32]{3,2,0,1:T(8,128)(2,1)S(1)} %copy.15), channel_id=1, source_target_pairs={{16,0},{32,16},{48,32},{64,48},{80,64},{96,80},{112,96},{128,112},... | collective-permute-start | bytes 18440 | tf_op jit(solution)/shard_map/ppermute | solution.py:170
  60.1 4.7 %collective-permute-done.16 = bf16[2,3,16,32]{3,2,0,1:T(8,128)(2,1)S(1)} collective-permute-done((bf16[2,3,16,32]{3,2,0,1:T(8,128)(2,1)S(1)}, bf16[2,3,16,32]{3,2,0,1:T(8,128)(2,1)S(1)}, u32[]{:S(2)}, u32[]{:S(2)}) %collective-permute-start.16) | collective-permute-done | bytes 6176 | tf_op jit(solution)/shard_map/ppermute | solution.py:170
  64.8 5.4 %collective-permute-start.17 = (bf16[2,22,3,32]{3,2,0,1:T(4,128)(2,1)S(1)}, bf16[2,22,3,32]{3,2,0,1:T(4,128)(2,1)S(1)}, u32[]{:S(2)}, u32[]{:S(2)}) collective-permute-start(bf16[2,22,3,32]{3,2,0,1:T(4,128)(2,1)S(1)} %get-tuple-element.12), channel_id=1, source_target_pairs={{0,1},{1,2},{2,3},{3,4},{4,5},{5,6},{6,7},{7,8},{8,9},{9,10},{10,1... | collective-permute-start | bytes 25352 | tf_op jit(solution)/shard_map/ppermute | solution.py:169
  70.3 1.9 %collective-permute-start.18 = (bf16[2,22,3,32]{3,2,0,1:T(4,128)(2,1)S(1)}, bf16[2,22,3,32]{3,2,0,1:T(4,128)(2,1)S(1)}, u32[]{:S(2)}, u32[]{:S(2)}) collective-permute-start(bf16[2,22,3,32]{3,2,0,1:T(4,128)(2,1)S(1)} %get-tuple-element.13), channel_id=1, source_target_pairs={{1,0},{2,1},{3,2},{4,3},{5,4},{6,5},{7,6},{8,7},{9,8},{10,9},{11,1... | collective-permute-start | bytes 25352 | tf_op jit(solution)/shard_map/ppermute | solution.py:170
  72.3 2.0 %phases.1.upscale_ref = bf16[9,512,512]{2,1,0:T(8,128)(2,1)S(1)} custom-call(bf16[9,512,512]{2,1,0:T(8,128)(2,1)S(1)} %bitcast.48), custom_call_target="tpu_custom_call" | custom-call | flops 2621440 | bytes 9437184 | tf_op jit(solution)/shard_map/phases/pallas_call | solution.py:305
  74.3 2.1 %copy-done.5 = bf16[9,512,512]{2,1,0:T(8,128)(2,1)} copy-done((bf16[9,512,512]{2,1,0:T(8,128)(2,1)}, bf16[9,512,512]{2,1,0:T(8,128)(2,1)S(1)}, u32[]{:S(2)}) %copy-start.5) | copy-done | bytes 4718616
  76.6 11.1 %decode.1 = bf16[2,32,32,512]{3,2,1,0:T(8,128)(2,1)} custom-call(s32[2]{0:T(128)S(1)} %pad_add_fusion.at_ref, f32[44,32,32]{2,1,0:T(8,128)S(1)} %bitcast.49, bf16[3,96,512]{2,1,0:T(8,128)(2,1)S(1)} %bitcast.56, f32[1,512]{1,0:T(1,128)S(1)} %bitcast.57, bf16[4608,512]{1,0:T(8,128)(2,1)S(1)} %bitcast.54, bf16[9,512,512]{2,1,0:T(8,128)(2,1)} %copy-done.5), custom_call_target="tpu_custom_call" | custom-call | flops 8000000000 | bytes 12582912 | tf_op jit(solution)/shard_map/decode/pallas_call | solution.py:328
  (57 shorter events, 4.2 us)
Async XLA Ops:
  0.0 1.7 %copy-start = (bf16[2,16,16,2240]{3,2,1,0:T(8,128)(2,1)S(1)}, bf16[2,16,16,2240]{3,2,1,0:T(8,128)(2,1)}, u32[]{:S(2)}) copy-start(bf16[2,16,16,2240]{3,2,1,0:T(8,128)(2,1)} %param.9) | copy-start | bytes 6881284
  1.7 1.7 %copy-start.2 = (bf16[2,16,16,2240]{3,2,1,0:T(8,128)(2,1)S(1)}, bf16[2,16,16,2240]{3,2,1,0:T(8,128)(2,1)}, u32[]{:S(2)}) copy-start(bf16[2,16,16,2240]{3,2,1,0:T(8,128)(2,1)} %param.10) | copy-start | bytes 6881284
  3.3 1.7 %copy-start.1 = (bf16[2,16,16,2240]{3,2,1,0:T(8,128)(2,1)S(1)}, bf16[2,16,16,2240]{3,2,1,0:T(8,128)(2,1)}, u32[]{:S(2)}) copy-start(bf16[2,16,16,2240]{3,2,1,0:T(8,128)(2,1)} %param.9) | copy-start | bytes 6881284
  3.9 3.3 %collective-permute-start = (bf16[4,16,1280]{2,1,0:T(8,128)(2,1)S(1)}, bf16[4,16,1280]{2,1,0:T(8,128)(2,1)S(1)}, u32[]{:S(2)}, u32[]{:S(2)}) collective-permute-start(bf16[4,16,1280]{2,1,0:T(8,128)(2,1)S(1)} %image_sums.3), channel_id=1, source_target_pairs={{0,1},{1,0},{2,3},{3,2},{4,5},{5,4},{6,7},{7,6},{8,9},{9,8},{10,11... | collective-permute-start | bytes 491528 | tf_op jit(solution)/shard_map/ppermute | solution.py:140
  5.0 1.7 %copy-start.3 = (bf16[2,16,16,2240]{3,2,1,0:T(8,128)(2,1)S(1)}, bf16[2,16,16,2240]{3,2,1,0:T(8,128)(2,1)}, u32[]{:S(2)}) copy-start(bf16[2,16,16,2240]{3,2,1,0:T(8,128)(2,1)} %param.10) | copy-start | bytes 6881284
  6.7 32.6 %copy-start.9 = (bf16[2240,32]{0,1:T(8,128)(2,1)S(1)}, bf16[2240,32]{0,1:T(8,128)(2,1)}, u32[]{:S(2)}) copy-start(bf16[2240,32]{0,1:T(8,128)(2,1)} %param.11) | copy-start | bytes 430084
  7.2 40.5 %copy-start.6 = (bf16[2,16,16,2240]{3,2,1,0:T(8,128)(2,1)S(1)}, bf16[2,16,16,2240]{3,2,1,0:T(8,128)(2,1)}, u32[]{:S(2)}) copy-start(bf16[2,16,16,2240]{3,2,1,0:T(8,128)(2,1)} %param.8) | copy-start | bytes 6881284
  7.3 4.0 %collective-permute-start.1 = (bf16[16,1280]{1,0:T(8,128)(2,1)S(1)}, bf16[16,1280]{1,0:T(8,128)(2,1)S(1)}, u32[]{:S(2)}, u32[]{:S(2)}) collective-permute-start(bf16[16,1280]{1,0:T(8,128)(2,1)S(1)} %get-tuple-element.9), channel_id=1, source_target_pairs={{0,16},{16,0},{32,48},{48,32},{64,80},{80,64},{96,112},{112,96},{1... | collective-permute-start | bytes 122888 | tf_op jit(solution)/shard_map/ppermute | solution.py:143
  8.0 4.4 %collective-permute-start.3 = (bf16[16,1280]{1,0:T(8,128)(2,1)S(1)}, bf16[16,1280]{1,0:T(8,128)(2,1)S(1)}, u32[]{:S(2)}, u32[]{:S(2)}) collective-permute-start(bf16[16,1280]{1,0:T(8,128)(2,1)S(1)} %get-tuple-element.10), channel_id=1, source_target_pairs={{0,32},{16,48},{32,0},{48,16},{64,96},{80,112},{96,64},{112,80},{1... | collective-permute-start | bytes 122888 | tf_op jit(solution)/shard_map/ppermute | solution.py:143
  8.8 4.1 %collective-permute-start.2 = (bf16[16,1280]{1,0:T(8,128)(2,1)S(1)}, bf16[16,1280]{1,0:T(8,128)(2,1)S(1)}, u32[]{:S(2)}, u32[]{:S(2)}) collective-permute-start(bf16[16,1280]{1,0:T(8,128)(2,1)S(1)} %get-tuple-element.11), channel_id=1, source_target_pairs={{0,48},{16,32},{32,16},{48,0},{64,112},{80,96},{96,80},{112,64},{1... | collective-permute-start | bytes 122888 | tf_op jit(solution)/shard_map/ppermute | solution.py:143
  12.9 4.5 %collective-permute-start.6 = (bf16[16,1280]{1,0:T(8,128)(2,1)S(1)}, bf16[16,1280]{1,0:T(8,128)(2,1)S(1)}, u32[]{:S(2)}, u32[]{:S(2)}) collective-permute-start(bf16[16,1280]{1,0:T(8,128)(2,1)S(1)} %fusion.8), channel_id=1, source_target_pairs={{0,128},{16,144},{32,160},{48,176},{64,192},{80,208},{96,224},{112... | collective-permute-start | bytes 122888 | tf_op jit(solution)/shard_map/ppermute | solution.py:130
  14.4 3.3 %collective-permute-start.5 = (bf16[16,1280]{1,0:T(8,128)(2,1)S(1)}, bf16[16,1280]{1,0:T(8,128)(2,1)S(1)}, u32[]{:S(2)}, u32[]{:S(2)}) collective-permute-start(bf16[16,1280]{1,0:T(8,128)(2,1)S(1)} %fusion.8), channel_id=1, source_target_pairs={{0,192},{16,208},{32,224},{48,240},{64,128},{80,144},{96,160},{112... | collective-permute-start | bytes 122888 | tf_op jit(solution)/shard_map/ppermute | solution.py:130
  15.2 3.1 %collective-permute-start.4 = (bf16[16,1280]{1,0:T(8,128)(2,1)S(1)}, bf16[16,1280]{1,0:T(8,128)(2,1)S(1)}, u32[]{:S(2)}, u32[]{:S(2)}) collective-permute-start(bf16[16,1280]{1,0:T(8,128)(2,1)S(1)} %fusion.8), channel_id=1, source_target_pairs={{0,64},{16,80},{32,96},{48,112},{64,0},{80,16},{96,32},{112,48},{1... | collective-permute-start | bytes 122888 | tf_op jit(solution)/shard_map/ppermute | solution.py:130
  18.3 3.4 %collective-permute-start.7 = (bf16[16,1280]{1,0:T(8,128)(2,1)S(1)}, bf16[16,1280]{1,0:T(8,128)(2,1)S(1)}, u32[]{:S(2)}, u32[]{:S(2)}) collective-permute-start(bf16[16,1280]{1,0:T(8,128)(2,1)S(1)} %add_convert_fusion.2), channel_id=1, source_target_pairs={{0,2},{1,3},{2,0},{3,1},{4,6},{5,7},{6,4},{7,5},{8,10},{9,11},{10,... | collective-permute-start | bytes 122888 | tf_op jit(solution)/shard_map/ppermute | solution.py:130
  21.7 7.8 %collective-permute-start.10 = (bf16[16,1280]{1,0:T(8,128)(2,1)S(1)}, bf16[16,1280]{1,0:T(8,128)(2,1)S(1)}, u32[]{:S(2)}, u32[]{:S(2)}) collective-permute-start(bf16[16,1280]{1,0:T(8,128)(2,1)S(1)} %add_convert_fusion.1), channel_id=1, source_target_pairs={{0,10},{1,11},{2,8},{3,9},{4,14},{5,15},{6,12},{7,13},{8,2},{9,3},... | collective-permute-start | bytes 122888 | tf_op jit(solution)/shard_map/ppermute | solution.py:130
  28.1 5.0 %collective-permute-start.9 = (bf16[16,1280]{1,0:T(8,128)(2,1)S(1)}, bf16[16,1280]{1,0:T(8,128)(2,1)S(1)}, u32[]{:S(2)}, u32[]{:S(2)}) collective-permute-start(bf16[16,1280]{1,0:T(8,128)(2,1)S(1)} %add_convert_fusion.1), channel_id=1, source_target_pairs={{0,12},{1,13},{2,14},{3,15},{4,8},{5,9},{6,10},{7,11},{8,4},{9,5},... | collective-permute-start | bytes 122888 | tf_op jit(solution)/shard_map/ppermute | solution.py:130
  28.3 4.7 %collective-permute-start.8 = (bf16[16,1280]{1,0:T(8,128)(2,1)S(1)}, bf16[16,1280]{1,0:T(8,128)(2,1)S(1)}, u32[]{:S(2)}, u32[]{:S(2)}) collective-permute-start(bf16[16,1280]{1,0:T(8,128)(2,1)S(1)} %add_convert_fusion.1), channel_id=1, source_target_pairs={{0,4},{1,5},{2,6},{3,7},{4,0},{5,1},{6,2},{7,3},{8,12},{9,13},{10,... | collective-permute-start | bytes 122888 | tf_op jit(solution)/shard_map/ppermute | solution.py:130
  33.1 7.1 %collective-permute-start.11 = (bf16[16,1280]{1,0:T(8,128)(2,1)S(1)}, bf16[16,1280]{1,0:T(8,128)(2,1)S(1)}, u32[]{:S(2)}, u32[]{:S(2)}) collective-permute-start(bf16[16,1280]{1,0:T(8,128)(2,1)S(1)} %add_convert_fusion), channel_id=1, source_target_pairs={{0,1},{1,0},{2,3},{3,2},{4,5},{5,4},{6,7},{7,6},{8,9},{9,8},{10,11... | collective-permute-start | bytes 122888 | tf_op jit(solution)/shard_map/ppermute | solution.py:154
  40.2 5.1 %collective-permute-start.14 = (bf16[2,16,1280]{2,1,0:T(8,128)(2,1)S(1)}, bf16[2,16,1280]{2,1,0:T(8,128)(2,1)S(1)}, u32[]{:S(2)}, u32[]{:S(2)}) collective-permute-start(bf16[2,16,1280]{2,1,0:T(8,128)(2,1)S(1)} %maximum_select_fusion.1), channel_id=1, source_target_pairs={{0,48},{16,32},{32,16},{48,0},{64,112},{80,96},{96,80},{112,64},{1... | collective-permute-start | bytes 245768 | tf_op jit(solution)/shard_map/ppermute | solution.py:156
  42.8 4.8 %collective-permute-start.13 = (bf16[2,16,1280]{2,1,0:T(8,128)(2,1)S(1)}, bf16[2,16,1280]{2,1,0:T(8,128)(2,1)S(1)}, u32[]{:S(2)}, u32[]{:S(2)}) collective-permute-start(bf16[2,16,1280]{2,1,0:T(8,128)(2,1)S(1)} %maximum_select_fusion.1), channel_id=1, source_target_pairs={{0,32},{16,48},{32,0},{48,16},{64,96},{80,112},{96,64},{112,80},{1... | collective-permute-start | bytes 245768 | tf_op jit(solution)/shard_map/ppermute | solution.py:156
  42.8 4.8 %collective-permute-start.12 = (bf16[2,16,1280]{2,1,0:T(8,128)(2,1)S(1)}, bf16[2,16,1280]{2,1,0:T(8,128)(2,1)S(1)}, u32[]{:S(2)}, u32[]{:S(2)}) collective-permute-start(bf16[2,16,1280]{2,1,0:T(8,128)(2,1)S(1)} %maximum_select_fusion.1), channel_id=1, source_target_pairs={{0,16},{16,0},{32,48},{48,32},{64,80},{80,64},{96,112},{112,96},{1... | collective-permute-start | bytes 245768 | tf_op jit(solution)/shard_map/ppermute | solution.py:156
  47.7 24.6 %copy-start.4 = (bf16[3,3,512,512]{3,2,1,0:T(8,128)(2,1)S(1)}, bf16[3,3,512,512]{3,2,1,0:T(8,128)(2,1)}, u32[]{:S(2)}) copy-start(bf16[3,3,512,512]{3,2,1,0:T(8,128)(2,1)} %param.15) | copy-start | bytes 14155780
  52.7 7.4 %collective-permute-start.15 = (bf16[2,3,16,32]{3,2,0,1:T(8,128)(2,1)S(1)}, bf16[2,3,16,32]{3,2,0,1:T(8,128)(2,1)S(1)}, u32[]{:S(2)}, u32[]{:S(2)}) collective-permute-start(bf16[2,3,16,32]{3,2,0,1:T(8,128)(2,1)S(1)} %copy.14), channel_id=1, source_target_pairs={{0,16},{16,32},{32,48},{48,64},{64,80},{80,96},{96,112},{112,128},... | collective-permute-start | bytes 18440 | tf_op jit(solution)/shard_map/ppermute | solution.py:169
  58.1 6.7 %collective-permute-start.16 = (bf16[2,3,16,32]{3,2,0,1:T(8,128)(2,1)S(1)}, bf16[2,3,16,32]{3,2,0,1:T(8,128)(2,1)S(1)}, u32[]{:S(2)}, u32[]{:S(2)}) collective-permute-start(bf16[2,3,16,32]{3,2,0,1:T(8,128)(2,1)S(1)} %copy.15), channel_id=1, source_target_pairs={{16,0},{32,16},{48,32},{64,48},{80,64},{96,80},{112,96},{128,112},... | collective-permute-start | bytes 18440 | tf_op jit(solution)/shard_map/ppermute | solution.py:170
  60.0 16.6 %slice-start = ((s8[4718592]{0:T(1024)(128)(4,1)}), s8[4194304]{0:T(1024)(128)(4,1)S(1)}, s32[]{:S(2)}) async-start(s8[4718592]{0:T(1024)(128)(4,1)} %bitcast.52), calls=%async_computation | async-start | bytes 8388608
  64.8 11.6 %collective-permute-start.17 = (bf16[2,22,3,32]{3,2,0,1:T(4,128)(2,1)S(1)}, bf16[2,22,3,32]{3,2,0,1:T(4,128)(2,1)S(1)}, u32[]{:S(2)}, u32[]{:S(2)}) collective-permute-start(bf16[2,22,3,32]{3,2,0,1:T(4,128)(2,1)S(1)} %get-tuple-element.12), channel_id=1, source_target_pairs={{0,1},{1,2},{2,3},{3,4},{4,5},{5,6},{6,7},{7,8},{8,9},{9,10},{10,1... | collective-permute-start | bytes 25352 | tf_op jit(solution)/shard_map/ppermute | solution.py:169
  70.3 6.2 %collective-permute-start.18 = (bf16[2,22,3,32]{3,2,0,1:T(4,128)(2,1)S(1)}, bf16[2,22,3,32]{3,2,0,1:T(4,128)(2,1)S(1)}, u32[]{:S(2)}, u32[]{:S(2)}) collective-permute-start(bf16[2,22,3,32]{3,2,0,1:T(4,128)(2,1)S(1)} %get-tuple-element.13), channel_id=1, source_target_pairs={{1,0},{2,1},{3,2},{4,3},{5,4},{6,5},{7,6},{8,7},{9,8},{10,9},{11,1... | collective-permute-start | bytes 25352 | tf_op jit(solution)/shard_map/ppermute | solution.py:170
  72.3 4.3 %slice-start.1 = ((s8[4718592]{0:T(1024)(128)(4,1)}), s8[524288]{0:T(1024)(128)(4,1)S(1)}, s32[]{:S(2)}) async-start(s8[4718592]{0:T(1024)(128)(4,1)} %bitcast.52), calls=%async_computation.1 | async-start | bytes 1048576
  72.3 4.3 %copy-start.7 = (bf16[3,3,32,512]{3,2,1,0:T(8,128)(2,1)S(1)}, bf16[3,3,32,512]{3,2,1,0:T(8,128)(2,1)}, u32[]{:S(2)}) copy-start(bf16[3,3,32,512]{3,2,1,0:T(8,128)(2,1)} %param.12) | copy-start | bytes 884740
  72.3 4.3 %copy-start.8 = (f32[512]{0:T(512)S(1)}, f32[512]{0:T(512)}, u32[]{:S(2)}) copy-start(f32[512]{0:T(512)} %param.13) | copy-start | bytes 6148
  74.3 2.1 %copy-start.5 = (bf16[9,512,512]{2,1,0:T(8,128)(2,1)}, bf16[9,512,512]{2,1,0:T(8,128)(2,1)S(1)}, u32[]{:S(2)}) copy-start(bf16[9,512,512]{2,1,0:T(8,128)(2,1)S(1)} %phases.1.upscale_ref) | copy-start | bytes 14155780
where the time goes:
time: 88.1 us; the launch traced here: 87.8 us
  starting transfers between devices  42.2 us (48%)
  Pallas kernels  19.1 us (22%)
  waiting for transfers between devices  17.7 us (20%)
  local copies, waits for them, and re-layouts  7.96 us (9%)
    ppermute x7, starting transfers between devices, exchange_group(): arrived = [lax.ppermute(value, axis, xor_pairs(d)) for d in distances]  13.2 us
    pallas_call x1, Pallas kernels, decode(): pl.pallas_call(functools.partial(decode_kernel, tiles), out_shape=jax.Sha...  11.1 us
    ppermute x2, starting transfers between devices, extended(): before = lax.ppermute(last, axis, up)  10.8 us
    unnamed x29, local copies, waits for them, and re-layouts  7.85 us
    ppermute x7, waiting for transfers between devices, exchange_group(): arrived = [lax.ppermute(value, axis, xor_pairs(d)) for d in distances]  6.85 us
    ppermute x1, starting transfers between devices, sum_over_mesh(): twin = lax.ppermute(chunk, 'col', xor_pairs(1))  6.25 us
    pallas_call x1, Pallas kernels, attend(): pl.pallas_call(attend_kernel, out_shape=jax.ShapeDtypeStruct((images, tok...  4.91 us
    ppermute x2, waiting for transfers between devices, extended(): after = lax.ppermute(initial, axis, down)  4.69 us
  transfers between devices with their start and end apart: 19, of which 12 were waited for; matrix products, arithmetic and copies ran while one was open for 0% of the time, Pallas kernels for 3%

commit v1 on v0

--- a/solution.py
+++ b/solution.py
@@ -14,51 +14,70 @@
 KS_AT = 2304
 
 
-def sums_kernel(scale, _, k_ref, v_ref, out_ref):
-    tokens, width = k_ref.shape[1:]
+def sums_kernel(scale, core_ref, k_hbm, v_hbm, mine_ref, other_ref, k_ref, v_ref, sems):
+    images, tokens, width = k_ref.shape
+    core = core_ref[0]
+    half = tokens // 2
+    copies = []
+    for n in range(images):
+        image = 1 - core if n == 0 else core
+        for c in range(2):
+            at = pl.ds(half * c, half)
+            for m, (source, target) in enumerate(((k_hbm, k_ref), (v_hbm, v_ref))):
+                copies.append(
+                    pltpu.make_async_copy(source.at[image, at], target.at[n, at], sems.at[n, c, m])
+                )
+    for copy in copies:
+        copy.start()
     ones = jnp.ones((tokens, LANES), jnp.bfloat16)
     lane = lax.broadcasted_iota(jnp.int32, (HEAD, LANES), 1)
-    parts = []
-    key_sums = jnp.zeros((HEAD, LANES), jnp.float32)
-    for start in range(0, width, LANES):
-        size = min(LANES, width - start)
-        keys = jnp.maximum(k_ref[0, :, start : start + size], 0)
-        values = jnp.concatenate([v_ref[0, :, start : start + size], ones], axis=1)
-        product = lax.dot_general(
-            keys, values, (((0,), (0,)), ((), ())), preferred_element_type=jnp.float32
-        )
-        packed = jnp.zeros((HEAD, size), jnp.float32)
-        for h in range(size // HEAD):
-            rows = product[h * HEAD : (h + 1) * HEAD]
-            packed = jnp.where(lane[:, :size] // HEAD == h, rows[:, :size], packed)
-            key_sums = jnp.where(lane == start // HEAD + h, rows[:, size:], key_sums)
-        parts.append(packed)
-    parts.append(jnp.zeros((HEAD, KS_AT - width), jnp.float32))
-    parts.append(key_sums)
-    parts.append(jnp.zeros((HEAD, PACK - KS_AT - LANES), jnp.float32))
-    total = (jnp.concatenate(parts, axis=1) * scale).astype(jnp.bfloat16)
-    half = PACK // 2
-    for r in range(2):
-        for c in range(2):
-            out_ref[2 * r + c] = total[16 * r : 16 * r + 16, half * c : half * (c + 1)]
-
-
-def image_sums(keys, values, image, scale):
+    for n, out_ref in ((0, other_ref), (1, mine_ref)):
+        for copy in copies[4 * n : 4 * n + 4]:
+            copy.wait()
+        parts = []
+        key_sums = jnp.zeros((HEAD, LANES), jnp.float32)
+        for start in range(0, width, LANES):
+            size = min(LANES, width - start)
+            keys = jnp.maximum(k_ref[n, :, start : start + size], 0)
+            values = jnp.concatenate([v_ref[n, :, start : start + size], ones], axis=1)
+            product = lax.dot_general(
+                keys, values, (((0,), (0,)), ((), ())), preferred_element_type=jnp.float32
+            )
+            packed = jnp.zeros((HEAD, size), jnp.float32)
+            for h in range(size // HEAD):
+                rows = product[h * HEAD : (h + 1) * HEAD]
+                packed = jnp.where(lane[:, :size] // HEAD == h, rows[:, :size], packed)
+                key_sums = jnp.where(lane == start // HEAD + h, rows[:, size:], key_sums)
+            parts.append(packed)
+        parts.append(jnp.zeros((HEAD, KS_AT - width), jnp.float32))
+        parts.append(key_sums)
+        parts.append(jnp.zeros((HEAD, PACK - KS_AT - LANES), jnp.float32))
+        total = (jnp.concatenate(parts, axis=1) * scale).astype(jnp.bfloat16)
+        wide = PACK // 2
+        for r in range(2):
+            for c in range(2):
+                out_ref[2 * r + c] = total[16 * r : 16 * r + 16, wide * c : wide * (c + 1)]
+
+
+def image_sums(keys, values, core, scale):
     images, tokens, width = keys.shape
-    spec = pl.BlockSpec((1, tokens, width), lambda i, at: (at[0], 0, 0))
+    out = jax.ShapeDtypeStruct((4, 16, PACK // 2), jnp.bfloat16)
+    vmem = pl.BlockSpec(memory_space=pltpu.VMEM)
+    hbm = pl.BlockSpec(memory_space=pl.ANY)
     return pl.pallas_call(
         functools.partial(sums_kernel, scale),
-        out_shape=jax.ShapeDtypeStruct((4, 16, PACK // 2), jnp.bfloat16),
-        grid_spec=pltpu.PrefetchScalarGridSpec(
-            num_scalar_prefetch=1,
-            grid=(1,),
-            in_specs=[spec, spec],
-            out_specs=pl.BlockSpec((4, 16, PACK // 2), lambda i, at: (0, 0, 0)),
-        ),
-        compiler_params=pltpu.CompilerParams(vmem_limit_bytes=32 << 20),
-        cost_estimate=pl.CostEstimate(flops=2 * tokens * width * 256, bytes_accessed=4 * tokens * width, transcendentals=0),
+        out_shape=[out, out],
+        in_specs=[pl.BlockSpec(memory_space=pltpu.SMEM), hbm, hbm],
+        out_specs=[vmem, vmem],
+        scratch_shapes=[
+            pltpu.VMEM(keys.shape, keys.dtype),
+            pltpu.VMEM(values.shape, values.dtype),
+            pltpu.SemaphoreType.DMA((images, 2, 2)),
+        ],
+        compiler_params=pltpu.CompilerParams(vmem_limit_bytes=58 << 20),
+        cost_estimate=pl.CostEstimate(flops=4 * tokens * width * 256, bytes_accessed=8 * tokens * width, transcendentals=0),
         name="image_sums",
-    )(image.reshape(1), keys, values)
+    )(core.reshape(1), keys, values)
 
 
 def attend_kernel(q_ref, kv_ref, w_ref, out_ref):
@@ -116,7 +135,7 @@
             pl.BlockSpec((width, channels), lambda i: (0, 0)),
         ],
         out_specs=pl.BlockSpec((1, tokens, channels), lambda i: (i, 0, 0)),
-        compiler_params=pltpu.CompilerParams(vmem_limit_bytes=32 << 20),
+        compiler_params=pltpu.CompilerParams(vmem_limit_bytes=24 << 20),
         cost_estimate=pl.CostEstimate(flops=2 * images * tokens * width * 512, bytes_accessed=2 * images * tokens * width, transcendentals=0),
         name="attend",
     )(queries, kv, weight)
@@ -134,7 +153,7 @@
     return total.astype(jnp.bfloat16)
 
 
-def sum_over_mesh(mine, other):
+def sum_over_mesh(mine, other, upscale):
     at_x = lax.axis_index("row") % 4
     core = lax.axis_index("col") % 2
     arrived = lax.ppermute(other, "col", xor_pairs(1))
@@ -150,13 +169,20 @@
         total = total + part.astype(jnp.float32)
     chunk = exchange_group(total.astype(jnp.bfloat16), "row", (4, 12, 8))
     chunk = exchange_group(chunk, "col", (2,))
-    chunk = exchange_group(chunk, "col", (4, 12, 10))
+    chunk, upscale = lax.optimization_barrier((chunk, upscale))
+    arrived = [lax.ppermute(chunk, "col", xor_pairs(d)) for d in (4, 12, 10)]
+    arrived, combined = lax.optimization_barrier((arrived, phases(upscale)))
+    total = chunk.astype(jnp.float32)
+    for part in arrived:
+        total = total + part.astype(jnp.float32)
+    chunk = total.astype(jnp.bfloat16)
     twin = lax.ppermute(chunk, "col", xor_pairs(1))
     both = jnp.where(core == 0, jnp.stack([chunk, twin]), jnp.stack([twin, chunk]))
     gathered = jnp.stack([both] + [lax.ppermute(both, "row", xor_pairs(d)) for d in (1, 2, 3)])
-    return jnp.stack(
+    whole = jnp.stack(
         [lax.dynamic_index_in_dim(gathered, at_x ^ c, 0, False) for c in range(4)], axis=1
     )
+    return whole, combined
 
 
 def extended(value, sides, width):
@@ -182,11 +208,11 @@
 
 
 def decode_kernel(
-    tiles, at_ref, lat_ref, entry_ref, gain_ref, residual_ref, upscale_ref, out_ref,
-    wide, dec, hid, taps, ref, centre, slope, mix,
+    tiles, at_ref, lat_ref, entry_ref, gain_ref, residual_ref, upscale_ref, out_hbm,
+    wide, dec, hid, taps, ref, centre, slope, mix, out_ref, sems,
 ):
     tile = 16
-    channels = out_ref.shape[-1]
+    channels = out_hbm.shape[-1]
     pitch = 24
     f32, bf16 = jnp.float32, jnp.bfloat16
     rows = tile + 4
@@ -274,17 +300,21 @@
         return jnp.dot(source, upscale_ref[3 * p + q], preferred_element_type=f32)
 
     middle = product(1, 1)
+    stores = []
     shared = (middle + product(1, 0), middle + product(1, 2))
     for a in range(2):
         between = product(2 * a, 1)
         for b in range(2):
             value = shared[b] + between + product(2 * a, 2 * b)
             write(mix.at[a], pl.ds(b, total, stride=2), value)
-    for y in range(tile):
-        for image in range(2):
-            at = 2 * tile * (2 * y + image)
-            for a in range(2):
-                out_ref[image, 2 * y + a] = read(mix.at[a], pl.ds(at, 2 * tile)).astype(bf16)
+        for y in range(tile):
+            for image in range(2):
+                at = 2 * tile * (2 * y + image)
+                out_ref[a, image, y] = read(mix.at[a], pl.ds(at, 2 * tile)).astype(bf16)
+        stores.append(pltpu.make_async_copy(out_ref.at[a], out_hbm.at[:, :, a], sems.at[a]))
+        stores[a].start()
+    for store in stores:
+        store.wait()
 
 
 def phases_kernel(w_ref, out_ref):
@@ -325,11 +355,11 @@
     total = images * tile * tile
     f32, bf16 = jnp.float32, jnp.bfloat16
     vmem = pl.BlockSpec(memory_space=pltpu.VMEM)
-    return pl.pallas_call(
+    out = pl.pallas_call(
         functools.partial(decode_kernel, tiles),
-        out_shape=jax.ShapeDtypeStruct((images, 2 * tile, 2 * tile, channels), bf16),
+        out_shape=jax.ShapeDtypeStruct((images, tile, 2, 2 * tile, channels), bf16),
         in_specs=[pl.BlockSpec(memory_space=pltpu.SMEM)] + [vmem] * 5,
-        out_specs=vmem,
+        out_specs=pl.BlockSpec(memory_space=pl.ANY),
         scratch_shapes=[
             pltpu.VMEM((images * (tile + 6) * pitch, 3 * latent.shape[-1]), bf16),
             pltpu.VMEM((channels // LANES, rows * pitch, LANES), f32),
@@ -339,8 +369,10 @@
             pltpu.VMEM((3, total, channels), bf16),
             pltpu.VMEM((3, total + images * tile, channels), bf16),
             pltpu.VMEM((2, channels // LANES, 2 * total, LANES), f32),
+            pltpu.VMEM((2, images, tile, 2 * tile, channels), bf16),
+            pltpu.SemaphoreType.DMA((2,)),
         ],
-        compiler_params=pltpu.CompilerParams(vmem_limit_bytes=44 << 20),
+        compiler_params=pltpu.CompilerParams(vmem_limit_bytes=38 << 20),
         cost_estimate=pl.CostEstimate(flops=8 * 10**9, bytes_accessed=12 << 20, transcendentals=0),
         name="decode",
     )(
@@ -351,6 +383,7 @@
         residual.reshape(9 * channels, channels),
         u,
     )
+    return out.reshape(images, 2 * tile, 2 * tile, channels)
 
 
 def local(
@@ -368,9 +401,8 @@
     flat = (images, tile * tile, width)
     keys, values = key_rows_per_head.reshape(flat), value_rows_per_head.reshape(flat)
     core = (lax.axis_index("col") % 2).astype(jnp.int32)
-    other = image_sums(keys, values, 1 - core, scale)
-    mine = image_sums(keys, values, core, scale)
-    kv = sum_over_mesh(mine, other)
+    mine, other = image_sums(keys, values, core, scale)
+    kv, combined = sum_over_mesh(mine, other, upscale_conv_weight)
     latent = attend(queries.reshape(flat), kv, latent_projection_weight)
     latent = latent.reshape(images, tile, tile, latent.shape[-1])
     widened = extended(latent, (("row", 1), ("col", 2)), 3)
@@ -382,7 +414,7 @@
         entry_conv_weight,
         residual_norm_gain,
         residual_conv_weight,
-        phases(upscale_conv_weight),
+        combined,
         tiles,
     )
 

time: 88.1 us -> 89.6 us (1.017)
  the two profiles are of different devices: /device:TPU:23 before, /device:TPU:119 now
where the time goes in v1:
time: 89.6 us; the launch traced here: 89.3 us
  starting transfers between devices  39.6 us (44%)
  waiting for transfers between devices  21.1 us (24%)
  Pallas kernels  19.4 us (22%)
  local copies, waits for them, and re-layouts  7.3 us (8%)
  other arithmetic  1.38 us (2%)
    ppermute x2, starting transfers between devices, extended(): before = lax.ppermute(last, axis, up)  13.5 us
    ppermute x2, waiting for transfers between devices, extended(): after = lax.ppermute(initial, axis, down)  9.27 us
    pallas_call x1, Pallas kernels, decode(): pl.pallas_call(functools.partial(decode_kernel, tiles), out_shape=jax.Sha...  8.97 us
    unnamed x21, local copies, waits for them, and re-layouts  7.19 us
    ppermute x1, starting transfers between devices, sum_over_mesh(): twin = lax.ppermute(chunk, 'col', xor_pairs(1))  5.17 us
    ppermute x3, starting transfers between devices, sum_over_mesh(): arrived = [lax.ppermute(chunk, 'col', xor_pairs(d)) for d in (4, 12, 10)]  5.02 us
    pallas_call x1, Pallas kernels, attend(): pl.pallas_call(attend_kernel, out_shape=jax.ShapeDtypeStruct((images, tok...  4.91 us
    ppermute x4, waiting for transfers between devices, exchange_group(): arrived = [lax.ppermute(value, axis, xor_pairs(d)) for d in distances]  4.44 us
  transfers between devices with their start and end apart: 19, of which 11 were waited for; matrix products, arithmetic and copies ran while one was open for 0% of the time, Pallas kernels for 2%

profile of v1, /device:TPU:119, one launch (start us, length us, event | category | flops | bytes accessed | tf_op | source)
XLA Modules:
  0.0 89.3 jit_solution(8116563035119866194)
XLA Ops:
  0.0 3.6 %image_sums.1 = (bf16[4,16,1280]{2,1,0:T(8,128)(2,1)}, bf16[4,16,1280]{2,1,0:T(8,128)(2,1)}) custom-call(s32[1]{0:T(128)} %bitcast.3.core_ref, bf16[2,256,2240]{2,1,0:T(8,128)(2,1)} %bitcast.52, bf16[2,256,2240]{2,1,0:T(8,128)(2,1)} %bitcast.53), custom_call_target="tpu_custom_call" | custom-call | flops 587202560 | bytes 4587520 | tf_op jit(solution)/shard_map/image_sums/pallas_call | solution.py:67
  3.6 0.8 collective-permute-start
  4.4 1.2 %collective-permute-done = bf16[4,16,1280]{2,1,0:T(8,128)(2,1)S(1)} collective-permute-done((bf16[4,16,1280]{2,1,0:T(8,128)(2,1)}, bf16[4,16,1280]{2,1,0:T(8,128)(2,1)S(1)}, u32[]{:S(2)}, u32[]{:S(2)}) %collective-permute-start) | collective-permute-done | bytes 163872 | tf_op jit(solution)/shard_map/ppermute | solution.py:159
  5.6 0.9 %convert_add_fusion = f32[4,16,1280]{2,1,0:T(8,128)S(1)} fusion(bf16[4,16,1280]{2,1,0:T(8,128)(2,1)S(1)} %collective-permute-done, bf16[4,16,1280]{2,1,0:T(8,128)(2,1)} %get-tuple-element.13), kind=kLoop, calls=%fused_computation.9 | loop fusion | flops 245760 | bytes 655360 | tf_op jit(solution)/shard_map/add | solution.py:160
  6.6 0.6 collective-permute-start.1
  7.2 0.8 collective-permute-start.3
  8.1 2.5 %collective-permute-start.2 = (bf16[16,1280]{1,0:T(8,128)(2,1)S(1)}, bf16[16,1280]{1,0:T(8,128)(2,1)S(1)}, u32[]{:S(2)}, u32[]{:S(2)}) collective-permute-start(bf16[16,1280]{1,0:T(8,128)(2,1)S(1)} %get-tuple-element.27), channel_id=1, source_target_pairs={{0,48},{16,32},{32,16},{48,0},{64,112},{80,96},{96,80},{112,64},{1... | collective-permute-start | bytes 122888 | tf_op jit(solution)/shard_map/ppermute | solution.py:162
  10.5 1.0 %collective-permute-done.3 = bf16[16,1280]{1,0:T(8,128)(2,1)S(1)} collective-permute-done((bf16[16,1280]{1,0:T(8,128)(2,1)S(1)}, bf16[16,1280]{1,0:T(8,128)(2,1)S(1)}, u32[]{:S(2)}, u32[]{:S(2)}) %collective-permute-start.3) | collective-permute-done | bytes 40992 | tf_op jit(solution)/shard_map/ppermute | solution.py:162
  12.3 2.1 %collective-permute-start.5 = (bf16[16,1280]{1,0:T(8,128)(2,1)S(1)}, bf16[16,1280]{1,0:T(8,128)(2,1)S(1)}, u32[]{:S(2)}, u32[]{:S(2)}) collective-permute-start(bf16[16,1280]{1,0:T(8,128)(2,1)S(1)} %fusion.8), channel_id=1, source_target_pairs={{0,192},{16,208},{32,224},{48,240},{64,128},{80,144},{96,160},{112... | collective-permute-start | bytes 122888 | tf_op jit(solution)/shard_map/ppermute | solution.py:149
  14.4 1.7 %collective-permute-start.4 = (bf16[16,1280]{1,0:T(8,128)(2,1)S(1)}, bf16[16,1280]{1,0:T(8,128)(2,1)S(1)}, u32[]{:S(2)}, u32[]{:S(2)}) collective-permute-start(bf16[16,1280]{1,0:T(8,128)(2,1)S(1)} %fusion.8), channel_id=1, source_target_pairs={{0,64},{16,80},{32,96},{48,112},{64,0},{80,16},{96,32},{112,48},{1... | collective-permute-start | bytes 122888 | tf_op jit(solution)/shard_map/ppermute | solution.py:149
  16.6 0.9 collective-permute-done.4
  17.6 3.1 %collective-permute-done.7 = bf16[16,1280]{1,0:T(8,128)(2,1)S(1)} collective-permute-done((bf16[16,1280]{1,0:T(8,128)(2,1)S(1)}, bf16[16,1280]{1,0:T(8,128)(2,1)S(1)}, u32[]{:S(2)}, u32[]{:S(2)}) %collective-permute-start.7) | collective-permute-done | bytes 40992 | tf_op jit(solution)/shard_map/ppermute | solution.py:149
  20.7 3.8 %collective-permute-start.10 = (bf16[16,1280]{1,0:T(8,128)(2,1)S(1)}, bf16[16,1280]{1,0:T(8,128)(2,1)S(1)}, u32[]{:S(2)}, u32[]{:S(2)}) collective-permute-start(bf16[16,1280]{1,0:T(8,128)(2,1)S(1)} %add_convert_fusion.1), channel_id=1, source_target_pairs={{0,10},{1,11},{2,8},{3,9},{4,14},{5,15},{6,12},{7,13},{8,2},{9,3},... | collective-permute-start | bytes 122888 | tf_op jit(solution)/shard_map/ppermute | solution.py:173
  24.5 1.2 %collective-permute-start.8 = (bf16[16,1280]{1,0:T(8,128)(2,1)S(1)}, bf16[16,1280]{1,0:T(8,128)(2,1)S(1)}, u32[]{:S(2)}, u32[]{:S(2)}) collective-permute-start(bf16[16,1280]{1,0:T(8,128)(2,1)S(1)} %add_convert_fusion.1), channel_id=1, source_target_pairs={{0,4},{1,5},{2,6},{3,7},{4,0},{5,1},{6,2},{7,3},{8,12},{9,13},{10,... | collective-permute-start | bytes 122888 | tf_op jit(solution)/shard_map/ppermute | solution.py:173
  25.7 2.3 %copy-done = bf16[3,3,512,512]{3,2,1,0:T(8,128)(2,1)S(1)} copy-done((bf16[3,3,512,512]{3,2,1,0:T(8,128)(2,1)S(1)}, bf16[3,3,512,512]{3,2,1,0:T(8,128)(2,1)}, u32[]{:S(2)}) %copy-start) | copy-done | bytes 4718616
  28.1 2.0 %phases.1.upscale_ref = bf16[9,512,512]{2,1,0:T(8,128)(2,1)S(1)} custom-call(bf16[9,512,512]{2,1,0:T(8,128)(2,1)S(1)} %bitcast.44), custom_call_target="tpu_custom_call" | custom-call | flops 2621440 | bytes 9437184 | tf_op jit(solution)/shard_map/phases/pallas_call | solution.py:335
  30.0 2.1 %copy-done.1 = bf16[9,512,512]{2,1,0:T(8,128)(2,1)} copy-done((bf16[9,512,512]{2,1,0:T(8,128)(2,1)}, bf16[9,512,512]{2,1,0:T(8,128)(2,1)S(1)}, u32[]{:S(2)}) %copy-start.1) | copy-done | bytes 4718616
  32.2 5.2 %collective-permute-start.11 = (bf16[16,1280]{1,0:T(8,128)(2,1)S(1)}, bf16[16,1280]{1,0:T(8,128)(2,1)S(1)}, u32[]{:S(2)}, u32[]{:S(2)}) collective-permute-start(bf16[16,1280]{1,0:T(8,128)(2,1)S(1)} %add_convert_fusion), channel_id=1, source_target_pairs={{0,1},{1,0},{2,3},{3,2},{4,5},{5,4},{6,7},{7,6},{8,9},{9,8},{10,11... | collective-permute-start | bytes 122888 | tf_op jit(solution)/shard_map/ppermute | solution.py:179
  37.7 0.6 collective-permute-done.11
  38.3 2.6 %collective-permute-start.14 = (bf16[2,16,1280]{2,1,0:T(8,128)(2,1)S(1)}, bf16[2,16,1280]{2,1,0:T(8,128)(2,1)S(1)}, u32[]{:S(2)}, u32[]{:S(2)}) collective-permute-start(bf16[2,16,1280]{2,1,0:T(8,128)(2,1)S(1)} %maximum_select_fusion.1), channel_id=1, source_target_pairs={{0,48},{16,32},{32,16},{48,0},{64,112},{80,96},{96,80},{112,64},{1... | collective-permute-start | bytes 245768 | tf_op jit(solution)/shard_map/ppermute | solution.py:181
  40.9 0.8 collective-permute-start.12
  41.7 1.7 %collective-permute-done.14 = bf16[2,16,1280]{2,1,0:T(8,128)(2,1)S(1)} collective-permute-done((bf16[2,16,1280]{2,1,0:T(8,128)(2,1)S(1)}, bf16[2,16,1280]{2,1,0:T(8,128)(2,1)S(1)}, u32[]{:S(2)}, u32[]{:S(2)}) %collective-permute-start.14) | collective-permute-done | bytes 81952 | tf_op jit(solution)/shard_map/ppermute | solution.py:181
  43.4 2.3 %collective-permute-done.13 = bf16[2,16,1280]{2,1,0:T(8,128)(2,1)S(1)} collective-permute-done((bf16[2,16,1280]{2,1,0:T(8,128)(2,1)S(1)}, bf16[2,16,1280]{2,1,0:T(8,128)(2,1)S(1)}, u32[]{:S(2)}, u32[]{:S(2)}) %collective-permute-start.13) | collective-permute-done | bytes 81952 | tf_op jit(solution)/shard_map/ppermute | solution.py:181
  45.8 4.9 %attend.1 = bf16[2,256,32]{2,1,0:T(8,128)(2,1)S(1)} custom-call(bf16[2,256,2240]{2,1,0:T(8,128)(2,1)S(1)} %bitcast.49, bf16[2,4,16,1280]{3,2,1,0:T(8,128)(2,1)S(1)} %pad_maximum_fusion.1.kv_ref, bf16[2240,32]{1,0:T(8,128)(2,1)S(1)} %copy.9.w_ref), custom_call_target="tpu_custom_call" | custom-call | flops 1174405120 | bytes 2293760 | tf_op jit(solution)/shard_map/attend/pallas_call | solution.py:128
  50.8 5.4 %collective-permute-start.15 = (bf16[2,3,16,32]{3,2,0,1:T(8,128)(2,1)S(1)}, bf16[2,3,16,32]{3,2,0,1:T(8,128)(2,1)S(1)}, u32[]{:S(2)}, u32[]{:S(2)}) collective-permute-start(bf16[2,3,16,32]{3,2,0,1:T(8,128)(2,1)S(1)} %copy.14), channel_id=1, source_target_pairs={{0,16},{16,32},{32,48},{48,64},{64,80},{80,96},{96,112},{112,128},... | collective-permute-start | bytes 18440 | tf_op jit(solution)/shard_map/ppermute | solution.py:195
  56.2 1.9 %collective-permute-start.16 = (bf16[2,3,16,32]{3,2,0,1:T(8,128)(2,1)S(1)}, bf16[2,3,16,32]{3,2,0,1:T(8,128)(2,1)S(1)}, u32[]{:S(2)}, u32[]{:S(2)}) collective-permute-start(bf16[2,3,16,32]{3,2,0,1:T(8,128)(2,1)S(1)} %copy.15), channel_id=1, source_target_pairs={{16,0},{32,16},{48,32},{64,48},{80,64},{96,80},{112,96},{128,112},... | collective-permute-start | bytes 18440 | tf_op jit(solution)/shard_map/ppermute | solution.py:196
  58.2 4.7 %collective-permute-done.16 = bf16[2,3,16,32]{3,2,0,1:T(8,128)(2,1)S(1)} collective-permute-done((bf16[2,3,16,32]{3,2,0,1:T(8,128)(2,1)S(1)}, bf16[2,3,16,32]{3,2,0,1:T(8,128)(2,1)S(1)}, u32[]{:S(2)}, u32[]{:S(2)}) %collective-permute-start.16) | collective-permute-done | bytes 6176 | tf_op jit(solution)/shard_map/ppermute | solution.py:196
  62.9 8.1 %collective-permute-start.17 = (bf16[2,22,3,32]{3,2,0,1:T(4,128)(2,1)S(1)}, bf16[2,22,3,32]{3,2,0,1:T(4,128)(2,1)S(1)}, u32[]{:S(2)}, u32[]{:S(2)}) collective-permute-start(bf16[2,22,3,32]{3,2,0,1:T(4,128)(2,1)S(1)} %get-tuple-element.28), channel_id=1, source_target_pairs={{0,1},{1,2},{2,3},{3,4},{4,5},{5,6},{6,7},{7,8},{8,9},{9,10},{10,1... | collective-permute-start | bytes 25352 | tf_op jit(solution)/shard_map/ppermute | solution.py:195
  71.1 1.9 %collective-permute-start.18 = (bf16[2,22,3,32]{3,2,0,1:T(4,128)(2,1)S(1)}, bf16[2,22,3,32]{3,2,0,1:T(4,128)(2,1)S(1)}, u32[]{:S(2)}, u32[]{:S(2)}) collective-permute-start(bf16[2,22,3,32]{3,2,0,1:T(4,128)(2,1)S(1)} %get-tuple-element.29), channel_id=1, source_target_pairs={{1,0},{2,1},{3,2},{4,3},{5,4},{6,5},{7,6},{8,7},{9,8},{10,9},{11,1... | collective-permute-start | bytes 25352 | tf_op jit(solution)/shard_map/ppermute | solution.py:196
  73.1 4.6 %collective-permute-done.18 = bf16[2,22,3,32]{3,2,0,1:T(4,128)(2,1)S(1)} collective-permute-done((bf16[2,22,3,32]{3,2,0,1:T(4,128)(2,1)S(1)}, bf16[2,22,3,32]{3,2,0,1:T(4,128)(2,1)S(1)}, u32[]{:S(2)}, u32[]{:S(2)}) %collective-permute-start.18) | collective-permute-done | bytes 8480 | tf_op jit(solution)/shard_map/ppermute | solution.py:196
  77.9 2.3 %copy-done.3 = bf16[3,3,512,512]{3,2,1,0:T(8,128)(2,1)S(1)} copy-done((bf16[3,3,512,512]{3,2,1,0:T(8,128)(2,1)S(1)}, bf16[3,3,512,512]{3,2,1,0:T(8,128)(2,1)}, u32[]{:S(2)}) %copy-start.3) | copy-done | bytes 4718616
  80.2 9.0 %decode.1 = bf16[2,16,2,32,512]{4,3,2,1,0:T(8,128)(2,1)} custom-call(s32[2]{0:T(128)S(1)} %pad_add_fusion.at_ref, f32[44,32,32]{2,1,0:T(8,128)S(1)} %bitcast.45, bf16[3,96,512]{2,1,0:T(8,128)(2,1)S(1)} %bitcast.50, f32[1,512]{1,0:T(1,128)S(1)} %bitcast.51, bf16[4608,512]{1,0:T(8,128)(2,1)S(1)} %bitcast.48, bf16[9,512,512]{2,1,0:T(8,128)(2,1)S(1)} %copy-done.2), custom_call_target="tpu_custom_call" | custom-call | flops 8000000000 | bytes 12582912 | tf_op jit(solution)/shard_map/decode/pallas_call | solution.py:358
  (47 shorter events, 2.2 us)
Async XLA Ops:
  3.6 2.0 %collective-permute-start = (bf16[4,16,1280]{2,1,0:T(8,128)(2,1)}, bf16[4,16,1280]{2,1,0:T(8,128)(2,1)S(1)}, u32[]{:S(2)}, u32[]{:S(2)}) collective-permute-start(bf16[4,16,1280]{2,1,0:T(8,128)(2,1)} %get-tuple-element.14), channel_id=1, source_target_pairs={{0,1},{1,0},{2,3},{3,2},{4,5},{5,4},{6,7},{7,6},{8,9},{9,8},{10,11... | collective-permute-start | bytes 491528 | tf_op jit(solution)/shard_map/ppermute | solution.py:159
  6.6 3.9 %collective-permute-start.1 = (bf16[16,1280]{1,0:T(8,128)(2,1)S(1)}, bf16[16,1280]{1,0:T(8,128)(2,1)S(1)}, u32[]{:S(2)}, u32[]{:S(2)}) collective-permute-start(bf16[16,1280]{1,0:T(8,128)(2,1)S(1)} %get-tuple-element.25), channel_id=1, source_target_pairs={{0,16},{16,0},{32,48},{48,32},{64,80},{80,64},{96,112},{112,96},{1... | collective-permute-start | bytes 122888 | tf_op jit(solution)/shard_map/ppermute | solution.py:162
  7.2 4.4 %collective-permute-start.3 = (bf16[16,1280]{1,0:T(8,128)(2,1)S(1)}, bf16[16,1280]{1,0:T(8,128)(2,1)S(1)}, u32[]{:S(2)}, u32[]{:S(2)}) collective-permute-start(bf16[16,1280]{1,0:T(8,128)(2,1)S(1)} %get-tuple-element.26), channel_id=1, source_target_pairs={{0,32},{16,48},{32,0},{48,16},{64,96},{80,112},{96,64},{112,80},{1... | collective-permute-start | bytes 122888 | tf_op jit(solution)/shard_map/ppermute | solution.py:162
  8.1 4.1 %collective-permute-start.2 = (bf16[16,1280]{1,0:T(8,128)(2,1)S(1)}, bf16[16,1280]{1,0:T(8,128)(2,1)S(1)}, u32[]{:S(2)}, u32[]{:S(2)}) collective-permute-start(bf16[16,1280]{1,0:T(8,128)(2,1)S(1)} %get-tuple-element.27), channel_id=1, source_target_pairs={{0,48},{16,32},{32,16},{48,0},{64,112},{80,96},{96,80},{112,64},{1... | collective-permute-start | bytes 122888 | tf_op jit(solution)/shard_map/ppermute | solution.py:162
  12.2 4.4 %collective-permute-start.6 = (bf16[16,1280]{1,0:T(8,128)(2,1)S(1)}, bf16[16,1280]{1,0:T(8,128)(2,1)S(1)}, u32[]{:S(2)}, u32[]{:S(2)}) collective-permute-start(bf16[16,1280]{1,0:T(8,128)(2,1)S(1)} %fusion.8), channel_id=1, source_target_pairs={{0,128},{16,144},{32,160},{48,176},{64,192},{80,208},{96,224},{112... | collective-permute-start | bytes 122888 | tf_op jit(solution)/shard_map/ppermute | solution.py:149
  12.3 4.3 %collective-permute-start.5 = (bf16[16,1280]{1,0:T(8,128)(2,1)S(1)}, bf16[16,1280]{1,0:T(8,128)(2,1)S(1)}, u32[]{:S(2)}, u32[]{:S(2)}) collective-permute-start(bf16[16,1280]{1,0:T(8,128)(2,1)S(1)} %fusion.8), channel_id=1, source_target_pairs={{0,192},{16,208},{32,224},{48,240},{64,128},{80,144},{96,160},{112... | collective-permute-start | bytes 122888 | tf_op jit(solution)/shard_map/ppermute | solution.py:149
  14.4 3.1 %collective-permute-start.4 = (bf16[16,1280]{1,0:T(8,128)(2,1)S(1)}, bf16[16,1280]{1,0:T(8,128)(2,1)S(1)}, u32[]{:S(2)}, u32[]{:S(2)}) collective-permute-start(bf16[16,1280]{1,0:T(8,128)(2,1)S(1)} %fusion.8), channel_id=1, source_target_pairs={{0,64},{16,80},{32,96},{48,112},{64,0},{80,16},{96,32},{112,48},{1... | collective-permute-start | bytes 122888 | tf_op jit(solution)/shard_map/ppermute | solution.py:149
  17.5 3.2 %collective-permute-start.7 = (bf16[16,1280]{1,0:T(8,128)(2,1)S(1)}, bf16[16,1280]{1,0:T(8,128)(2,1)S(1)}, u32[]{:S(2)}, u32[]{:S(2)}) collective-permute-start(bf16[16,1280]{1,0:T(8,128)(2,1)S(1)} %add_convert_fusion.2), channel_id=1, source_target_pairs={{0,2},{1,3},{2,0},{3,1},{4,6},{5,7},{6,4},{7,5},{8,10},{9,11},{10,... | collective-permute-start | bytes 122888 | tf_op jit(solution)/shard_map/ppermute | solution.py:149
  20.7 11.5 %collective-permute-start.10 = (bf16[16,1280]{1,0:T(8,128)(2,1)S(1)}, bf16[16,1280]{1,0:T(8,128)(2,1)S(1)}, u32[]{:S(2)}, u32[]{:S(2)}) collective-permute-start(bf16[16,1280]{1,0:T(8,128)(2,1)S(1)} %add_convert_fusion.1), channel_id=1, source_target_pairs={{0,10},{1,11},{2,8},{3,9},{4,14},{5,15},{6,12},{7,13},{8,2},{9,3},... | collective-permute-start | bytes 122888 | tf_op jit(solution)/shard_map/ppermute | solution.py:173
  24.5 7.7 %collective-permute-start.9 = (bf16[16,1280]{1,0:T(8,128)(2,1)S(1)}, bf16[16,1280]{1,0:T(8,128)(2,1)S(1)}, u32[]{:S(2)}, u32[]{:S(2)}) collective-permute-start(bf16[16,1280]{1,0:T(8,128)(2,1)S(1)} %add_convert_fusion.1), channel_id=1, source_target_pairs={{0,12},{1,13},{2,14},{3,15},{4,8},{5,9},{6,10},{7,11},{8,4},{9,5},... | collective-permute-start | bytes 122888 | tf_op jit(solution)/shard_map/ppermute | solution.py:173
  24.5 7.7 %collective-permute-start.8 = (bf16[16,1280]{1,0:T(8,128)(2,1)S(1)}, bf16[16,1280]{1,0:T(8,128)(2,1)S(1)}, u32[]{:S(2)}, u32[]{:S(2)}) collective-permute-start(bf16[16,1280]{1,0:T(8,128)(2,1)S(1)} %add_convert_fusion.1), channel_id=1, source_target_pairs={{0,4},{1,5},{2,6},{3,7},{4,0},{5,1},{6,2},{7,3},{8,12},{9,13},{10,... | collective-permute-start | bytes 122888 | tf_op jit(solution)/shard_map/ppermute | solution.py:173
  25.7 2.3 %copy-start = (bf16[3,3,512,512]{3,2,1,0:T(8,128)(2,1)S(1)}, bf16[3,3,512,512]{3,2,1,0:T(8,128)(2,1)}, u32[]{:S(2)}) copy-start(bf16[3,3,512,512]{3,2,1,0:T(8,128)(2,1)} %param.15) | copy-start | bytes 14155780
  28.0 9.4 %copy-start.7 = (bf16[2240,32]{0,1:T(8,128)(2,1)S(1)}, bf16[2240,32]{0,1:T(8,128)(2,1)}, u32[]{:S(2)}) copy-start(bf16[2240,32]{0,1:T(8,128)(2,1)} %param.11) | copy-start | bytes 430084
  30.0 2.2 %copy-start.1 = (bf16[9,512,512]{2,1,0:T(8,128)(2,1)}, bf16[9,512,512]{2,1,0:T(8,128)(2,1)S(1)}, u32[]{:S(2)}) copy-start(bf16[9,512,512]{2,1,0:T(8,128)(2,1)S(1)} %phases.1.upscale_ref) | copy-start | bytes 14155780
  32.2 13.6 %copy-start.4 = (bf16[2,16,16,2240]{3,2,1,0:T(8,128)(2,1)S(1)}, bf16[2,16,16,2240]{3,2,1,0:T(8,128)(2,1)}, u32[]{:S(2)}) copy-start(bf16[2,16,16,2240]{3,2,1,0:T(8,128)(2,1)} %param.8) | copy-start | bytes 6881284
  32.2 6.0 %collective-permute-start.11 = (bf16[16,1280]{1,0:T(8,128)(2,1)S(1)}, bf16[16,1280]{1,0:T(8,128)(2,1)S(1)}, u32[]{:S(2)}, u32[]{:S(2)}) collective-permute-start(bf16[16,1280]{1,0:T(8,128)(2,1)S(1)} %add_convert_fusion), channel_id=1, source_target_pairs={{0,1},{1,0},{2,3},{3,2},{4,5},{5,4},{6,7},{7,6},{8,9},{9,8},{10,11... | collective-permute-start | bytes 122888 | tf_op jit(solution)/shard_map/ppermute | solution.py:179
  38.3 5.1 %collective-permute-start.14 = (bf16[2,16,1280]{2,1,0:T(8,128)(2,1)S(1)}, bf16[2,16,1280]{2,1,0:T(8,128)(2,1)S(1)}, u32[]{:S(2)}, u32[]{:S(2)}) collective-permute-start(bf16[2,16,1280]{2,1,0:T(8,128)(2,1)S(1)} %maximum_select_fusion.1), channel_id=1, source_target_pairs={{0,48},{16,32},{32,16},{48,0},{64,112},{80,96},{96,80},{112,64},{1... | collective-permute-start | bytes 245768 | tf_op jit(solution)/shard_map/ppermute | solution.py:181
  40.9 4.8 %collective-permute-start.13 = (bf16[2,16,1280]{2,1,0:T(8,128)(2,1)S(1)}, bf16[2,16,1280]{2,1,0:T(8,128)(2,1)S(1)}, u32[]{:S(2)}, u32[]{:S(2)}) collective-permute-start(bf16[2,16,1280]{2,1,0:T(8,128)(2,1)S(1)} %maximum_select_fusion.1), channel_id=1, source_target_pairs={{0,32},{16,48},{32,0},{48,16},{64,96},{80,112},{96,64},{112,80},{1... | collective-permute-start | bytes 245768 | tf_op jit(solution)/shard_map/ppermute | solution.py:181
  40.9 4.8 %collective-permute-start.12 = (bf16[2,16,1280]{2,1,0:T(8,128)(2,1)S(1)}, bf16[2,16,1280]{2,1,0:T(8,128)(2,1)S(1)}, u32[]{:S(2)}, u32[]{:S(2)}) collective-permute-start(bf16[2,16,1280]{2,1,0:T(8,128)(2,1)S(1)} %maximum_select_fusion.1), channel_id=1, source_target_pairs={{0,16},{16,0},{32,48},{48,32},{64,80},{80,64},{96,112},{112,96},{1... | collective-permute-start | bytes 245768 | tf_op jit(solution)/shard_map/ppermute | solution.py:181
  45.8 32.0 %copy-start.2 = (bf16[9,512,512]{2,1,0:T(8,128)(2,1)S(1)}, bf16[9,512,512]{2,1,0:T(8,128)(2,1)}, u32[]{:S(2)}) copy-start(bf16[9,512,512]{2,1,0:T(8,128)(2,1)} %copy-done.1) | copy-start | bytes 14155780
  45.8 32.0 %copy-start.5 = (bf16[3,3,32,512]{3,2,1,0:T(8,128)(2,1)S(1)}, bf16[3,3,32,512]{3,2,1,0:T(8,128)(2,1)}, u32[]{:S(2)}) copy-start(bf16[3,3,32,512]{3,2,1,0:T(8,128)(2,1)} %param.12) | copy-start | bytes 884740
  45.8 32.0 %copy-start.6 = (f32[512]{0:T(512)S(1)}, f32[512]{0:T(512)}, u32[]{:S(2)}) copy-start(f32[512]{0:T(512)} %param.13) | copy-start | bytes 6148
  50.8 7.3 %collective-permute-start.15 = (bf16[2,3,16,32]{3,2,0,1:T(8,128)(2,1)S(1)}, bf16[2,3,16,32]{3,2,0,1:T(8,128)(2,1)S(1)}, u32[]{:S(2)}, u32[]{:S(2)}) collective-permute-start(bf16[2,3,16,32]{3,2,0,1:T(8,128)(2,1)S(1)} %copy.14), channel_id=1, source_target_pairs={{0,16},{16,32},{32,48},{48,64},{64,80},{80,96},{96,112},{112,128},... | collective-permute-start | bytes 18440 | tf_op jit(solution)/shard_map/ppermute | solution.py:195
  56.2 6.7 %collective-permute-start.16 = (bf16[2,3,16,32]{3,2,0,1:T(8,128)(2,1)S(1)}, bf16[2,3,16,32]{3,2,0,1:T(8,128)(2,1)S(1)}, u32[]{:S(2)}, u32[]{:S(2)}) collective-permute-start(bf16[2,3,16,32]{3,2,0,1:T(8,128)(2,1)S(1)} %copy.15), channel_id=1, source_target_pairs={{16,0},{32,16},{48,32},{64,48},{80,64},{96,80},{112,96},{128,112},... | collective-permute-start | bytes 18440 | tf_op jit(solution)/shard_map/ppermute | solution.py:196
  62.9 10.2 %collective-permute-start.17 = (bf16[2,22,3,32]{3,2,0,1:T(4,128)(2,1)S(1)}, bf16[2,22,3,32]{3,2,0,1:T(4,128)(2,1)S(1)}, u32[]{:S(2)}, u32[]{:S(2)}) collective-permute-start(bf16[2,22,3,32]{3,2,0,1:T(4,128)(2,1)S(1)} %get-tuple-element.28), channel_id=1, source_target_pairs={{0,1},{1,2},{2,3},{3,4},{4,5},{5,6},{6,7},{7,8},{8,9},{9,10},{10,1... | collective-permute-start | bytes 25352 | tf_op jit(solution)/shard_map/ppermute | solution.py:195
  71.1 6.6 %collective-permute-start.18 = (bf16[2,22,3,32]{3,2,0,1:T(4,128)(2,1)S(1)}, bf16[2,22,3,32]{3,2,0,1:T(4,128)(2,1)S(1)}, u32[]{:S(2)}, u32[]{:S(2)}) collective-permute-start(bf16[2,22,3,32]{3,2,0,1:T(4,128)(2,1)S(1)} %get-tuple-element.29), channel_id=1, source_target_pairs={{1,0},{2,1},{3,2},{4,3},{5,4},{6,5},{7,6},{8,7},{9,8},{10,9},{11,1... | collective-permute-start | bytes 25352 | tf_op jit(solution)/shard_map/ppermute | solution.py:196
  77.8 2.3 %copy-start.3 = (bf16[3,3,512,512]{3,2,1,0:T(8,128)(2,1)S(1)}, bf16[3,3,512,512]{3,2,1,0:T(8,128)(2,1)}, u32[]{:S(2)}) copy-start(bf16[3,3,512,512]{3,2,1,0:T(8,128)(2,1)} %param.14) | copy-start | bytes 14155780

commit v2 on v1

--- a/solution.py
+++ b/solution.py
@@ -80,82 +80,102 @@
     )(core.reshape(1), keys, values)
 
 
-def attend_kernel(q_ref, kv_ref, w_ref, out_ref):
-    tokens, width = q_ref.shape[1:]
+def attend_kernel(at_ref, q_ref, piece0_ref, piece1_ref, piece2_ref, piece3_ref, weight_ref, out_ref, sums):
+    f32, bf16 = jnp.float32, jnp.bfloat16
+    images, tokens, width = q_ref.shape
     group = 2 * LANES
+    for n, piece in enumerate((piece0_ref, piece1_ref, piece2_ref, piece3_ref)):
+        sums[at_ref[2] ^ n] = piece[...]
     same = (
         lax.broadcasted_iota(jnp.int32, (group, group), 0) // HEAD
         == lax.broadcasted_iota(jnp.int32, (group, group), 1) // HEAD
     )
-    kv = jnp.concatenate(
-        [jnp.concatenate([kv_ref[0, 2 * r + c] for c in range(2)], axis=1) for r in range(2)], axis=0
-    )
-    key_means = kv[:, KS_AT : KS_AT + LANES]
-    head_of = lax.broadcasted_iota(jnp.int32, (LANES, group), 0)
-    lane_head = lax.broadcasted_iota(jnp.int32, (LANES, group), 1) // HEAD
-    squares = jnp.zeros((tokens, 1), jnp.float32)
-    latent = jnp.zeros((tokens, w_ref.shape[1]), jnp.float32)
+    same = same.astype(f32).astype(bf16)
+    head_of = lax.broadcasted_iota(jnp.int32, (LANES, PACK), 0)
+    lane_head = lax.broadcasted_iota(jnp.int32, (LANES, PACK), 1) // HEAD
+    spread = (head_of == lane_head).astype(f32).astype(bf16)
+    kv = [
+        jnp.concatenate(
+            [jnp.concatenate([sums[2 * r + c, image] for c in range(2)], axis=1) for r in range(2)], axis=0
+        )
+        for image in range(images)
+    ]
+    key_means = jnp.concatenate([part[:, KS_AT : KS_AT + LANES] for part in kv], axis=0)
+    means = jnp.dot(key_means, spread, preferred_element_type=f32).astype(bf16)
+    squares = [jnp.zeros((tokens, LANES), f32)] * images
+    latent = jnp.zeros((images * tokens, weight_ref.shape[0]), f32)
     for start in range(0, width, group):
         size = min(group, width - start)
-        spread = (head_of == lane_head + start // HEAD).astype(jnp.bfloat16)[:, :size]
-        means = jnp.dot(key_means, spread, preferred_element_type=jnp.float32).astype(jnp.bfloat16)
+        repeat = size // HEAD
         here = same[:size, :size]
-        zero = jnp.zeros((size, size), jnp.bfloat16)
-        numerator_weights = jnp.where(
-            here, jnp.concatenate([kv[:, start : start + size]] * (size // HEAD), axis=0), zero
+        parts = []
+        for image in range(images):
+            upper = kv[image][:, start : start + size]
+            lower = means[HEAD * image : HEAD * (image + 1), start : start + size]
+            query = jnp.maximum(q_ref[image, :, start : start + size], 0)
+            numerator = jnp.dot(
+                query, jnp.concatenate([upper] * repeat, axis=0) * here, preferred_element_type=f32
+            )
+            denominator = jnp.dot(
+                query, jnp.concatenate([lower] * repeat, axis=0) * here, preferred_element_type=f32
+            )
+            attended = numerator * pl.reciprocal(jnp.maximum(denominator, 1.0), approx=True)
+            square = attended * attended
+            for c in range(0, size, LANES):
+                part = square[:, c : min(c + LANES, size)]
+                if part.shape[1] < LANES:
+                    rest = jnp.zeros((tokens, LANES - part.shape[1]), f32)
+                    part = jnp.concatenate([part, rest], axis=1)
+                squares[image] += part
+            parts.append(attended.astype(bf16))
+        latent += lax.dot_general(
+            jnp.concatenate(parts, axis=0),
+            weight_ref[:, start : start + size],
+            (((1,), (1,)), ((), ())),
+            preferred_element_type=f32,
         )
-        denominator_weights = jnp.where(
-            here, jnp.concatenate([means] * (size // HEAD), axis=0), zero
-        )
-        query = jnp.maximum(q_ref[0, :, start : start + size], 0)
-        numerator = jnp.dot(query, numerator_weights, preferred_element_type=jnp.float32)
-        denominator = jnp.dot(query, denominator_weights, preferred_element_type=jnp.float32)
-        bound = jnp.maximum(denominator, 1.0)
-        inverse = pl.reciprocal(bound, approx=True)
-        attended = numerator * (inverse * (2.0 - bound * inverse))
-        squares += jnp.sum(attended * attended, axis=1, keepdims=True)
-        latent += jnp.dot(
-            attended.astype(jnp.bfloat16),
-            w_ref[start : start + size],
-            preferred_element_type=jnp.float32,
-        )
-    out_ref[0] = (latent * lax.rsqrt(squares / width + NORM_EPS)).astype(jnp.bfloat16)
-
-
-def attend(queries, kv, weight):
+    for image in range(images):
+        total = jnp.sum(squares[image], axis=1, keepdims=True)
+        normed = latent[tokens * image : tokens * (image + 1)] * lax.rsqrt(total / width + NORM_EPS)
+        out_ref[image] = normed.astype(bf16)
+
+
+def attend(at, queries, pieces, weight):
     images, tokens, width = queries.shape
     channels = weight.shape[1]
+    vmem = pl.BlockSpec(memory_space=pltpu.VMEM)
     return pl.pallas_call(
         attend_kernel,
         out_shape=jax.ShapeDtypeStruct((images, tokens, channels), jnp.bfloat16),
-        grid=(images,),
-        in_specs=[
-            pl.BlockSpec((1, tokens, width), lambda i: (i, 0, 0)),
-            pl.BlockSpec((1, 4, 16, PACK // 2), lambda i: (i, 0, 0, 0)),
-            pl.BlockSpec((width, channels), lambda i: (0, 0)),
-        ],
-        out_specs=pl.BlockSpec((1, tokens, channels), lambda i: (i, 0, 0)),
-        compiler_params=pltpu.CompilerParams(vmem_limit_bytes=24 << 20),
+        in_specs=[pl.BlockSpec(memory_space=pltpu.SMEM)] + [vmem] * 6,
+        out_specs=vmem,
+        scratch_shapes=[pltpu.VMEM((4, images, 16, PACK // 2), jnp.bfloat16)],
+        compiler_params=pltpu.CompilerParams(vmem_limit_bytes=32 << 20),
         cost_estimate=pl.CostEstimate(flops=2 * images * tokens * width * 512, bytes_accessed=2 * images * tokens * width, transcendentals=0),
         name="attend",
-    )(queries, kv, weight)
+    )(at, queries, *pieces, weight.T)
 
 
 def xor_pairs(distance):
     return [(i, i ^ distance) for i in range(16)]
 
 
-def exchange_group(value, axis, distances):
-    arrived = [lax.ppermute(value, axis, xor_pairs(d)) for d in distances]
+def added(value, arrived):
     total = value.astype(jnp.float32)
     for part in arrived:
         total = total + part.astype(jnp.float32)
     return total.astype(jnp.bfloat16)
 
 
-def sum_over_mesh(mine, other, upscale):
+def sent(value, axis, distances):
+    return [lax.ppermute(value, axis, xor_pairs(d)) for d in distances]
+
+
+def gather_all(mine, other, residual, upscale):
+    hold = lax.optimization_barrier
     at_x = lax.axis_index("row") % 4
-    core = lax.axis_index("col") % 2
+    first = lax.axis_index("col") % 2 == 0
+    mine, other, first = hold((mine, other, first))
     arrived = lax.ppermute(other, "col", xor_pairs(1))
     image = mine.astype(jnp.float32) + arrived.astype(jnp.float32)
     parts = [
@@ -164,25 +184,24 @@
         )
         for d in (1, 3, 2)
     ]
-    total = lax.dynamic_index_in_dim(image, at_x, 0, False)
-    for part in parts:
-        total = total + part.astype(jnp.float32)
-    chunk = exchange_group(total.astype(jnp.bfloat16), "row", (4, 12, 8))
-    chunk = exchange_group(chunk, "col", (2,))
-    chunk, upscale = lax.optimization_barrier((chunk, upscale))
-    arrived = [lax.ppermute(chunk, "col", xor_pairs(d)) for d in (4, 12, 10)]
-    arrived, combined = lax.optimization_barrier((arrived, phases(upscale)))
-    total = chunk.astype(jnp.float32)
-    for part in arrived:
-        total = total + part.astype(jnp.float32)
-    chunk = total.astype(jnp.bfloat16)
+    chunk = added(lax.dynamic_index_in_dim(image, at_x, 0, False), parts)
+
+    chunk, weights = hold((chunk, residual))
+    arrived = sent(chunk, "row", (4, 12, 8))
+    arrived, kept = hold((arrived, keep(weights)))
+    chunk = added(chunk, arrived)
+
+    chunk = added(chunk, sent(chunk, "col", (2,)))
+
+    chunk, weights = hold((chunk, upscale))
+    arrived = sent(chunk, "col", (4, 12, 10))
+    arrived, combined = hold((arrived, phases(weights)))
+    chunk = added(chunk, arrived)
+
     twin = lax.ppermute(chunk, "col", xor_pairs(1))
-    both = jnp.where(core == 0, jnp.stack([chunk, twin]), jnp.stack([twin, chunk]))
-    gathered = jnp.stack([both] + [lax.ppermute(both, "row", xor_pairs(d)) for d in (1, 2, 3)])
-    whole = jnp.stack(
-        [lax.dynamic_index_in_dim(gathered, at_x ^ c, 0, False) for c in range(4)], axis=1
-    )
-    return whole, combined
+    both = jnp.where(first, jnp.stack([chunk, twin]), jnp.stack([twin, chunk]))
+    pieces = [both] + sent(both, "row", (1, 2, 3))
+    return pieces, kept, combined
 
 
 def extended(value, sides, width):
@@ -317,34 +336,69 @@
         store.wait()
 
 
-def phases_kernel(w_ref, out_ref):
-    wide = [w_ref[t].astype(jnp.float32) for t in range(9)]
-    down = [
-        [wide[q], wide[q] + wide[3 + q] + wide[6 + q], -wide[6 + q]] for q in range(3)
-    ]
-    for p in range(3):
-        parts = [down[q][p] for q in range(3)]
-        out_ref[3 * p] = parts[0].astype(jnp.bfloat16)
-        out_ref[3 * p + 1] = (parts[0] + parts[1] + parts[2]).astype(jnp.bfloat16)
-        out_ref[3 * p + 2] = parts[2].astype(jnp.bfloat16)
+def keep_kernel(source_hbm, out_ref, sems):
+    parts = sems.shape[0]
+    size = source_hbm.shape[0] // parts
+    copies = []
+    for n in range(parts):
+        at = pl.ds(n * size, size)
+        copies.append(pltpu.make_async_copy(source_hbm.at[at], out_ref.at[at], sems.at[n]))
+        copies[n].start()
+    for copy in copies:
+        copy.wait()
+
+
+def keep(value):
+    return pl.pallas_call(
+        keep_kernel,
+        out_shape=pltpu.VMEM(value.shape, value.dtype),
+        in_specs=[pl.BlockSpec(memory_space=pl.ANY)],
+        out_specs=pl.BlockSpec(memory_space=pltpu.VMEM),
+        scratch_shapes=[pltpu.SemaphoreType.DMA((4,))],
+        compiler_params=pltpu.CompilerParams(vmem_limit_bytes=16 << 20),
+        cost_estimate=pl.CostEstimate(flops=0, bytes_accessed=2 * value.size, transcendentals=0),
+        name="keep",
+    )(value)
+
+
+def phases_kernel(w_hbm, out_ref, w_ref, sems):
+    parts = sems.shape[0]
+    size = w_hbm.shape[1] // parts
+    copies = []
+    for n in range(parts):
+        at = pl.ds(n * size, size)
+        copies.append(pltpu.make_async_copy(w_hbm.at[:, at], w_ref.at[:, at], sems.at[n]))
+        copies[n].start()
+    for n in range(parts):
+        copies[n].wait()
+        at = pl.ds(n * size, size)
+        wide = [w_ref[t, at].astype(jnp.float32) for t in range(9)]
+        down = [
+            [wide[q], wide[q] + wide[3 + q] + wide[6 + q], -wide[6 + q]] for q in range(3)
+        ]
+        for p in range(3):
+            left, middle, right = (down[q][p] for q in range(3))
+            out_ref[3 * p, at] = left.astype(jnp.bfloat16)
+            out_ref[3 * p + 1, at] = (left + middle + right).astype(jnp.bfloat16)
+            out_ref[3 * p + 2, at] = right.astype(jnp.bfloat16)
 
 
 def phases(upscale):
     deep, channels = upscale.shape[2:]
-    block = pl.BlockSpec((9, deep // 4, channels), lambda i: (0, i, 0))
+    shape = (9, deep, channels)
     return pl.pallas_call(
         phases_kernel,
-        out_shape=jax.ShapeDtypeStruct((9, deep, channels), jnp.bfloat16),
-        grid=(4,),
-        in_specs=[block],
-        out_specs=block,
-        compiler_params=pltpu.CompilerParams(vmem_limit_bytes=24 << 20),
-        cost_estimate=pl.CostEstimate(flops=10 * deep * channels, bytes_accessed=36 * deep * channels, transcendentals=0),
+        out_shape=pltpu.VMEM(shape, jnp.bfloat16),
+        in_specs=[pl.BlockSpec(memory_space=pl.ANY)],
+        out_specs=pl.BlockSpec(memory_space=pltpu.VMEM),
+        scratch_shapes=[pltpu.VMEM(shape, jnp.bfloat16), pltpu.SemaphoreType.DMA((8,))],
+        compiler_params=pltpu.CompilerParams(vmem_limit_bytes=32 << 20),
+        cost_estimate=pl.CostEstimate(flops=10 * deep * channels, bytes_accessed=18 * deep * channels, transcendentals=0),
         name="phases",
-    )(upscale.reshape(9, deep, channels))
-
-
-def decode(at, latent, entry, gain, residual, u, tiles):
+    )(upscale.reshape(shape))
+
+
+def decode(at, latent, entry, gain, residual, combined, tiles):
     images, tile = latent.shape[0], 16
     channels = entry.shape[-1]
     pitch = 24
@@ -355,11 +409,12 @@
     total = images * tile * tile
     f32, bf16 = jnp.float32, jnp.bfloat16
     vmem = pl.BlockSpec(memory_space=pltpu.VMEM)
+    hbm = pl.BlockSpec(memory_space=pl.ANY)
     out = pl.pallas_call(
         functools.partial(decode_kernel, tiles),
         out_shape=jax.ShapeDtypeStruct((images, tile, 2, 2 * tile, channels), bf16),
         in_specs=[pl.BlockSpec(memory_space=pltpu.SMEM)] + [vmem] * 5,
-        out_specs=pl.BlockSpec(memory_space=pl.ANY),
+        out_specs=hbm,
         scratch_shapes=[
             pltpu.VMEM((images * (tile + 6) * pitch, 3 * latent.shape[-1]), bf16),
             pltpu.VMEM((channels // LANES, rows * pitch, LANES), f32),
@@ -372,7 +427,7 @@
             pltpu.VMEM((2, images, tile, 2 * tile, channels), bf16),
             pltpu.SemaphoreType.DMA((2,)),
         ],
-        compiler_params=pltpu.CompilerParams(vmem_limit_bytes=38 << 20),
+        compiler_params=pltpu.CompilerParams(vmem_limit_bytes=40 << 20),
         cost_estimate=pl.CostEstimate(flops=8 * 10**9, bytes_accessed=12 << 20, transcendentals=0),
         name="decode",
     )(
@@ -380,8 +435,8 @@
         padded,
         entry.reshape(3, 3 * entry.shape[2], channels),
         gain.reshape(1, channels),
-        residual.reshape(9 * channels, channels),
-        u,
+        residual,
+        combined,
     )
     return out.reshape(images, 2 * tile, 2 * tile, channels)
 
@@ -402,20 +457,22 @@
     keys, values = key_rows_per_head.reshape(flat), value_rows_per_head.reshape(flat)
     core = (lax.axis_index("col") % 2).astype(jnp.int32)
     mine, other = image_sums(keys, values, core, scale)
-    kv, combined = sum_over_mesh(mine, other, upscale_conv_weight)
-    latent = attend(queries.reshape(flat), kv, latent_projection_weight)
+    channels = residual_conv_weight.shape[-1]
+    residual = residual_conv_weight.reshape(9 * channels, channels)
+    pieces, residual, combined = gather_all(mine, other, residual, upscale_conv_weight)
+    row, col = lax.axis_index("row"), lax.axis_index("col")
+    at = jnp.stack([row, col, row % 4]).astype(jnp.int32)
+    latent = attend(at, queries.reshape(flat), pieces, latent_projection_weight)
     latent = latent.reshape(images, tile, tile, latent.shape[-1])
     widened = extended(latent, (("row", 1), ("col", 2)), 3)
-    at = jnp.stack([lax.axis_index("row"), lax.axis_index("col")]).astype(jnp.int32)
-    tiles = (lax.axis_size("row"), lax.axis_size("col"))
     return decode(
         at,
         widened,
         entry_conv_weight,
         residual_norm_gain,
-        residual_conv_weight,
+        residual,
         combined,
-        tiles,
+        (lax.axis_size("row"), lax.axis_size("col")),
     )
 
 

time: 89.6 us -> 83.8 us (0.935)
  the two profiles are of different devices: /device:TPU:119 before, /device:TPU:15 now
where the time goes in v2:
time: 83.8 us; the launch traced here: 83.5 us
  starting transfers between devices  42 us (50%)
  waiting for transfers between devices  19.4 us (23%)
  Pallas kernels  18 us (21%)
  local copies, waits for them, and re-layouts  2.47 us (3%)
  other arithmetic  1.28 us (2%)
    ppermute x10, starting transfers between devices, sent(): return [lax.ppermute(value, axis, xor_pairs(d)) for d in distances]  16.6 us
    ppermute x2, starting transfers between devices, extended(): before = lax.ppermute(last, axis, up)  11.3 us
    pallas_call x1, Pallas kernels, decode(): pl.pallas_call(functools.partial(decode_kernel, tiles), out_shape=jax.Sha...  9.04 us
    ppermute x2, waiting for transfers between devices, extended(): after = lax.ppermute(initial, axis, down)  8.13 us
    ppermute x10, waiting for transfers between devices, sent(): return [lax.ppermute(value, axis, xor_pairs(d)) for d in distances]  7.61 us
    ppermute x1, starting transfers between devices, gather_all(): twin = lax.ppermute(chunk, 'col', xor_pairs(1))  5.58 us
    ppermute x3, starting transfers between devices, gather_all(): lax.ppermute(lax.dynamic_index_in_dim(image, at_x ^ d, 0, False).astype(j...  3.95 us
    ppermute x2, starting transfers between devices, extended(): after = lax.ppermute(initial, axis, down)  3.84 us
  transfers between devices with their start and end apart: 19, of which 10 were waited for; matrix products, arithmetic and copies ran while one was open for 0% of the time, Pallas kernels for 3%

profile of v2, /device:TPU:15, one launch (start us, length us, event | category | flops | bytes accessed | tf_op | source)
XLA Modules:
  0.0 83.5 jit_solution(10767251536161323580)
XLA Ops:
  0.0 3.6 %image_sums.1 = (bf16[4,16,1280]{2,1,0:T(8,128)(2,1)}, bf16[4,16,1280]{2,1,0:T(8,128)(2,1)}) custom-call(s32[1]{0:T(128)} %bitcast.4.core_ref, bf16[2,256,2240]{2,1,0:T(8,128)(2,1)} %bitcast.42, bf16[2,256,2240]{2,1,0:T(8,128)(2,1)} %bitcast.43), custom_call_target="tpu_custom_call" | custom-call | flops 587202560 | bytes 4587520 | tf_op jit(solution)/shard_map/image_sums/pallas_call | solution.py:67
  3.6 0.8 collective-permute-start
  4.4 1.2 %collective-permute-done = bf16[4,16,1280]{2,1,0:T(8,128)(2,1)S(1)} collective-permute-done((bf16[4,16,1280]{2,1,0:T(8,128)(2,1)}, bf16[4,16,1280]{2,1,0:T(8,128)(2,1)S(1)}, u32[]{:S(2)}, u32[]{:S(2)}) %collective-permute-start) | collective-permute-done | bytes 163872 | tf_op jit(solution)/shard_map/ppermute | solution.py:179
  5.6 0.9 %convert_add_fusion = f32[4,16,1280]{2,1,0:T(8,128)S(1)} fusion(bf16[4,16,1280]{2,1,0:T(8,128)(2,1)S(1)} %collective-permute-done, bf16[4,16,1280]{2,1,0:T(8,128)(2,1)} %get-tuple-element.25), kind=kLoop, calls=%fused_computation.7 | loop fusion | flops 245760 | bytes 655360 | tf_op jit(solution)/shard_map/add | solution.py:180
  7.2 0.8 collective-permute-start.3
  8.1 2.5 %collective-permute-start.2 = (bf16[16,1280]{1,0:T(8,128)(2,1)S(1)}, bf16[16,1280]{1,0:T(8,128)(2,1)S(1)}, u32[]{:S(2)}, u32[]{:S(2)}) collective-permute-start(bf16[16,1280]{1,0:T(8,128)(2,1)S(1)} %get-tuple-element.41), channel_id=1, source_target_pairs={{0,48},{16,32},{32,16},{48,0},{64,112},{80,96},{96,80},{112,64},{1... | collective-permute-start | bytes 122888 | tf_op jit(solution)/shard_map/ppermute | solution.py:182
  10.5 1.0 %collective-permute-done.3 = bf16[16,1280]{1,0:T(8,128)(2,1)S(1)} collective-permute-done((bf16[16,1280]{1,0:T(8,128)(2,1)S(1)}, bf16[16,1280]{1,0:T(8,128)(2,1)S(1)}, u32[]{:S(2)}, u32[]{:S(2)}) %collective-permute-start.3) | collective-permute-done | bytes 40992 | tf_op jit(solution)/shard_map/ppermute | solution.py:182
  12.2 2.1 %collective-permute-start.6 = (bf16[16,1280]{1,0:T(8,128)(2,1)S(1)}, bf16[16,1280]{1,0:T(8,128)(2,1)S(1)}, u32[]{:S(2)}, u32[]{:S(2)}) collective-permute-start(bf16[16,1280]{1,0:T(8,128)(2,1)S(1)} %fusion.8), channel_id=1, source_target_pairs={{0,128},{16,144},{32,160},{48,176},{64,192},{80,208},{96,224},{112... | collective-permute-start | bytes 122888 | tf_op jit(solution)/shard_map/ppermute | solution.py:171
  14.3 1.1 %collective-permute-start.5 = (bf16[16,1280]{1,0:T(8,128)(2,1)S(1)}, bf16[16,1280]{1,0:T(8,128)(2,1)S(1)}, u32[]{:S(2)}, u32[]{:S(2)}) collective-permute-start(bf16[16,1280]{1,0:T(8,128)(2,1)S(1)} %fusion.8), channel_id=1, source_target_pairs={{0,192},{16,208},{32,224},{48,240},{64,128},{80,144},{96,160},{112... | collective-permute-start | bytes 122888 | tf_op jit(solution)/shard_map/ppermute | solution.py:171
  15.3 0.8 collective-permute-start.4
  16.1 2.3 %copy-done = bf16[3,3,512,512]{3,2,1,0:T(8,128)(2,1)S(1)} copy-done((bf16[3,3,512,512]{3,2,1,0:T(8,128)(2,1)S(1)}, bf16[3,3,512,512]{3,2,1,0:T(8,128)(2,1)}, u32[]{:S(2)}) %copy-start) | copy-done | bytes 4718616
  18.4 1.0 %keep.1.residual_ref = bf16[4608,512]{1,0:T(8,128)(2,1)S(1)} custom-call(bf16[4608,512]{1,0:T(8,128)(2,1)S(1)} %bitcast.33), custom_call_target="tpu_custom_call" | custom-call | bytes 4718592 | tf_op jit(solution)/shard_map/keep/pallas_call | solution.py:352
  19.5 1.7 %collective-permute-start.7 = (bf16[16,1280]{1,0:T(8,128)(2,1)S(1)}, bf16[16,1280]{1,0:T(8,128)(2,1)S(1)}, u32[]{:S(2)}, u32[]{:S(2)}) collective-permute-start(bf16[16,1280]{1,0:T(8,128)(2,1)S(1)} %add_convert_fusion.2), channel_id=1, source_target_pairs={{0,2},{1,3},{2,0},{3,1},{4,6},{5,7},{6,4},{7,5},{8,10},{9,11},{10,... | collective-permute-start | bytes 122888 | tf_op jit(solution)/shard_map/ppermute | solution.py:171
  21.2 1.4 %collective-permute-done.7 = bf16[16,1280]{1,0:T(8,128)(2,1)S(1)} collective-permute-done((bf16[16,1280]{1,0:T(8,128)(2,1)S(1)}, bf16[16,1280]{1,0:T(8,128)(2,1)S(1)}, u32[]{:S(2)}, u32[]{:S(2)}) %collective-permute-start.7) | collective-permute-done | bytes 40992 | tf_op jit(solution)/shard_map/ppermute | solution.py:171
  22.6 6.4 %collective-permute-start.10 = (bf16[16,1280]{1,0:T(8,128)(2,1)S(1)}, bf16[16,1280]{1,0:T(8,128)(2,1)S(1)}, u32[]{:S(2)}, u32[]{:S(2)}) collective-permute-start(bf16[16,1280]{1,0:T(8,128)(2,1)S(1)} %add_convert_fusion.1), channel_id=1, source_target_pairs={{0,10},{1,11},{2,8},{3,9},{4,14},{5,15},{6,12},{7,13},{8,2},{9,3},... | collective-permute-start | bytes 122888 | tf_op jit(solution)/shard_map/ppermute | solution.py:171
  29.3 0.9 %collective-permute-start.8 = (bf16[16,1280]{1,0:T(8,128)(2,1)S(1)}, bf16[16,1280]{1,0:T(8,128)(2,1)S(1)}, u32[]{:S(2)}, u32[]{:S(2)}) collective-permute-start(bf16[16,1280]{1,0:T(8,128)(2,1)S(1)} %add_convert_fusion.1), channel_id=1, source_target_pairs={{0,4},{1,5},{2,6},{3,7},{4,0},{5,1},{6,2},{7,3},{8,12},{9,13},{10,... | collective-permute-start | bytes 122888 | tf_op jit(solution)/shard_map/ppermute | solution.py:171
  30.2 1.6 %phases.1.upscale_ref = bf16[9,512,512]{2,1,0:T(8,128)(2,1)S(1)} custom-call(bf16[9,512,512]{2,1,0:T(8,128)(2,1)S(1)} %bitcast.34), custom_call_target="tpu_custom_call" | custom-call | flops 2621440 | bytes 4718592 | tf_op jit(solution)/shard_map/phases/pallas_call | solution.py:389
  31.8 2.3 %collective-permute-done.9 = bf16[16,1280]{1,0:T(8,128)(2,1)S(1)} collective-permute-done((bf16[16,1280]{1,0:T(8,128)(2,1)S(1)}, bf16[16,1280]{1,0:T(8,128)(2,1)S(1)}, u32[]{:S(2)}, u32[]{:S(2)}) %collective-permute-start.9) | collective-permute-done | bytes 40992 | tf_op jit(solution)/shard_map/ppermute | solution.py:171
  34.1 5.6 %collective-permute-start.11 = (bf16[16,1280]{1,0:T(8,128)(2,1)S(1)}, bf16[16,1280]{1,0:T(8,128)(2,1)S(1)}, u32[]{:S(2)}, u32[]{:S(2)}) collective-permute-start(bf16[16,1280]{1,0:T(8,128)(2,1)S(1)} %add_convert_fusion), channel_id=1, source_target_pairs={{0,1},{1,0},{2,3},{3,2},{4,5},{5,4},{6,7},{7,6},{8,9},{9,8},{10,11... | collective-permute-start | bytes 122888 | tf_op jit(solution)/shard_map/ppermute | solution.py:201
  39.7 0.9 %collective-permute-done.11 = bf16[16,1280]{1,0:T(8,128)(2,1)S(1)} collective-permute-done((bf16[16,1280]{1,0:T(8,128)(2,1)S(1)}, bf16[16,1280]{1,0:T(8,128)(2,1)S(1)}, u32[]{:S(2)}, u32[]{:S(2)}) %collective-permute-start.11) | collective-permute-done | bytes 40992 | tf_op jit(solution)/shard_map/ppermute | solution.py:201
  40.6 2.6 %collective-permute-start.14 = (bf16[2,16,1280]{2,1,0:T(8,128)(2,1)S(1)}, bf16[2,16,1280]{2,1,0:T(8,128)(2,1)S(1)}, u32[]{:S(2)}, u32[]{:S(2)}) collective-permute-start(bf16[2,16,1280]{2,1,0:T(8,128)(2,1)S(1)} %maximum_select_fusion.piece0_ref), channel_id=1, source_target_pairs={{0,48},{16,32},{32,16},{48,0},{64,112},{80,96},{96,80},{112,64},{1... | collective-permute-start | bytes 245768 | tf_op jit(solution)/shard_map/ppermute | solution.py:171
  43.2 0.8 collective-permute-start.12
  44.0 1.7 %collective-permute-done.14.piece3_ref = bf16[2,16,1280]{2,1,0:T(8,128)(2,1)S(1)} collective-permute-done((bf16[2,16,1280]{2,1,0:T(8,128)(2,1)S(1)}, bf16[2,16,1280]{2,1,0:T(8,128)(2,1)S(1)}, u32[]{:S(2)}, u32[]{:S(2)}) %collective-permute-start.14) | collective-permute-done | bytes 81952 | tf_op jit(solution)/shard_map/ppermute | solution.py:171
  45.7 2.3 %collective-permute-done.13.piece2_ref = bf16[2,16,1280]{2,1,0:T(8,128)(2,1)S(1)} collective-permute-done((bf16[2,16,1280]{2,1,0:T(8,128)(2,1)S(1)}, bf16[2,16,1280]{2,1,0:T(8,128)(2,1)S(1)}, u32[]{:S(2)}, u32[]{:S(2)}) %collective-permute-start.13) | collective-permute-done | bytes 81952 | tf_op jit(solution)/shard_map/ppermute | solution.py:171
  48.0 2.8 %attend.1 = bf16[2,256,32]{2,1,0:T(8,128)(2,1)S(1)} custom-call(s32[3]{0:T(128)S(1)} %pad_add_fusion.at_ref, bf16[2,256,2240]{2,1,0:T(8,128)(2,1)S(1)} %bitcast.38, bf16[2,16,1280]{2,1,0:T(8,128)(2,1)S(1)} %maximum_select_fusion.piece0_ref, bf16[2,16,1280]{2,1,0:T(8,128)(2,1)S(1)} %collective-permute-done.12.piece1_ref, ...), custom_call_target="tpu_custom_call" | custom-call | flops 1174405120 | bytes 2293760 | tf_op jit(solution)/shard_map/attend/pallas_call | solution.py:147
  50.8 5.0 %collective-permute-start.15 = (bf16[2,3,16,32]{3,2,0,1:T(8,128)(2,1)S(1)}, bf16[2,3,16,32]{3,2,0,1:T(8,128)(2,1)S(1)}, u32[]{:S(2)}, u32[]{:S(2)}) collective-permute-start(bf16[2,3,16,32]{3,2,0,1:T(8,128)(2,1)S(1)} %copy.13), channel_id=1, source_target_pairs={{0,16},{16,32},{32,48},{48,64},{64,80},{80,96},{96,112},{112,128},... | collective-permute-start | bytes 18440 | tf_op jit(solution)/shard_map/ppermute | solution.py:214
  55.8 1.9 %collective-permute-start.16 = (bf16[2,3,16,32]{3,2,0,1:T(8,128)(2,1)S(1)}, bf16[2,3,16,32]{3,2,0,1:T(8,128)(2,1)S(1)}, u32[]{:S(2)}, u32[]{:S(2)}) collective-permute-start(bf16[2,3,16,32]{3,2,0,1:T(8,128)(2,1)S(1)} %copy.14), channel_id=1, source_target_pairs={{16,0},{32,16},{48,32},{64,48},{80,64},{96,80},{112,96},{128,112},... | collective-permute-start | bytes 18440 | tf_op jit(solution)/shard_map/ppermute | solution.py:215
  57.8 4.7 %collective-permute-done.16 = bf16[2,3,16,32]{3,2,0,1:T(8,128)(2,1)S(1)} collective-permute-done((bf16[2,3,16,32]{3,2,0,1:T(8,128)(2,1)S(1)}, bf16[2,3,16,32]{3,2,0,1:T(8,128)(2,1)S(1)}, u32[]{:S(2)}, u32[]{:S(2)}) %collective-permute-start.16) | collective-permute-done | bytes 6176 | tf_op jit(solution)/shard_map/ppermute | solution.py:215
  62.6 6.2 %collective-permute-start.17 = (bf16[2,22,3,32]{3,2,0,1:T(4,128)(2,1)S(1)}, bf16[2,22,3,32]{3,2,0,1:T(4,128)(2,1)S(1)}, u32[]{:S(2)}, u32[]{:S(2)}) collective-permute-start(bf16[2,22,3,32]{3,2,0,1:T(4,128)(2,1)S(1)} %get-tuple-element.42), channel_id=1, source_target_pairs={{0,1},{1,2},{2,3},{3,4},{4,5},{5,6},{6,7},{7,8},{8,9},{9,10},{10,1... | collective-permute-start | bytes 25352 | tf_op jit(solution)/shard_map/ppermute | solution.py:214
  68.8 1.9 %collective-permute-start.18 = (bf16[2,22,3,32]{3,2,0,1:T(4,128)(2,1)S(1)}, bf16[2,22,3,32]{3,2,0,1:T(4,128)(2,1)S(1)}, u32[]{:S(2)}, u32[]{:S(2)}) collective-permute-start(bf16[2,22,3,32]{3,2,0,1:T(4,128)(2,1)S(1)} %get-tuple-element.43), channel_id=1, source_target_pairs={{1,0},{2,1},{3,2},{4,3},{5,4},{6,5},{7,6},{8,7},{9,8},{10,9},{11,1... | collective-permute-start | bytes 25352 | tf_op jit(solution)/shard_map/ppermute | solution.py:215
  70.7 3.4 %collective-permute-done.18 = bf16[2,22,3,32]{3,2,0,1:T(4,128)(2,1)S(1)} collective-permute-done((bf16[2,22,3,32]{3,2,0,1:T(4,128)(2,1)S(1)}, bf16[2,22,3,32]{3,2,0,1:T(4,128)(2,1)S(1)}, u32[]{:S(2)}, u32[]{:S(2)}) %collective-permute-start.18) | collective-permute-done | bytes 8480 | tf_op jit(solution)/shard_map/ppermute | solution.py:215
  74.4 9.0 %decode.1 = bf16[2,16,2,32,512]{4,3,2,1,0:T(8,128)(2,1)} custom-call(s32[3]{0:T(128)S(1)} %pad_add_fusion.at_ref, f32[44,32,32]{2,1,0:T(8,128)S(1)} %bitcast.35, bf16[3,96,512]{2,1,0:T(8,128)(2,1)S(1)} %bitcast.39, f32[1,512]{1,0:T(1,128)S(1)} %bitcast.41, bf16[4608,512]{1,0:T(8,128)(2,1)S(1)} %keep.1.residual_ref, bf16[9,512,512]{2,1,0:T(8,128)(2,1)S(1)} %phases.1.upscale_ref), custom_call_target="tpu_custom_call" | custom-call | flops 8000000000 | bytes 12582912 | tf_op jit(solution)/shard_map/decode/pallas_call | solution.py:413
  (39 shorter events, 1.9 us)
Async XLA Ops:
  3.6 2.0 %collective-permute-start = (bf16[4,16,1280]{2,1,0:T(8,128)(2,1)}, bf16[4,16,1280]{2,1,0:T(8,128)(2,1)S(1)}, u32[]{:S(2)}, u32[]{:S(2)}) collective-permute-start(bf16[4,16,1280]{2,1,0:T(8,128)(2,1)} %get-tuple-element.26), channel_id=1, source_target_pairs={{0,1},{1,0},{2,3},{3,2},{4,5},{5,4},{6,7},{7,6},{8,9},{9,8},{10,11... | collective-permute-start | bytes 491528 | tf_op jit(solution)/shard_map/ppermute | solution.py:179
  6.6 4.0 %collective-permute-start.1 = (bf16[16,1280]{1,0:T(8,128)(2,1)S(1)}, bf16[16,1280]{1,0:T(8,128)(2,1)S(1)}, u32[]{:S(2)}, u32[]{:S(2)}) collective-permute-start(bf16[16,1280]{1,0:T(8,128)(2,1)S(1)} %get-tuple-element.39), channel_id=1, source_target_pairs={{0,16},{16,0},{32,48},{48,32},{64,80},{80,64},{96,112},{112,96},{1... | collective-permute-start | bytes 122888 | tf_op jit(solution)/shard_map/ppermute | solution.py:182
  7.2 4.4 %collective-permute-start.3 = (bf16[16,1280]{1,0:T(8,128)(2,1)S(1)}, bf16[16,1280]{1,0:T(8,128)(2,1)S(1)}, u32[]{:S(2)}, u32[]{:S(2)}) collective-permute-start(bf16[16,1280]{1,0:T(8,128)(2,1)S(1)} %get-tuple-element.40), channel_id=1, source_target_pairs={{0,32},{16,48},{32,0},{48,16},{64,96},{80,112},{96,64},{112,80},{1... | collective-permute-start | bytes 122888 | tf_op jit(solution)/shard_map/ppermute | solution.py:182
  8.1 4.1 %collective-permute-start.2 = (bf16[16,1280]{1,0:T(8,128)(2,1)S(1)}, bf16[16,1280]{1,0:T(8,128)(2,1)S(1)}, u32[]{:S(2)}, u32[]{:S(2)}) collective-permute-start(bf16[16,1280]{1,0:T(8,128)(2,1)S(1)} %get-tuple-element.41), channel_id=1, source_target_pairs={{0,48},{16,32},{32,16},{48,0},{64,112},{80,96},{96,80},{112,64},{1... | collective-permute-start | bytes 122888 | tf_op jit(solution)/shard_map/ppermute | solution.py:182
  12.2 7.3 %collective-permute-start.6 = (bf16[16,1280]{1,0:T(8,128)(2,1)S(1)}, bf16[16,1280]{1,0:T(8,128)(2,1)S(1)}, u32[]{:S(2)}, u32[]{:S(2)}) collective-permute-start(bf16[16,1280]{1,0:T(8,128)(2,1)S(1)} %fusion.8), channel_id=1, source_target_pairs={{0,128},{16,144},{32,160},{48,176},{64,192},{80,208},{96,224},{112... | collective-permute-start | bytes 122888 | tf_op jit(solution)/shard_map/ppermute | solution.py:171
  14.3 5.2 %collective-permute-start.5 = (bf16[16,1280]{1,0:T(8,128)(2,1)S(1)}, bf16[16,1280]{1,0:T(8,128)(2,1)S(1)}, u32[]{:S(2)}, u32[]{:S(2)}) collective-permute-start(bf16[16,1280]{1,0:T(8,128)(2,1)S(1)} %fusion.8), channel_id=1, source_target_pairs={{0,192},{16,208},{32,224},{48,240},{64,128},{80,144},{96,160},{112... | collective-permute-start | bytes 122888 | tf_op jit(solution)/shard_map/ppermute | solution.py:171
  15.3 4.1 %collective-permute-start.4 = (bf16[16,1280]{1,0:T(8,128)(2,1)S(1)}, bf16[16,1280]{1,0:T(8,128)(2,1)S(1)}, u32[]{:S(2)}, u32[]{:S(2)}) collective-permute-start(bf16[16,1280]{1,0:T(8,128)(2,1)S(1)} %fusion.8), channel_id=1, source_target_pairs={{0,64},{16,80},{32,96},{48,112},{64,0},{80,16},{96,32},{112,48},{1... | collective-permute-start | bytes 122888 | tf_op jit(solution)/shard_map/ppermute | solution.py:171
  16.1 2.3 %copy-start = (bf16[3,3,512,512]{3,2,1,0:T(8,128)(2,1)S(1)}, bf16[3,3,512,512]{3,2,1,0:T(8,128)(2,1)}, u32[]{:S(2)}) copy-start(bf16[3,3,512,512]{3,2,1,0:T(8,128)(2,1)} %param.14) | copy-start | bytes 14155780
  18.4 11.8 %copy-start.1 = (bf16[3,3,512,512]{3,2,1,0:T(8,128)(2,1)S(1)}, bf16[3,3,512,512]{3,2,1,0:T(8,128)(2,1)}, u32[]{:S(2)}) copy-start(bf16[3,3,512,512]{3,2,1,0:T(8,128)(2,1)} %param.15) | copy-start | bytes 14155780
  19.5 3.1 %collective-permute-start.7 = (bf16[16,1280]{1,0:T(8,128)(2,1)S(1)}, bf16[16,1280]{1,0:T(8,128)(2,1)S(1)}, u32[]{:S(2)}, u32[]{:S(2)}) collective-permute-start(bf16[16,1280]{1,0:T(8,128)(2,1)S(1)} %add_convert_fusion.2), channel_id=1, source_target_pairs={{0,2},{1,3},{2,0},{3,1},{4,6},{5,7},{6,4},{7,5},{8,10},{9,11},{10,... | collective-permute-start | bytes 122888 | tf_op jit(solution)/shard_map/ppermute | solution.py:171
  22.6 9.2 %collective-permute-start.10 = (bf16[16,1280]{1,0:T(8,128)(2,1)S(1)}, bf16[16,1280]{1,0:T(8,128)(2,1)S(1)}, u32[]{:S(2)}, u32[]{:S(2)}) collective-permute-start(bf16[16,1280]{1,0:T(8,128)(2,1)S(1)} %add_convert_fusion.1), channel_id=1, source_target_pairs={{0,10},{1,11},{2,8},{3,9},{4,14},{5,15},{6,12},{7,13},{8,2},{9,3},... | collective-permute-start | bytes 122888 | tf_op jit(solution)/shard_map/ppermute | solution.py:171
  29.0 5.1 %collective-permute-start.9 = (bf16[16,1280]{1,0:T(8,128)(2,1)S(1)}, bf16[16,1280]{1,0:T(8,128)(2,1)S(1)}, u32[]{:S(2)}, u32[]{:S(2)}) collective-permute-start(bf16[16,1280]{1,0:T(8,128)(2,1)S(1)} %add_convert_fusion.1), channel_id=1, source_target_pairs={{0,12},{1,13},{2,14},{3,15},{4,8},{5,9},{6,10},{7,11},{8,4},{9,5},... | collective-permute-start | bytes 122888 | tf_op jit(solution)/shard_map/ppermute | solution.py:171
  29.3 4.8 %collective-permute-start.8 = (bf16[16,1280]{1,0:T(8,128)(2,1)S(1)}, bf16[16,1280]{1,0:T(8,128)(2,1)S(1)}, u32[]{:S(2)}, u32[]{:S(2)}) collective-permute-start(bf16[16,1280]{1,0:T(8,128)(2,1)S(1)} %add_convert_fusion.1), channel_id=1, source_target_pairs={{0,4},{1,5},{2,6},{3,7},{4,0},{5,1},{6,2},{7,3},{8,12},{9,13},{10,... | collective-permute-start | bytes 122888 | tf_op jit(solution)/shard_map/ppermute | solution.py:171
  30.2 17.7 %copy-start.2 = (bf16[2,16,16,2240]{3,2,1,0:T(8,128)(2,1)S(1)}, bf16[2,16,16,2240]{3,2,1,0:T(8,128)(2,1)}, u32[]{:S(2)}) copy-start(bf16[2,16,16,2240]{3,2,1,0:T(8,128)(2,1)} %param.8) | copy-start | bytes 6881284
  30.2 17.7 %copy-start.4 = (bf16[2240,32]{0,1:T(8,128)(2,1)S(1)}, bf16[2240,32]{0,1:T(8,128)(2,1)}, u32[]{:S(2)}) copy-start(bf16[2240,32]{0,1:T(8,128)(2,1)} %param.11) | copy-start | bytes 430084
  31.8 42.5 %copy-start.3 = (bf16[3,3,32,512]{3,2,1,0:T(8,128)(2,1)S(1)}, bf16[3,3,32,512]{3,2,1,0:T(8,128)(2,1)}, u32[]{:S(2)}) copy-start(bf16[3,3,32,512]{3,2,1,0:T(8,128)(2,1)} %param.12) | copy-start | bytes 884740
  31.8 42.5 %copy-start.5 = (f32[512]{0:T(512)S(1)}, f32[512]{0:T(512)}, u32[]{:S(2)}) copy-start(f32[512]{0:T(512)} %param.13) | copy-start | bytes 6148
  34.1 6.5 %collective-permute-start.11 = (bf16[16,1280]{1,0:T(8,128)(2,1)S(1)}, bf16[16,1280]{1,0:T(8,128)(2,1)S(1)}, u32[]{:S(2)}, u32[]{:S(2)}) collective-permute-start(bf16[16,1280]{1,0:T(8,128)(2,1)S(1)} %add_convert_fusion), channel_id=1, source_target_pairs={{0,1},{1,0},{2,3},{3,2},{4,5},{5,4},{6,7},{7,6},{8,9},{9,8},{10,11... | collective-permute-start | bytes 122888 | tf_op jit(solution)/shard_map/ppermute | solution.py:201
  40.6 5.1 %collective-permute-start.14 = (bf16[2,16,1280]{2,1,0:T(8,128)(2,1)S(1)}, bf16[2,16,1280]{2,1,0:T(8,128)(2,1)S(1)}, u32[]{:S(2)}, u32[]{:S(2)}) collective-permute-start(bf16[2,16,1280]{2,1,0:T(8,128)(2,1)S(1)} %maximum_select_fusion.piece0_ref), channel_id=1, source_target_pairs={{0,48},{16,32},{32,16},{48,0},{64,112},{80,96},{96,80},{112,64},{1... | collective-permute-start | bytes 245768 | tf_op jit(solution)/shard_map/ppermute | solution.py:171
  43.2 4.8 %collective-permute-start.13 = (bf16[2,16,1280]{2,1,0:T(8,128)(2,1)S(1)}, bf16[2,16,1280]{2,1,0:T(8,128)(2,1)S(1)}, u32[]{:S(2)}, u32[]{:S(2)}) collective-permute-start(bf16[2,16,1280]{2,1,0:T(8,128)(2,1)S(1)} %maximum_select_fusion.piece0_ref), channel_id=1, source_target_pairs={{0,32},{16,48},{32,0},{48,16},{64,96},{80,112},{96,64},{112,80},{1... | collective-permute-start | bytes 245768 | tf_op jit(solution)/shard_map/ppermute | solution.py:171
  43.2 4.8 %collective-permute-start.12 = (bf16[2,16,1280]{2,1,0:T(8,128)(2,1)S(1)}, bf16[2,16,1280]{2,1,0:T(8,128)(2,1)S(1)}, u32[]{:S(2)}, u32[]{:S(2)}) collective-permute-start(bf16[2,16,1280]{2,1,0:T(8,128)(2,1)S(1)} %maximum_select_fusion.piece0_ref), channel_id=1, source_target_pairs={{0,16},{16,0},{32,48},{48,32},{64,80},{80,64},{96,112},{112,96},{1... | collective-permute-start | bytes 245768 | tf_op jit(solution)/shard_map/ppermute | solution.py:171
  50.8 7.0 %collective-permute-start.15 = (bf16[2,3,16,32]{3,2,0,1:T(8,128)(2,1)S(1)}, bf16[2,3,16,32]{3,2,0,1:T(8,128)(2,1)S(1)}, u32[]{:S(2)}, u32[]{:S(2)}) collective-permute-start(bf16[2,3,16,32]{3,2,0,1:T(8,128)(2,1)S(1)} %copy.13), channel_id=1, source_target_pairs={{0,16},{16,32},{32,48},{48,64},{64,80},{80,96},{96,112},{112,128},... | collective-permute-start | bytes 18440 | tf_op jit(solution)/shard_map/ppermute | solution.py:214
  55.8 6.7 %collective-permute-start.16 = (bf16[2,3,16,32]{3,2,0,1:T(8,128)(2,1)S(1)}, bf16[2,3,16,32]{3,2,0,1:T(8,128)(2,1)S(1)}, u32[]{:S(2)}, u32[]{:S(2)}) collective-permute-start(bf16[2,3,16,32]{3,2,0,1:T(8,128)(2,1)S(1)} %copy.14), channel_id=1, source_target_pairs={{16,0},{32,16},{48,32},{64,48},{80,64},{96,80},{112,96},{128,112},... | collective-permute-start | bytes 18440 | tf_op jit(solution)/shard_map/ppermute | solution.py:215
  62.6 8.2 %collective-permute-start.17 = (bf16[2,22,3,32]{3,2,0,1:T(4,128)(2,1)S(1)}, bf16[2,22,3,32]{3,2,0,1:T(4,128)(2,1)S(1)}, u32[]{:S(2)}, u32[]{:S(2)}) collective-permute-start(bf16[2,22,3,32]{3,2,0,1:T(4,128)(2,1)S(1)} %get-tuple-element.42), channel_id=1, source_target_pairs={{0,1},{1,2},{2,3},{3,4},{4,5},{5,6},{6,7},{7,8},{8,9},{9,10},{10,1... | collective-permute-start | bytes 25352 | tf_op jit(solution)/shard_map/ppermute | solution.py:214
  68.8 5.4 %collective-permute-start.18 = (bf16[2,22,3,32]{3,2,0,1:T(4,128)(2,1)S(1)}, bf16[2,22,3,32]{3,2,0,1:T(4,128)(2,1)S(1)}, u32[]{:S(2)}, u32[]{:S(2)}) collective-permute-start(bf16[2,22,3,32]{3,2,0,1:T(4,128)(2,1)S(1)} %get-tuple-element.43), channel_id=1, source_target_pairs={{1,0},{2,1},{3,2},{4,3},{5,4},{6,5},{7,6},{8,7},{9,8},{10,9},{11,1... | collective-permute-start | bytes 25352 | tf_op jit(solution)/shard_map/ppermute | solution.py:215

commit v3 on v2

--- a/solution.py
+++ b/solution.py
@@ -12,11 +12,13 @@
 LANES = 128
 PACK = 2560
 KS_AT = 2304
-
-
-def sums_kernel(scale, core_ref, k_hbm, v_hbm, mine_ref, other_ref, k_ref, v_ref, sems):
+WIDE = 3
+SPLIT = (1, 3, 2)
+
+
+def sums_kernel(scale, at_ref, k_hbm, v_hbm, mine_ref, other_ref, k_ref, v_ref, sems):
     images, tokens, width = k_ref.shape
-    core = core_ref[0]
+    core = at_ref[3]
     half = tokens // 2
     copies = []
     for n in range(images):
@@ -59,9 +61,9 @@
                 out_ref[2 * r + c] = total[16 * r : 16 * r + 16, wide * c : wide * (c + 1)]
 
 
-def image_sums(keys, values, core, scale):
+def image_sums(keys, values, at, scale):
     images, tokens, width = keys.shape
-    out = jax.ShapeDtypeStruct((4, 16, PACK // 2), jnp.bfloat16)
+    out = pltpu.VMEM((4, 16, PACK // 2), jnp.bfloat16)
     vmem = pl.BlockSpec(memory_space=pltpu.VMEM)
     hbm = pl.BlockSpec(memory_space=pl.ANY)
     return pl.pallas_call(
@@ -74,15 +76,52 @@
             pltpu.VMEM(values.shape, values.dtype),
             pltpu.SemaphoreType.DMA((images, 2, 2)),
         ],
-        compiler_params=pltpu.CompilerParams(vmem_limit_bytes=58 << 20),
+        compiler_params=pltpu.CompilerParams(vmem_limit_bytes=56 << 20),
         cost_estimate=pl.CostEstimate(flops=4 * tokens * width * 256, bytes_accessed=8 * tokens * width, transcendentals=0),
         name="image_sums",
-    )(core.reshape(1), keys, values)
-
-
-def attend_kernel(at_ref, q_ref, piece0_ref, piece1_ref, piece2_ref, piece3_ref, weight_ref, out_ref, sums):
+    )(at, keys, values)
+
+
+def sides_kernel(q_ref, left_ref, right_ref):
+    tokens = q_ref.shape[1]
+    edge = left_ref.shape[1]
+    side = 16
+    row = lax.broadcasted_iota(jnp.int32, (2 * edge, tokens), 0)
+    column = lax.broadcasted_iota(jnp.int32, (2 * edge, tokens), 1)
+    place = row % edge
+    wanted = side * (place // WIDE) + place % WIDE + (row // edge) * (side - WIDE)
+    pick = (column == wanted).astype(jnp.bfloat16)
+    picked = jnp.dot(pick, q_ref[0], preferred_element_type=jnp.float32).astype(jnp.bfloat16)
+    left_ref[0] = picked[:edge]
+    right_ref[0] = picked[edge:]
+
+
+def sides(queries):
+    images, tokens, width = queries.shape
+    edge = 16 * WIDE
+    out = jax.ShapeDtypeStruct((images, edge, width), queries.dtype)
+    block = pl.BlockSpec((1, edge, width), lambda i: (i, 0, 0))
+    return pl.pallas_call(
+        sides_kernel,
+        out_shape=[out, out],
+        grid=(images,),
+        in_specs=[pl.BlockSpec((1, tokens, width), lambda i: (i, 0, 0))],
+        out_specs=[block, block],
+        compiler_params=pltpu.CompilerParams(vmem_limit_bytes=48 << 20),
+        cost_estimate=pl.CostEstimate(flops=10**9, bytes_accessed=3 * images * tokens * width, transcendentals=0),
+        name="sides",
+    )(queries)
+
+
+def attend_kernel(
+    at_ref, q_ref, left_ref, right_ref, piece0_ref, piece1_ref, piece2_ref, piece3_ref, weight_ref,
+    out_ref, first_ref, last_ref, sums,
+):
     f32, bf16 = jnp.float32, jnp.bfloat16
-    images, tokens, width = q_ref.shape
+    images, inner, width = q_ref.shape
+    edge = left_ref.shape[1]
+    tokens = inner + 2 * edge
+    tile = 16
     group = 2 * LANES
     for n, piece in enumerate((piece0_ref, piece1_ref, piece2_ref, piece3_ref)):
         sums[at_ref[2] ^ n] = piece[...]
@@ -112,7 +151,9 @@
         for image in range(images):
             upper = kv[image][:, start : start + size]
             lower = means[HEAD * image : HEAD * (image + 1), start : start + size]
-            query = jnp.maximum(q_ref[image, :, start : start + size], 0)
+            lanes = slice(start, start + size)
+            query = [ref[image, :, lanes] for ref in (q_ref, left_ref, right_ref)]
+            query = jnp.maximum(jnp.concatenate(query, axis=0), 0)
             numerator = jnp.dot(
                 query, jnp.concatenate([upper] * repeat, axis=0) * here, preferred_element_type=f32
             )
@@ -137,23 +178,35 @@
     for image in range(images):
         total = jnp.sum(squares[image], axis=1, keepdims=True)
         normed = latent[tokens * image : tokens * (image + 1)] * lax.rsqrt(total / width + NORM_EPS)
-        out_ref[image] = normed.astype(bf16)
-
-
-def attend(at, queries, pieces, weight):
+        normed = normed.astype(bf16).astype(f32)
+        for y in range(tile):
+            line = images * y + image
+            at = inner + WIDE * y
+            out_ref[line, :WIDE] = normed[at : at + WIDE]
+            out_ref[line, WIDE : WIDE + tile] = normed[tile * y : tile * (y + 1)]
+            at += edge
+            out_ref[line, WIDE + tile : 2 * WIDE + tile] = normed[at : at + WIDE]
+    out_ref[:, 2 * WIDE + tile :] = jnp.zeros((images * tile, 10, weight_ref.shape[0]), f32)
+    first_ref[...] = out_ref[: images * WIDE]
+    last_ref[...] = out_ref[images * (tile - WIDE) :]
+
+
+def attend(at, queries, sides, pieces, weight):
     images, tokens, width = queries.shape
     channels = weight.shape[1]
     vmem = pl.BlockSpec(memory_space=pltpu.VMEM)
     return pl.pallas_call(
         attend_kernel,
-        out_shape=jax.ShapeDtypeStruct((images, tokens, channels), jnp.bfloat16),
-        in_specs=[pl.BlockSpec(memory_space=pltpu.SMEM)] + [vmem] * 6,
-        out_specs=vmem,
+        out_shape=[
+            jax.ShapeDtypeStruct((images * lines, 32, channels), jnp.float32) for lines in (16, WIDE, WIDE)
+        ],
+        in_specs=[pl.BlockSpec(memory_space=pltpu.SMEM)] + [vmem] * 8,
+        out_specs=[vmem] * 3,
         scratch_shapes=[pltpu.VMEM((4, images, 16, PACK // 2), jnp.bfloat16)],
         compiler_params=pltpu.CompilerParams(vmem_limit_bytes=32 << 20),
         cost_estimate=pl.CostEstimate(flops=2 * images * tokens * width * 512, bytes_accessed=2 * images * tokens * width, transcendentals=0),
         name="attend",
-    )(at, queries, *pieces, weight.T)
+    )(at, queries, *sides, *pieces, weight.T)
 
 
 def xor_pairs(distance):
@@ -171,23 +224,65 @@
     return [lax.ppermute(value, axis, xor_pairs(d)) for d in distances]
 
 
-def gather_all(mine, other, residual, upscale):
+def shifted(first, last, axis):
+    up = [(i, i + 1) for i in range(lax.axis_size(axis) - 1)]
+    down = [(j, i) for i, j in up]
+    return lax.ppermute(last, axis, up), lax.ppermute(first, axis, down)
+
+
+def split_kernel(at_ref, mine_ref, arrived_ref, own_ref, *parts_ref):
+    f32 = jnp.float32
+    for d, out_ref in zip((0,) + SPLIT, (own_ref,) + parts_ref):
+        chunk = at_ref[2] ^ d
+        total = mine_ref[chunk].astype(f32) + arrived_ref[chunk].astype(f32)
+        out_ref[...] = total.astype(out_ref.dtype)
+
+
+def split(at, mine, arrived):
+    shape = mine.shape[1:]
+    vmem = pl.BlockSpec(memory_space=pltpu.VMEM)
+    return pl.pallas_call(
+        split_kernel,
+        out_shape=[jax.ShapeDtypeStruct(shape, jnp.float32)]
+        + [jax.ShapeDtypeStruct(shape, jnp.bfloat16)] * len(SPLIT),
+        in_specs=[pl.BlockSpec(memory_space=pltpu.SMEM), vmem, vmem],
+        out_specs=[vmem] * (1 + len(SPLIT)),
+        compiler_params=pltpu.CompilerParams(vmem_limit_bytes=8 << 20),
+        name="split",
+    )(at, mine, arrived)
+
+
+def join_kernel(at_ref, mine_ref, twin_ref, out_ref):
+    core = at_ref[3]
+    out_ref[core] = mine_ref[...]
+    out_ref[1 - core] = twin_ref[...]
+
+
+def join(at, mine, twin):
+    vmem = pl.BlockSpec(memory_space=pltpu.VMEM)
+    return pl.pallas_call(
+        join_kernel,
+        out_shape=jax.ShapeDtypeStruct((2, *mine.shape), mine.dtype),
+        in_specs=[pl.BlockSpec(memory_space=pltpu.SMEM), vmem, vmem],
+        out_specs=vmem,
+        compiler_params=pltpu.CompilerParams(vmem_limit_bytes=8 << 20),
+        name="join",
+    )(at, mine, twin)
+
+
+def gather_all(at, mine, other, queries, residual, upscale):
     hold = lax.optimization_barrier
-    at_x = lax.axis_index("row") % 4
-    first = lax.axis_index("col") % 2 == 0
-    mine, other, first = hold((mine, other, first))
     arrived = lax.ppermute(other, "col", xor_pairs(1))
-    image = mine.astype(jnp.float32) + arrived.astype(jnp.float32)
-    parts = [
-        lax.ppermute(
-            lax.dynamic_index_in_dim(image, at_x ^ d, 0, False).astype(jnp.bfloat16), "row", xor_pairs(d)
-        )
-        for d in (1, 3, 2)
-    ]
-    chunk = added(lax.dynamic_index_in_dim(image, at_x, 0, False), parts)
-
-    chunk, weights = hold((chunk, residual))
+    near, mine = hold((queries, mine))
+    start, end = sides(near)
+    arrived, start, end = hold((arrived, start, end))
+    own, *parts = split(at, mine, arrived)
+    parts = [lax.ppermute(part, "row", xor_pairs(d)) for part, d in zip(parts, SPLIT)]
+    chunk = added(own, parts)
+
+    chunk, weights, start, end = hold((chunk, residual, start, end))
     arrived = sent(chunk, "row", (4, 12, 8))
+    beside = shifted(start, end, "col")
     arrived, kept = hold((arrived, keep(weights)))
     chunk = added(chunk, arrived)
 
@@ -199,22 +294,9 @@
     chunk = added(chunk, arrived)
 
     twin = lax.ppermute(chunk, "col", xor_pairs(1))
-    both = jnp.where(first, jnp.stack([chunk, twin]), jnp.stack([twin, chunk]))
+    both = join(at, chunk, twin)
     pieces = [both] + sent(both, "row", (1, 2, 3))
-    return pieces, kept, combined
-
-
-def extended(value, sides, width):
-    for axis, dim in sides:
-        devices, length = (lax.axis_size(axis), value.shape[dim])
-        up = [(i, (i + 1) % devices) for i in range(devices - 1)]
-        down = [(j, i) for i, j in up]
-        last = lax.slice_in_dim(value, length - width, length, axis=dim)
-        initial = lax.slice_in_dim(value, 0, width, axis=dim)
-        before = lax.ppermute(last, axis, up)
-        after = lax.ppermute(initial, axis, down)
-        value = jnp.concatenate([before, value, after], axis=dim)
-    return value
+    return pieces, beside, kept, combined
 
 
 def read(ref, at):
@@ -227,7 +309,7 @@
 
 
 def decode_kernel(
-    tiles, at_ref, lat_ref, entry_ref, gain_ref, residual_ref, upscale_ref, out_hbm,
+    tiles, at_ref, above_ref, lat_ref, below_ref, entry_ref, gain_ref, residual_ref, upscale_ref, out_hbm,
     wide, dec, hid, taps, ref, centre, slope, mix, out_ref, sems,
 ):
     tile = 16
@@ -241,7 +323,10 @@
         return (at >= 0) & (at < tile * tiles[axis])
 
     for i in range(2 * (tile + 6)):
-        block = [lat_ref[i, dx : dx + pitch, :] for dx in range(3)]
+        source, line = (above_ref, i) if i < 2 * WIDE else (lat_ref, i - 2 * WIDE)
+        if i >= 2 * (tile + WIDE):
+            source, line = below_ref, i - 2 * (tile + WIDE)
+        block = [source[line, dx : dx + pitch, :] for dx in range(3)]
         wide[pitch * i : pitch * (i + 1)] = jnp.concatenate(block, axis=1).astype(bf16)
 
     across = real(at_ref[1] * tile - 2 + spot, 1)
@@ -399,11 +484,10 @@
 
 
 def decode(at, latent, entry, gain, residual, combined, tiles):
-    images, tile = latent.shape[0], 16
+    images, tile = 2, 16
+    latents = latent[1].shape[-1]
     channels = entry.shape[-1]
     pitch = 24
-    padded = jnp.pad(latent, ((0, 0), (0, 0), (0, 10), (0, 0))).astype(jnp.float32)
-    padded = padded.transpose(1, 0, 2, 3).reshape(images * (tile + 6), 32, latent.shape[-1])
     rows = images * (tile + 4) + 8
     inner = images * (tile + 2)
     total = images * tile * tile
@@ -413,10 +497,10 @@
     out = pl.pallas_call(
         functools.partial(decode_kernel, tiles),
         out_shape=jax.ShapeDtypeStruct((images, tile, 2, 2 * tile, channels), bf16),
-        in_specs=[pl.BlockSpec(memory_space=pltpu.SMEM)] + [vmem] * 5,
+        in_specs=[pl.BlockSpec(memory_space=pltpu.SMEM)] + [vmem] * 7,
         out_specs=hbm,
         scratch_shapes=[
-            pltpu.VMEM((images * (tile + 6) * pitch, 3 * latent.shape[-1]), bf16),
+            pltpu.VMEM((images * (tile + 6) * pitch, 3 * latents), bf16),
             pltpu.VMEM((channels // LANES, rows * pitch, LANES), f32),
             pltpu.VMEM((channels // LANES, rows * pitch, LANES), f32),
             pltpu.VMEM((inner * tile + 80, 9 * channels), bf16),
@@ -432,7 +516,7 @@
         name="decode",
     )(
         at,
-        padded,
+        *latent,
         entry.reshape(3, 3 * entry.shape[2], channels),
         gain.reshape(1, channels),
         residual,
@@ -455,19 +539,20 @@
     scale = 1.0 / (tile * lax.axis_size("row") * tile * lax.axis_size("col"))
     flat = (images, tile * tile, width)
     keys, values = key_rows_per_head.reshape(flat), value_rows_per_head.reshape(flat)
-    core = (lax.axis_index("col") % 2).astype(jnp.int32)
-    mine, other = image_sums(keys, values, core, scale)
+    row, col = lax.axis_index("row"), lax.axis_index("col")
+    at = jnp.stack([row, col, row % 4, col % 2]).astype(jnp.int32)
+    mine, other = image_sums(keys, values, at, scale)
     channels = residual_conv_weight.shape[-1]
     residual = residual_conv_weight.reshape(9 * channels, channels)
-    pieces, residual, combined = gather_all(mine, other, residual, upscale_conv_weight)
-    row, col = lax.axis_index("row"), lax.axis_index("col")
-    at = jnp.stack([row, col, row % 4]).astype(jnp.int32)
-    latent = attend(at, queries.reshape(flat), pieces, latent_projection_weight)
-    latent = latent.reshape(images, tile, tile, latent.shape[-1])
-    widened = extended(latent, (("row", 1), ("col", 2)), 3)
+    queries = queries.reshape(flat)
+    pieces, beside, residual, combined = gather_all(
+        at, mine, other, queries, residual, upscale_conv_weight
+    )
+    latent, first, last = attend(at, queries, beside, pieces, latent_projection_weight)
+    above, below = shifted(first, last, "row")
     return decode(
         at,
-        widened,
+        (above, latent, below),
         entry_conv_weight,
         residual_norm_gain,
         residual,

time: 83.8 us -> 77.1 us (0.920)
  the two profiles are of different devices: /device:TPU:15 before, /device:TPU:22 now
where the time goes in v3:
time: 77.1 us; the launch traced here: 76.9 us
  starting transfers between devices  34.9 us (45%)
  Pallas kernels  21.1 us (27%)
  waiting for transfers between devices  19.8 us (26%)
    ppermute x10, starting transfers between devices, sent(): return [lax.ppermute(value, axis, xor_pairs(d)) for d in distances]  19.3 us
    ppermute x4, starting transfers between devices, shifted(): return (lax.ppermute(last, axis, up), lax.ppermute(first, axis, down))  9.25 us
    pallas_call x1, Pallas kernels, decode(): pl.pallas_call(functools.partial(decode_kernel, tiles), out_shape=jax.Sha...  9.14 us
    ppermute x10, waiting for transfers between devices, sent(): return [lax.ppermute(value, axis, xor_pairs(d)) for d in distances]  8.28 us
    ppermute x4, waiting for transfers between devices, shifted(): return (lax.ppermute(last, axis, up), lax.ppermute(first, axis, down))  6.7 us
    ppermute x3, starting transfers between devices, gather_all(): lax.ppermute(part, 'row', xor_pairs(d))  4.18 us
    pallas_call x1, Pallas kernels, image_sums(): pl.pallas_call(functools.partial(sums_kernel, scale), out_shape=[out, out...  3.95 us
    pallas_call x1, Pallas kernels, attend(): pl.pallas_call(attend_kernel, out_shape=[jax.ShapeDtypeStruct((images * l...  3.57 us
  transfers between devices with their start and end apart: 19, of which 11 were waited for; matrix products, arithmetic and copies ran while one was open for 0% of the time, Pallas kernels for 5%

profile of v3, /device:TPU:22, one launch (start us, length us, event | category | flops | bytes accessed | tf_op | source)
XLA Modules:
  0.0 76.9 jit_solution(12418060652144768274)
XLA Ops:
  0.6 3.9 %image_sums.1 = (bf16[4,16,1280]{2,1,0:T(8,128)(2,1)S(1)}, bf16[4,16,1280]{2,1,0:T(8,128)(2,1)S(1)}) custom-call(s32[4]{0:T(128)} %pad_add_fusion.at_ref, bf16[2,256,2240]{2,1,0:T(8,128)(2,1)} %bitcast.24, bf16[2,256,2240]{2,1,0:T(8,128)(2,1)} %bitcast.25), custom_call_target="tpu_custom_call" | custom-call | flops 587202560 | bytes 4587520 | tf_op jit(solution)/shard_map/image_sums/pallas_call | solution.py:69
  4.7 0.8 sides.1
  5.4 0.6 collective-permute-done.arrived_ref
  6.0 0.6 split.1
  6.6 0.9 %collective-permute-start.1 = (bf16[16,1280]{1,0:T(8,128)(2,1)S(1)}, bf16[16,1280]{1,0:T(8,128)(2,1)S(1)}, u32[]{:S(2)}, u32[]{:S(2)}) collective-permute-start(bf16[16,1280]{1,0:T(8,128)(2,1)S(1)} %get-tuple-element.43), channel_id=1, source_target_pairs={{0,16},{16,0},{32,48},{48,32},{64,80},{80,64},{96,112},{112,96},{1... | collective-permute-start | bytes 122888 | tf_op jit(solution)/shard_map/ppermute | solution.py:280
  7.5 1.1 %collective-permute-start.2 = (bf16[16,1280]{1,0:T(8,128)(2,1)S(1)}, bf16[16,1280]{1,0:T(8,128)(2,1)S(1)}, u32[]{:S(2)}, u32[]{:S(2)}) collective-permute-start(bf16[16,1280]{1,0:T(8,128)(2,1)S(1)} %get-tuple-element.44), channel_id=1, source_target_pairs={{0,48},{16,32},{32,16},{48,0},{64,112},{80,96},{96,80},{112,64},{1... | collective-permute-start | bytes 122888 | tf_op jit(solution)/shard_map/ppermute | solution.py:280
  8.7 2.1 %collective-permute-start.3 = (bf16[16,1280]{1,0:T(8,128)(2,1)S(1)}, bf16[16,1280]{1,0:T(8,128)(2,1)S(1)}, u32[]{:S(2)}, u32[]{:S(2)}) collective-permute-start(bf16[16,1280]{1,0:T(8,128)(2,1)S(1)} %get-tuple-element.45), channel_id=1, source_target_pairs={{0,32},{16,48},{32,0},{48,16},{64,96},{80,112},{96,64},{112,80},{1... | collective-permute-start | bytes 122888 | tf_op jit(solution)/shard_map/ppermute | solution.py:280
  10.8 2.4 %collective-permute-done.2 = bf16[16,1280]{1,0:T(8,128)(2,1)S(1)} collective-permute-done((bf16[16,1280]{1,0:T(8,128)(2,1)S(1)}, bf16[16,1280]{1,0:T(8,128)(2,1)S(1)}, u32[]{:S(2)}, u32[]{:S(2)}) %collective-permute-start.2) | collective-permute-done | bytes 40992 | tf_op jit(solution)/shard_map/ppermute | solution.py:280
  13.2 1.0 %collective-permute-done.3 = bf16[16,1280]{1,0:T(8,128)(2,1)S(1)} collective-permute-done((bf16[16,1280]{1,0:T(8,128)(2,1)S(1)}, bf16[16,1280]{1,0:T(8,128)(2,1)S(1)}, u32[]{:S(2)}, u32[]{:S(2)}) %collective-permute-start.3) | collective-permute-done | bytes 40992 | tf_op jit(solution)/shard_map/ppermute | solution.py:280
  14.2 0.8 collective-permute-start.8
  15.0 2.1 %collective-permute-start.7 = (bf16[16,1280]{1,0:T(8,128)(2,1)S(1)}, bf16[16,1280]{1,0:T(8,128)(2,1)S(1)}, u32[]{:S(2)}, u32[]{:S(2)}) collective-permute-start(bf16[16,1280]{1,0:T(8,128)(2,1)S(1)} %add_convert_fusion.3), channel_id=1, source_target_pairs={{0,192},{16,208},{32,224},{48,240},{64,128},{80,144},{96,160},{112... | collective-permute-start | bytes 122888 | tf_op jit(solution)/shard_map/ppermute | solution.py:224
  17.1 2.0 %collective-permute-start.6 = (bf16[16,1280]{1,0:T(8,128)(2,1)S(1)}, bf16[16,1280]{1,0:T(8,128)(2,1)S(1)}, u32[]{:S(2)}, u32[]{:S(2)}) collective-permute-start(bf16[16,1280]{1,0:T(8,128)(2,1)S(1)} %add_convert_fusion.3), channel_id=1, source_target_pairs={{0,64},{16,80},{32,96},{48,112},{64,0},{80,16},{96,32},{112,48},{1... | collective-permute-start | bytes 122888 | tf_op jit(solution)/shard_map/ppermute | solution.py:224
  19.0 1.0 %keep.1.residual_ref = bf16[4608,512]{1,0:T(8,128)(2,1)S(1)} custom-call(bf16[4608,512]{1,0:T(8,128)(2,1)S(1)} %bitcast.15), custom_call_target="tpu_custom_call" | custom-call | bytes 4718592 | tf_op jit(solution)/shard_map/keep/pallas_call | solution.py:437
  20.1 1.0 %collective-permute-done.6 = bf16[16,1280]{1,0:T(8,128)(2,1)S(1)} collective-permute-done((bf16[16,1280]{1,0:T(8,128)(2,1)S(1)}, bf16[16,1280]{1,0:T(8,128)(2,1)S(1)}, u32[]{:S(2)}, u32[]{:S(2)}) %collective-permute-start.6) | collective-permute-done | bytes 40992 | tf_op jit(solution)/shard_map/ppermute | solution.py:224
  21.1 2.0 %collective-permute-start.9 = (bf16[16,1280]{1,0:T(8,128)(2,1)S(1)}, bf16[16,1280]{1,0:T(8,128)(2,1)S(1)}, u32[]{:S(2)}, u32[]{:S(2)}) collective-permute-start(bf16[16,1280]{1,0:T(8,128)(2,1)S(1)} %add_convert_fusion.2), channel_id=1, source_target_pairs={{0,2},{1,3},{2,0},{3,1},{4,6},{5,7},{6,4},{7,5},{8,10},{9,11},{10,... | collective-permute-start | bytes 122888 | tf_op jit(solution)/shard_map/ppermute | solution.py:224
  23.1 2.1 %collective-permute-done.9 = bf16[16,1280]{1,0:T(8,128)(2,1)S(1)} collective-permute-done((bf16[16,1280]{1,0:T(8,128)(2,1)S(1)}, bf16[16,1280]{1,0:T(8,128)(2,1)S(1)}, u32[]{:S(2)}, u32[]{:S(2)}) %collective-permute-start.9) | collective-permute-done | bytes 40992 | tf_op jit(solution)/shard_map/ppermute | solution.py:224
  25.2 6.8 %collective-permute-start.12 = (bf16[16,1280]{1,0:T(8,128)(2,1)S(1)}, bf16[16,1280]{1,0:T(8,128)(2,1)S(1)}, u32[]{:S(2)}, u32[]{:S(2)}) collective-permute-start(bf16[16,1280]{1,0:T(8,128)(2,1)S(1)} %add_convert_fusion.1), channel_id=1, source_target_pairs={{0,10},{1,11},{2,8},{3,9},{4,14},{5,15},{6,12},{7,13},{8,2},{9,3},... | collective-permute-start | bytes 122888 | tf_op jit(solution)/shard_map/ppermute | solution.py:224
  32.6 0.9 %collective-permute-start.10 = (bf16[16,1280]{1,0:T(8,128)(2,1)S(1)}, bf16[16,1280]{1,0:T(8,128)(2,1)S(1)}, u32[]{:S(2)}, u32[]{:S(2)}) collective-permute-start(bf16[16,1280]{1,0:T(8,128)(2,1)S(1)} %add_convert_fusion.1), channel_id=1, source_target_pairs={{0,4},{1,5},{2,6},{3,7},{4,0},{5,1},{6,2},{7,3},{8,12},{9,13},{10,... | collective-permute-start | bytes 122888 | tf_op jit(solution)/shard_map/ppermute | solution.py:224
  33.5 1.3 %collective-permute-start.4 = (bf16[2,48,2240]{2,1,0:T(8,128)(2,1)S(1)}, bf16[2,48,2240]{2,1,0:T(8,128)(2,1)S(1)}, u32[]{:S(2)}, u32[]{:S(2)}) collective-permute-start(bf16[2,48,2240]{2,1,0:T(8,128)(2,1)S(1)} %get-tuple-element.48), channel_id=1, source_target_pairs={{0,1},{1,2},{2,3},{3,4},{4,5},{5,6},{6,7},{7,8},{8,9},{9,10},{10,1... | collective-permute-start | bytes 1290248 | tf_op jit(solution)/shard_map/ppermute | solution.py:230
  34.8 1.3 %collective-permute-start.5 = (bf16[2,48,2240]{2,1,0:T(8,128)(2,1)S(1)}, bf16[2,48,2240]{2,1,0:T(8,128)(2,1)S(1)}, u32[]{:S(2)}, u32[]{:S(2)}) collective-permute-start(bf16[2,48,2240]{2,1,0:T(8,128)(2,1)S(1)} %get-tuple-element.49), channel_id=1, source_target_pairs={{1,0},{2,1},{3,2},{4,3},{5,4},{6,5},{7,6},{8,7},{9,8},{10,9},{11,1... | collective-permute-start | bytes 1290248 | tf_op jit(solution)/shard_map/ppermute | solution.py:230
  36.2 1.6 %phases.1.upscale_ref = bf16[9,512,512]{2,1,0:T(8,128)(2,1)S(1)} custom-call(bf16[9,512,512]{2,1,0:T(8,128)(2,1)S(1)} %bitcast.18), custom_call_target="tpu_custom_call" | custom-call | flops 2621440 | bytes 4718592 | tf_op jit(solution)/shard_map/phases/pallas_call | solution.py:474
  38.2 2.1 %collective-permute-start.13 = (bf16[16,1280]{1,0:T(8,128)(2,1)S(1)}, bf16[16,1280]{1,0:T(8,128)(2,1)S(1)}, u32[]{:S(2)}, u32[]{:S(2)}) collective-permute-start(bf16[16,1280]{1,0:T(8,128)(2,1)S(1)} %add_convert_fusion.mine_ref), channel_id=1, source_target_pairs={{0,1},{1,0},{2,3},{3,2},{4,5},{5,4},{6,7},{7,6},{8,9},{9,8},{10,11... | collective-permute-start | bytes 122888 | tf_op jit(solution)/shard_map/ppermute | solution.py:296
  40.3 0.9 %collective-permute-done.13.twin_ref = bf16[16,1280]{1,0:T(8,128)(2,1)S(1)} collective-permute-done((bf16[16,1280]{1,0:T(8,128)(2,1)S(1)}, bf16[16,1280]{1,0:T(8,128)(2,1)S(1)}, u32[]{:S(2)}, u32[]{:S(2)}) %collective-permute-start.13) | collective-permute-done | bytes 40992 | tf_op jit(solution)/shard_map/ppermute | solution.py:296
  41.7 2.2 %collective-permute-start.16 = (bf16[2,16,1280]{2,1,0:T(8,128)(2,1)S(1)}, bf16[2,16,1280]{2,1,0:T(8,128)(2,1)S(1)}, u32[]{:S(2)}, u32[]{:S(2)}) collective-permute-start(bf16[2,16,1280]{2,1,0:T(8,128)(2,1)S(1)} %join.1.piece0_ref), channel_id=1, source_target_pairs={{0,48},{16,32},{32,16},{48,0},{64,112},{80,96},{96,80},{112,64},{1... | collective-permute-start | bytes 245768 | tf_op jit(solution)/shard_map/ppermute | solution.py:224
  44.0 1.9 %collective-permute-start.14 = (bf16[2,16,1280]{2,1,0:T(8,128)(2,1)S(1)}, bf16[2,16,1280]{2,1,0:T(8,128)(2,1)S(1)}, u32[]{:S(2)}, u32[]{:S(2)}) collective-permute-start(bf16[2,16,1280]{2,1,0:T(8,128)(2,1)S(1)} %join.1.piece0_ref), channel_id=1, source_target_pairs={{0,16},{16,0},{32,48},{48,32},{64,80},{80,64},{96,112},{112,96},{1... | collective-permute-start | bytes 245768 | tf_op jit(solution)/shard_map/ppermute | solution.py:224
  45.9 1.8 %collective-permute-done.16.piece3_ref = bf16[2,16,1280]{2,1,0:T(8,128)(2,1)S(1)} collective-permute-done((bf16[2,16,1280]{2,1,0:T(8,128)(2,1)S(1)}, bf16[2,16,1280]{2,1,0:T(8,128)(2,1)S(1)}, u32[]{:S(2)}, u32[]{:S(2)}) %collective-permute-start.16) | collective-permute-done | bytes 81952 | tf_op jit(solution)/shard_map/ppermute | solution.py:224
  47.7 3.0 %collective-permute-done.15.piece2_ref = bf16[2,16,1280]{2,1,0:T(8,128)(2,1)S(1)} collective-permute-done((bf16[2,16,1280]{2,1,0:T(8,128)(2,1)S(1)}, bf16[2,16,1280]{2,1,0:T(8,128)(2,1)S(1)}, u32[]{:S(2)}, u32[]{:S(2)}) %collective-permute-start.15) | collective-permute-done | bytes 81952 | tf_op jit(solution)/shard_map/ppermute | solution.py:224
  50.7 3.6 %attend.1 = (f32[32,32,32]{2,1,0:T(8,128)S(1)}, f32[6,32,32]{2,1,0:T(8,128)S(1)}, f32[6,32,32]{2,1,0:T(8,128)S(1)}) custom-call(s32[4]{0:T(128)S(1)} %copy-done, bf16[2,256,2240]{2,1,0:T(8,128)(2,1)S(1)} %bitcast.20, bf16[2,48,2240]{2,1,0:T(8,128)(2,1)S(1)} %collective-permute-done.4.left_ref, bf16[2,48,2240]{2,1,0:T(8,128)(2,1)S(1)} %collective-permute-done.5.right_ref, ...), custom_call_target="tpu_custom_call" | custom-call | flops 1174405120 | bytes 2293760 | tf_op jit(solution)/shard_map/attend/pallas_call | solution.py:198
  54.3 4.7 %collective-permute-start.17 = (f32[6,32,32]{2,1,0:T(8,128)S(1)}, f32[6,32,32]{2,1,0:T(8,128)S(1)}, u32[]{:S(2)}, u32[]{:S(2)}) collective-permute-start(f32[6,32,32]{2,1,0:T(8,128)S(1)} %get-tuple-element.60), channel_id=1, source_target_pairs={{0,16},{16,32},{32,48},{48,64},{64,80},{80,96},{96,112},{112,128},... | collective-permute-start | bytes 73736 | tf_op jit(solution)/shard_map/ppermute | solution.py:230
  59.0 1.9 %collective-permute-start.18 = (f32[6,32,32]{2,1,0:T(8,128)S(1)}, f32[6,32,32]{2,1,0:T(8,128)S(1)}, u32[]{:S(2)}, u32[]{:S(2)}) collective-permute-start(f32[6,32,32]{2,1,0:T(8,128)S(1)} %get-tuple-element.62), channel_id=1, source_target_pairs={{16,0},{32,16},{48,32},{64,48},{80,64},{96,80},{112,96},{128,112},... | collective-permute-start | bytes 73736 | tf_op jit(solution)/shard_map/ppermute | solution.py:230
  61.2 6.4 %collective-permute-done.18.below_ref = f32[6,32,32]{2,1,0:T(8,128)S(1)} collective-permute-done((f32[6,32,32]{2,1,0:T(8,128)S(1)}, f32[6,32,32]{2,1,0:T(8,128)S(1)}, u32[]{:S(2)}, u32[]{:S(2)}) %collective-permute-start.18) | collective-permute-done | bytes 24608 | tf_op jit(solution)/shard_map/ppermute | solution.py:230
  67.6 9.1 %decode.1 = bf16[2,16,2,32,512]{4,3,2,1,0:T(8,128)(2,1)} custom-call(s32[4]{0:T(128)S(1)} %copy-done, f32[6,32,32]{2,1,0:T(8,128)S(1)} %collective-permute-done.17.above_ref, f32[32,32,32]{2,1,0:T(8,128)S(1)} %get-tuple-element.61.lat_ref, f32[6,32,32]{2,1,0:T(8,128)S(1)} %collective-permute-done.18.below_ref, bf16[3,96,512]{2,1,0:T(8,128)(2,1)S(1)} %bitcast.21, ...), custom_call_target="tpu_custom_call" | custom-call | flops 8000000000 | bytes 12582912 | tf_op jit(solution)/shard_map/decode/pallas_call | solution.py:497
  (39 shorter events, 2.7 us)
Async XLA Ops:
  0.0 4.6 %copy-start.1 = (bf16[2,16,16,2240]{3,2,1,0:T(8,128)(2,1)S(1)}, bf16[2,16,16,2240]{3,2,1,0:T(8,128)(2,1)}, u32[]{:S(2)}) copy-start(bf16[2,16,16,2240]{3,2,1,0:T(8,128)(2,1)} %param.8) | copy-start | bytes 6881284
  0.0 19.0 %slice-start = ((s8[4718592]{0:T(1024)(128)(4,1)}), s8[524288]{0:T(1024)(128)(4,1)S(1)}, s32[]{:S(2)}) async-start(s8[4718592]{0:T(1024)(128)(4,1)} %bitcast.13), calls=%async_computation | async-start | bytes 1048576
  0.6 5.4 %copy-start = (s32[4]{0:T(128)S(1)}, s32[4]{0:T(128)}, u32[]{:S(2)}) copy-start(s32[4]{0:T(128)} %pad_add_fusion.at_ref) | copy-start | bytes 52
  0.6 18.4 %slice-start.1 = ((s8[4718592]{0:T(1024)(128)(4,1)}), s8[4194304]{0:T(1024)(128)(4,1)S(1)}, s32[]{:S(2)}) async-start(s8[4718592]{0:T(1024)(128)(4,1)} %bitcast.13), calls=%async_computation.1 | async-start | bytes 8388608
  4.5 1.5 %collective-permute-start = (bf16[4,16,1280]{2,1,0:T(8,128)(2,1)S(1)}, bf16[4,16,1280]{2,1,0:T(8,128)(2,1)S(1)}, u32[]{:S(2)}, u32[]{:S(2)}) collective-permute-start(bf16[4,16,1280]{2,1,0:T(8,128)(2,1)S(1)} %get-tuple-element.37), channel_id=1, source_target_pairs={{0,1},{1,0},{2,3},{3,2},{4,5},{5,4},{6,7},{7,6},{8,9},{9,8},{10,11... | collective-permute-start | bytes 491528 | tf_op jit(solution)/shard_map/ppermute | solution.py:275
  6.6 4.2 %collective-permute-start.1 = (bf16[16,1280]{1,0:T(8,128)(2,1)S(1)}, bf16[16,1280]{1,0:T(8,128)(2,1)S(1)}, u32[]{:S(2)}, u32[]{:S(2)}) collective-permute-start(bf16[16,1280]{1,0:T(8,128)(2,1)S(1)} %get-tuple-element.43), channel_id=1, source_target_pairs={{0,16},{16,0},{32,48},{48,32},{64,80},{80,64},{96,112},{112,96},{1... | collective-permute-start | bytes 122888 | tf_op jit(solution)/shard_map/ppermute | solution.py:280
  7.5 5.7 %collective-permute-start.2 = (bf16[16,1280]{1,0:T(8,128)(2,1)S(1)}, bf16[16,1280]{1,0:T(8,128)(2,1)S(1)}, u32[]{:S(2)}, u32[]{:S(2)}) collective-permute-start(bf16[16,1280]{1,0:T(8,128)(2,1)S(1)} %get-tuple-element.44), channel_id=1, source_target_pairs={{0,48},{16,32},{32,16},{48,0},{64,112},{80,96},{96,80},{112,64},{1... | collective-permute-start | bytes 122888 | tf_op jit(solution)/shard_map/ppermute | solution.py:280
  8.7 5.5 %collective-permute-start.3 = (bf16[16,1280]{1,0:T(8,128)(2,1)S(1)}, bf16[16,1280]{1,0:T(8,128)(2,1)S(1)}, u32[]{:S(2)}, u32[]{:S(2)}) collective-permute-start(bf16[16,1280]{1,0:T(8,128)(2,1)S(1)} %get-tuple-element.45), channel_id=1, source_target_pairs={{0,32},{16,48},{32,0},{48,16},{64,96},{80,112},{96,64},{112,80},{1... | collective-permute-start | bytes 122888 | tf_op jit(solution)/shard_map/ppermute | solution.py:280
  14.2 21.9 %slice-start.2 = ((s8[4718592]{0:T(1024)(128)(4,1)}), s8[4194304]{0:T(1024)(128)(4,1)S(1)}, s32[]{:S(2)}) async-start(s8[4718592]{0:T(1024)(128)(4,1)} %bitcast.16), calls=%async_computation.2 | async-start | bytes 8388608
  14.2 21.9 %slice-start.3 = ((s8[4718592]{0:T(1024)(128)(4,1)}), s8[524288]{0:T(1024)(128)(4,1)S(1)}, s32[]{:S(2)}) async-start(s8[4718592]{0:T(1024)(128)(4,1)} %bitcast.16), calls=%async_computation.3 | async-start | bytes 1048576
  14.2 5.8 %collective-permute-start.8 = (bf16[16,1280]{1,0:T(8,128)(2,1)S(1)}, bf16[16,1280]{1,0:T(8,128)(2,1)S(1)}, u32[]{:S(2)}, u32[]{:S(2)}) collective-permute-start(bf16[16,1280]{1,0:T(8,128)(2,1)S(1)} %add_convert_fusion.3), channel_id=1, source_target_pairs={{0,128},{16,144},{32,160},{48,176},{64,192},{80,208},{96,224},{112... | collective-permute-start | bytes 122888 | tf_op jit(solution)/shard_map/ppermute | solution.py:224
  15.0 5.0 %collective-permute-start.7 = (bf16[16,1280]{1,0:T(8,128)(2,1)S(1)}, bf16[16,1280]{1,0:T(8,128)(2,1)S(1)}, u32[]{:S(2)}, u32[]{:S(2)}) collective-permute-start(bf16[16,1280]{1,0:T(8,128)(2,1)S(1)} %add_convert_fusion.3), channel_id=1, source_target_pairs={{0,192},{16,208},{32,224},{48,240},{64,128},{80,144},{96,160},{112... | collective-permute-start | bytes 122888 | tf_op jit(solution)/shard_map/ppermute | solution.py:224
  17.1 4.0 %collective-permute-start.6 = (bf16[16,1280]{1,0:T(8,128)(2,1)S(1)}, bf16[16,1280]{1,0:T(8,128)(2,1)S(1)}, u32[]{:S(2)}, u32[]{:S(2)}) collective-permute-start(bf16[16,1280]{1,0:T(8,128)(2,1)S(1)} %add_convert_fusion.3), channel_id=1, source_target_pairs={{0,64},{16,80},{32,96},{48,112},{64,0},{80,16},{96,32},{112,48},{1... | collective-permute-start | bytes 122888 | tf_op jit(solution)/shard_map/ppermute | solution.py:224
  21.1 4.1 %collective-permute-start.9 = (bf16[16,1280]{1,0:T(8,128)(2,1)S(1)}, bf16[16,1280]{1,0:T(8,128)(2,1)S(1)}, u32[]{:S(2)}, u32[]{:S(2)}) collective-permute-start(bf16[16,1280]{1,0:T(8,128)(2,1)S(1)} %add_convert_fusion.2), channel_id=1, source_target_pairs={{0,2},{1,3},{2,0},{3,1},{4,6},{5,7},{6,4},{7,5},{8,10},{9,11},{10,... | collective-permute-start | bytes 122888 | tf_op jit(solution)/shard_map/ppermute | solution.py:224
  25.2 12.6 %collective-permute-start.12 = (bf16[16,1280]{1,0:T(8,128)(2,1)S(1)}, bf16[16,1280]{1,0:T(8,128)(2,1)S(1)}, u32[]{:S(2)}, u32[]{:S(2)}) collective-permute-start(bf16[16,1280]{1,0:T(8,128)(2,1)S(1)} %add_convert_fusion.1), channel_id=1, source_target_pairs={{0,10},{1,11},{2,8},{3,9},{4,14},{5,15},{6,12},{7,13},{8,2},{9,3},... | collective-permute-start | bytes 122888 | tf_op jit(solution)/shard_map/ppermute | solution.py:224
  32.0 6.1 %collective-permute-start.11 = (bf16[16,1280]{1,0:T(8,128)(2,1)S(1)}, bf16[16,1280]{1,0:T(8,128)(2,1)S(1)}, u32[]{:S(2)}, u32[]{:S(2)}) collective-permute-start(bf16[16,1280]{1,0:T(8,128)(2,1)S(1)} %add_convert_fusion.1), channel_id=1, source_target_pairs={{0,12},{1,13},{2,14},{3,15},{4,8},{5,9},{6,10},{7,11},{8,4},{9,5},... | collective-permute-start | bytes 122888 | tf_op jit(solution)/shard_map/ppermute | solution.py:224
  32.6 5.6 %collective-permute-start.10 = (bf16[16,1280]{1,0:T(8,128)(2,1)S(1)}, bf16[16,1280]{1,0:T(8,128)(2,1)S(1)}, u32[]{:S(2)}, u32[]{:S(2)}) collective-permute-start(bf16[16,1280]{1,0:T(8,128)(2,1)S(1)} %add_convert_fusion.1), channel_id=1, source_target_pairs={{0,4},{1,5},{2,6},{3,7},{4,0},{5,1},{6,2},{7,3},{8,12},{9,13},{10,... | collective-permute-start | bytes 122888 | tf_op jit(solution)/shard_map/ppermute | solution.py:224
  33.5 17.2 %collective-permute-start.4 = (bf16[2,48,2240]{2,1,0:T(8,128)(2,1)S(1)}, bf16[2,48,2240]{2,1,0:T(8,128)(2,1)S(1)}, u32[]{:S(2)}, u32[]{:S(2)}) collective-permute-start(bf16[2,48,2240]{2,1,0:T(8,128)(2,1)S(1)} %get-tuple-element.48), channel_id=1, source_target_pairs={{0,1},{1,2},{2,3},{3,4},{4,5},{5,6},{6,7},{7,8},{8,9},{9,10},{10,1... | collective-permute-start | bytes 1290248 | tf_op jit(solution)/shard_map/ppermute | solution.py:230
  34.8 15.9 %collective-permute-start.5 = (bf16[2,48,2240]{2,1,0:T(8,128)(2,1)S(1)}, bf16[2,48,2240]{2,1,0:T(8,128)(2,1)S(1)}, u32[]{:S(2)}, u32[]{:S(2)}) collective-permute-start(bf16[2,48,2240]{2,1,0:T(8,128)(2,1)S(1)} %get-tuple-element.49), channel_id=1, source_target_pairs={{1,0},{2,1},{3,2},{4,3},{5,4},{6,5},{7,6},{8,7},{9,8},{10,9},{11,1... | collective-permute-start | bytes 1290248 | tf_op jit(solution)/shard_map/ppermute | solution.py:230
  36.2 14.5 %copy-start.3 = (bf16[2240,32]{0,1:T(8,128)(2,1)S(1)}, bf16[2240,32]{0,1:T(8,128)(2,1)}, u32[]{:S(2)}) copy-start(bf16[2240,32]{0,1:T(8,128)(2,1)} %param.11) | copy-start | bytes 430084
  37.7 29.9 %copy-start.2 = (bf16[3,3,32,512]{3,2,1,0:T(8,128)(2,1)S(1)}, bf16[3,3,32,512]{3,2,1,0:T(8,128)(2,1)}, u32[]{:S(2)}) copy-start(bf16[3,3,32,512]{3,2,1,0:T(8,128)(2,1)} %param.12) | copy-start | bytes 884740
  37.8 29.9 %copy-start.4 = (f32[512]{0:T(512)S(1)}, f32[512]{0:T(512)}, u32[]{:S(2)}) copy-start(f32[512]{0:T(512)} %param.13) | copy-start | bytes 6148
  38.2 3.0 %collective-permute-start.13 = (bf16[16,1280]{1,0:T(8,128)(2,1)S(1)}, bf16[16,1280]{1,0:T(8,128)(2,1)S(1)}, u32[]{:S(2)}, u32[]{:S(2)}) collective-permute-start(bf16[16,1280]{1,0:T(8,128)(2,1)S(1)} %add_convert_fusion.mine_ref), channel_id=1, source_target_pairs={{0,1},{1,0},{2,3},{3,2},{4,5},{5,4},{6,7},{7,6},{8,9},{9,8},{10,11... | collective-permute-start | bytes 122888 | tf_op jit(solution)/shard_map/ppermute | solution.py:296
  41.7 6.0 %collective-permute-start.16 = (bf16[2,16,1280]{2,1,0:T(8,128)(2,1)S(1)}, bf16[2,16,1280]{2,1,0:T(8,128)(2,1)S(1)}, u32[]{:S(2)}, u32[]{:S(2)}) collective-permute-start(bf16[2,16,1280]{2,1,0:T(8,128)(2,1)S(1)} %join.1.piece0_ref), channel_id=1, source_target_pairs={{0,48},{16,32},{32,16},{48,0},{64,112},{80,96},{96,80},{112,64},{1... | collective-permute-start | bytes 245768 | tf_op jit(solution)/shard_map/ppermute | solution.py:224
  43.9 6.8 %collective-permute-start.15 = (bf16[2,16,1280]{2,1,0:T(8,128)(2,1)S(1)}, bf16[2,16,1280]{2,1,0:T(8,128)(2,1)S(1)}, u32[]{:S(2)}, u32[]{:S(2)}) collective-permute-start(bf16[2,16,1280]{2,1,0:T(8,128)(2,1)S(1)} %join.1.piece0_ref), channel_id=1, source_target_pairs={{0,32},{16,48},{32,0},{48,16},{64,96},{80,112},{96,64},{112,80},{1... | collective-permute-start | bytes 245768 | tf_op jit(solution)/shard_map/ppermute | solution.py:224
  44.0 6.7 %collective-permute-start.14 = (bf16[2,16,1280]{2,1,0:T(8,128)(2,1)S(1)}, bf16[2,16,1280]{2,1,0:T(8,128)(2,1)S(1)}, u32[]{:S(2)}, u32[]{:S(2)}) collective-permute-start(bf16[2,16,1280]{2,1,0:T(8,128)(2,1)S(1)} %join.1.piece0_ref), channel_id=1, source_target_pairs={{0,16},{16,0},{32,48},{48,32},{64,80},{80,64},{96,112},{112,96},{1... | collective-permute-start | bytes 245768 | tf_op jit(solution)/shard_map/ppermute | solution.py:224
  54.3 6.9 %collective-permute-start.17 = (f32[6,32,32]{2,1,0:T(8,128)S(1)}, f32[6,32,32]{2,1,0:T(8,128)S(1)}, u32[]{:S(2)}, u32[]{:S(2)}) collective-permute-start(f32[6,32,32]{2,1,0:T(8,128)S(1)} %get-tuple-element.60), channel_id=1, source_target_pairs={{0,16},{16,32},{32,48},{48,64},{64,80},{80,96},{96,112},{112,128},... | collective-permute-start | bytes 73736 | tf_op jit(solution)/shard_map/ppermute | solution.py:230
  59.0 8.6 %collective-permute-start.18 = (f32[6,32,32]{2,1,0:T(8,128)S(1)}, f32[6,32,32]{2,1,0:T(8,128)S(1)}, u32[]{:S(2)}, u32[]{:S(2)}) collective-permute-start(f32[6,32,32]{2,1,0:T(8,128)S(1)} %get-tuple-element.62), channel_id=1, source_target_pairs={{16,0},{32,16},{48,32},{64,48},{80,64},{96,80},{112,96},{128,112},... | collective-permute-start | bytes 73736 | tf_op jit(solution)/shard_map/ppermute | solution.py:230

commit v4 on v3

--- a/solution.py
+++ b/solution.py
@@ -82,9 +82,10 @@
     )(at, keys, values)
 
 
-def sides_kernel(q_ref, left_ref, right_ref):
+def sides_kernel(at_ref, q_ref, near_ref, far_ref):
     tokens = q_ref.shape[1]
-    edge = left_ref.shape[1]
+    edge = near_ref.shape[1]
+    odd = at_ref[3] == 1
     side = 16
     row = lax.broadcasted_iota(jnp.int32, (2 * edge, tokens), 0)
     column = lax.broadcasted_iota(jnp.int32, (2 * edge, tokens), 1)
@@ -92,11 +93,11 @@
     wanted = side * (place // WIDE) + place % WIDE + (row // edge) * (side - WIDE)
     pick = (column == wanted).astype(jnp.bfloat16)
     picked = jnp.dot(pick, q_ref[0], preferred_element_type=jnp.float32).astype(jnp.bfloat16)
-    left_ref[0] = picked[:edge]
-    right_ref[0] = picked[edge:]
-
-
-def sides(queries):
+    near_ref[0] = jnp.where(odd, picked[:edge], picked[edge:])
+    far_ref[0] = jnp.where(odd, picked[edge:], picked[:edge])
+
+
+def sides(at, queries):
     images, tokens, width = queries.shape
     edge = 16 * WIDE
     out = jax.ShapeDtypeStruct((images, edge, width), queries.dtype)
@@ -105,26 +106,32 @@
         sides_kernel,
         out_shape=[out, out],
         grid=(images,),
-        in_specs=[pl.BlockSpec((1, tokens, width), lambda i: (i, 0, 0))],
+        in_specs=[
+            pl.BlockSpec(memory_space=pltpu.SMEM),
+            pl.BlockSpec((1, tokens, width), lambda i: (i, 0, 0)),
+        ],
         out_specs=[block, block],
         compiler_params=pltpu.CompilerParams(vmem_limit_bytes=48 << 20),
         cost_estimate=pl.CostEstimate(flops=10**9, bytes_accessed=3 * images * tokens * width, transcendentals=0),
         name="sides",
-    )(queries)
+    )(at, queries)
 
 
 def attend_kernel(
-    at_ref, q_ref, left_ref, right_ref, piece0_ref, piece1_ref, piece2_ref, piece3_ref, weight_ref,
-    out_ref, first_ref, last_ref, sums,
+    at_ref, q_ref, near_ref, far_ref, *rest,
 ):
+    pieces, (weight_ref, out_ref, near_out_ref, far_out_ref, sums) = rest[:8], rest[8:]
     f32, bf16 = jnp.float32, jnp.bfloat16
     images, inner, width = q_ref.shape
-    edge = left_ref.shape[1]
+    edge = near_ref.shape[1]
+    odd = at_ref[3] == 1
+    odd_row = at_ref[4] == 1
     tokens = inner + 2 * edge
     tile = 16
     group = 2 * LANES
-    for n, piece in enumerate((piece0_ref, piece1_ref, piece2_ref, piece3_ref)):
-        sums[at_ref[2] ^ n] = piece[...]
+    for n in range(4):
+        sums[at_ref[2] ^ n, at_ref[3]] = pieces[n][...]
+        sums[at_ref[2] ^ n, 1 - at_ref[3]] = pieces[4 + n][...]
     same = (
         lax.broadcasted_iota(jnp.int32, (group, group), 0) // HEAD
         == lax.broadcasted_iota(jnp.int32, (group, group), 1) // HEAD
@@ -152,7 +159,8 @@
             upper = kv[image][:, start : start + size]
             lower = means[HEAD * image : HEAD * (image + 1), start : start + size]
             lanes = slice(start, start + size)
-            query = [ref[image, :, lanes] for ref in (q_ref, left_ref, right_ref)]
+            near, far = near_ref[image, :, lanes], far_ref[image, :, lanes]
+            query = [q_ref[image, :, lanes], jnp.where(odd, near, far), jnp.where(odd, far, near)]
             query = jnp.maximum(jnp.concatenate(query, axis=0), 0)
             numerator = jnp.dot(
                 query, jnp.concatenate([upper] * repeat, axis=0) * here, preferred_element_type=f32
@@ -187,8 +195,10 @@
             at += edge
             out_ref[line, WIDE + tile : 2 * WIDE + tile] = normed[at : at + WIDE]
     out_ref[:, 2 * WIDE + tile :] = jnp.zeros((images * tile, 10, weight_ref.shape[0]), f32)
-    first_ref[...] = out_ref[: images * WIDE]
-    last_ref[...] = out_ref[images * (tile - WIDE) :]
+    first = out_ref[: images * WIDE]
+    last = out_ref[images * (tile - WIDE) :]
+    near_out_ref[...] = jnp.where(odd_row, first, last)
+    far_out_ref[...] = jnp.where(odd_row, last, first)
 
 
 def attend(at, queries, sides, pieces, weight):
@@ -200,7 +210,7 @@
         out_shape=[
             jax.ShapeDtypeStruct((images * lines, 32, channels), jnp.float32) for lines in (16, WIDE, WIDE)
         ],
-        in_specs=[pl.BlockSpec(memory_space=pltpu.SMEM)] + [vmem] * 8,
+        in_specs=[pl.BlockSpec(memory_space=pltpu.SMEM)] + [vmem] * 12,
         out_specs=[vmem] * 3,
         scratch_shapes=[pltpu.VMEM((4, images, 16, PACK // 2), jnp.bfloat16)],
         compiler_params=pltpu.CompilerParams(vmem_limit_bytes=32 << 20),
@@ -224,10 +234,11 @@
     return [lax.ppermute(value, axis, xor_pairs(d)) for d in distances]
 
 
-def shifted(first, last, axis):
-    up = [(i, i + 1) for i in range(lax.axis_size(axis) - 1)]
-    down = [(j, i) for i, j in up]
-    return lax.ppermute(last, axis, up), lax.ppermute(first, axis, down)
+def swapped(even, odd, axis):
+    size = lax.axis_size(axis)
+    near = [(i, i ^ 1) for i in range(size)]
+    far = [(i, i - 1 if i % 2 == 0 else i + 1) for i in range(1, size - 1)]
+    return lax.ppermute(even, axis, near), lax.ppermute(odd, axis, far)
 
 
 def split_kernel(at_ref, mine_ref, arrived_ref, own_ref, *parts_ref):
@@ -252,29 +263,11 @@
     )(at, mine, arrived)
 
 
-def join_kernel(at_ref, mine_ref, twin_ref, out_ref):
-    core = at_ref[3]
-    out_ref[core] = mine_ref[...]
-    out_ref[1 - core] = twin_ref[...]
-
-
-def join(at, mine, twin):
-    vmem = pl.BlockSpec(memory_space=pltpu.VMEM)
-    return pl.pallas_call(
-        join_kernel,
-        out_shape=jax.ShapeDtypeStruct((2, *mine.shape), mine.dtype),
-        in_specs=[pl.BlockSpec(memory_space=pltpu.SMEM), vmem, vmem],
-        out_specs=vmem,
-        compiler_params=pltpu.CompilerParams(vmem_limit_bytes=8 << 20),
-        name="join",
-    )(at, mine, twin)
-
-
 def gather_all(at, mine, other, queries, residual, upscale):
     hold = lax.optimization_barrier
     arrived = lax.ppermute(other, "col", xor_pairs(1))
     near, mine = hold((queries, mine))
-    start, end = sides(near)
+    start, end = sides(at, near)
     arrived, start, end = hold((arrived, start, end))
     own, *parts = split(at, mine, arrived)
     parts = [lax.ppermute(part, "row", xor_pairs(d)) for part, d in zip(parts, SPLIT)]
@@ -282,7 +275,7 @@
 
     chunk, weights, start, end = hold((chunk, residual, start, end))
     arrived = sent(chunk, "row", (4, 12, 8))
-    beside = shifted(start, end, "col")
+    beside = swapped(start, end, "col")
     arrived, kept = hold((arrived, keep(weights)))
     chunk = added(chunk, arrived)
 
@@ -293,9 +286,8 @@
     arrived, combined = hold((arrived, phases(weights)))
     chunk = added(chunk, arrived)
 
-    twin = lax.ppermute(chunk, "col", xor_pairs(1))
-    both = join(at, chunk, twin)
-    pieces = [both] + sent(both, "row", (1, 2, 3))
+    pieces = [chunk] + sent(chunk, "row", (1, 2, 3))
+    pieces += [lax.ppermute(piece, "col", xor_pairs(1)) for piece in pieces]
     return pieces, beside, kept, combined
 
 
@@ -309,7 +301,7 @@
 
 
 def decode_kernel(
-    tiles, at_ref, above_ref, lat_ref, below_ref, entry_ref, gain_ref, residual_ref, upscale_ref, out_hbm,
+    tiles, at_ref, lat_ref, near_ref, far_ref, entry_ref, gain_ref, residual_ref, upscale_ref, out_hbm,
     wide, dec, hid, taps, ref, centre, slope, mix, out_ref, sems,
 ):
     tile = 16
@@ -317,16 +309,21 @@
     pitch = 24
     f32, bf16 = jnp.float32, jnp.bfloat16
     rows = tile + 4
+    odd = at_ref[4] == 1
     spot = lax.broadcasted_iota(jnp.int32, (2 * pitch, 1), 0) % pitch
 
     def real(at, axis):
         return (at >= 0) & (at < tile * tiles[axis])
 
     for i in range(2 * (tile + 6)):
-        source, line = (above_ref, i) if i < 2 * WIDE else (lat_ref, i - 2 * WIDE)
-        if i >= 2 * (tile + WIDE):
-            source, line = below_ref, i - 2 * (tile + WIDE)
-        block = [source[line, dx : dx + pitch, :] for dx in range(3)]
+        if i < 2 * WIDE:
+            line = jnp.where(odd, near_ref[i], far_ref[i])
+        elif i < 2 * (tile + WIDE):
+            line = lat_ref[i - 2 * WIDE]
+        else:
+            line = i - 2 * (tile + WIDE)
+            line = jnp.where(odd, far_ref[line], near_ref[line])
+        block = [line[dx : dx + pitch] for dx in range(3)]
         wide[pitch * i : pitch * (i + 1)] = jnp.concatenate(block, axis=1).astype(bf16)
 
     across = real(at_ref[1] * tile - 2 + spot, 1)
@@ -485,7 +482,7 @@
 
 def decode(at, latent, entry, gain, residual, combined, tiles):
     images, tile = 2, 16
-    latents = latent[1].shape[-1]
+    latents = latent[0].shape[-1]
     channels = entry.shape[-1]
     pitch = 24
     rows = images * (tile + 4) + 8
@@ -540,7 +537,7 @@
     flat = (images, tile * tile, width)
     keys, values = key_rows_per_head.reshape(flat), value_rows_per_head.reshape(flat)
     row, col = lax.axis_index("row"), lax.axis_index("col")
-    at = jnp.stack([row, col, row % 4, col % 2]).astype(jnp.int32)
+    at = jnp.stack([row, col, row % 4, col % 2, row % 2]).astype(jnp.int32)
     mine, other = image_sums(keys, values, at, scale)
     channels = residual_conv_weight.shape[-1]
     residual = residual_conv_weight.reshape(9 * channels, channels)
@@ -548,11 +545,11 @@
     pieces, beside, residual, combined = gather_all(
         at, mine, other, queries, residual, upscale_conv_weight
     )
-    latent, first, last = attend(at, queries, beside, pieces, latent_projection_weight)
-    above, below = shifted(first, last, "row")
+    latent, near, far = attend(at, queries, beside, pieces, latent_projection_weight)
+    near, far = swapped(near, far, "row")
     return decode(
         at,
-        (above, latent, below),
+        (latent, near, far),
         entry_conv_weight,
         residual_norm_gain,
         residual,

time: 77.1 us -> 71.8 us (0.931)
  the two profiles are of different devices: /device:TPU:22 before, /device:TPU:24 now
where the time goes in v4:
time: 71.8 us; the launch traced here: 71.7 us
  starting transfers between devices  27.6 us (38%)
  waiting for transfers between devices  21.9 us (31%)
  Pallas kernels  21.1 us (29%)
    ppermute x10, starting transfers between devices, sent(): return [lax.ppermute(value, axis, xor_pairs(d)) for d in distances]  18.1 us
    ppermute x10, waiting for transfers between devices, sent(): return [lax.ppermute(value, axis, xor_pairs(d)) for d in distances]  10 us
    pallas_call x1, Pallas kernels, decode(): pl.pallas_call(functools.partial(decode_kernel, tiles), out_shape=jax.Sha...  9.15 us
    ppermute x4, waiting for transfers between devices, swapped(): return (lax.ppermute(even, axis, near), lax.ppermute(odd, axis, far))  6.06 us
    ppermute x3, waiting for transfers between devices, gather_all(): lax.ppermute(part, 'row', xor_pairs(d))  4.87 us
    ppermute x4, starting transfers between devices, swapped(): return (lax.ppermute(even, axis, near), lax.ppermute(odd, axis, far))  4.54 us
    ppermute x3, starting transfers between devices, gather_all(): lax.ppermute(part, 'row', xor_pairs(d))  4.31 us
    pallas_call x1, Pallas kernels, image_sums(): pl.pallas_call(functools.partial(sums_kernel, scale), out_shape=[out, out...  3.96 us
  transfers between devices with their start and end apart: 22, of which 14 were waited for; matrix products, arithmetic and copies ran while one was open for 0% of the time, Pallas kernels for 5%

profile of v4, /device:TPU:24, one launch (start us, length us, event | category | flops | bytes accessed | tf_op | source)
XLA Modules:
  0.0 71.7 jit_solution(10817322088494436306)
XLA Ops:
  0.6 4.0 %image_sums.1 = (bf16[4,16,1280]{2,1,0:T(8,128)(2,1)S(1)}, bf16[4,16,1280]{2,1,0:T(8,128)(2,1)S(1)}) custom-call(s32[5]{0:T(128)} %stack.23.at_ref, bf16[2,256,2240]{2,1,0:T(8,128)(2,1)} %bitcast.25, bf16[2,256,2240]{2,1,0:T(8,128)(2,1)} %bitcast.26), custom_call_target="tpu_custom_call" | custom-call | flops 587202560 | bytes 4587520 | tf_op jit(solution)/shard_map/image_sums/pallas_call | solution.py:69
  4.7 1.3 %sides.1 = (bf16[2,48,2240]{2,1,0:T(8,128)(2,1)S(1)}, bf16[2,48,2240]{2,1,0:T(8,128)(2,1)S(1)}) custom-call(s32[5]{0:T(128)S(1)} %copy-done, bf16[2,256,2240]{2,1,0:T(8,128)(2,1)S(1)} %bitcast.20), custom_call_target="tpu_custom_call" | custom-call | flops 1000000000 | bytes 3440640 | tf_op jit(solution)/shard_map/sides/pallas_call | solution.py:105
  6.7 1.6 %collective-permute-start.1 = (bf16[16,1280]{1,0:T(8,128)(2,1)S(1)}, bf16[16,1280]{1,0:T(8,128)(2,1)S(1)}, u32[]{:S(2)}, u32[]{:S(2)}) collective-permute-start(bf16[16,1280]{1,0:T(8,128)(2,1)S(1)} %get-tuple-element.43), channel_id=1, source_target_pairs={{0,16},{16,0},{32,48},{48,32},{64,80},{80,64},{96,112},{112,96},{1... | collective-permute-start | bytes 122888 | tf_op jit(solution)/shard_map/ppermute | solution.py:273
  8.2 2.1 %collective-permute-start.2 = (bf16[16,1280]{1,0:T(8,128)(2,1)S(1)}, bf16[16,1280]{1,0:T(8,128)(2,1)S(1)}, u32[]{:S(2)}, u32[]{:S(2)}) collective-permute-start(bf16[16,1280]{1,0:T(8,128)(2,1)S(1)} %get-tuple-element.44), channel_id=1, source_target_pairs={{0,48},{16,32},{32,16},{48,0},{64,112},{80,96},{96,80},{112,64},{1... | collective-permute-start | bytes 122888 | tf_op jit(solution)/shard_map/ppermute | solution.py:273
  10.3 0.6 collective-permute-start.3
  11.0 2.5 %collective-permute-done.2 = bf16[16,1280]{1,0:T(8,128)(2,1)S(1)} collective-permute-done((bf16[16,1280]{1,0:T(8,128)(2,1)S(1)}, bf16[16,1280]{1,0:T(8,128)(2,1)S(1)}, u32[]{:S(2)}, u32[]{:S(2)}) %collective-permute-start.2) | collective-permute-done | bytes 40992 | tf_op jit(solution)/shard_map/ppermute | solution.py:273
  13.4 2.4 %collective-permute-done.3 = bf16[16,1280]{1,0:T(8,128)(2,1)S(1)} collective-permute-done((bf16[16,1280]{1,0:T(8,128)(2,1)S(1)}, bf16[16,1280]{1,0:T(8,128)(2,1)S(1)}, u32[]{:S(2)}, u32[]{:S(2)}) %collective-permute-start.3) | collective-permute-done | bytes 40992 | tf_op jit(solution)/shard_map/ppermute | solution.py:273
  15.9 1.3 %collective-permute-start.8 = (bf16[16,1280]{1,0:T(8,128)(2,1)S(1)}, bf16[16,1280]{1,0:T(8,128)(2,1)S(1)}, u32[]{:S(2)}, u32[]{:S(2)}) collective-permute-start(bf16[16,1280]{1,0:T(8,128)(2,1)S(1)} %add_convert_fusion.3), channel_id=1, source_target_pairs={{0,128},{16,144},{32,160},{48,176},{64,192},{80,208},{96,224},{112... | collective-permute-start | bytes 122888 | tf_op jit(solution)/shard_map/ppermute | solution.py:234
  17.2 2.2 %collective-permute-start.7 = (bf16[16,1280]{1,0:T(8,128)(2,1)S(1)}, bf16[16,1280]{1,0:T(8,128)(2,1)S(1)}, u32[]{:S(2)}, u32[]{:S(2)}) collective-permute-start(bf16[16,1280]{1,0:T(8,128)(2,1)S(1)} %add_convert_fusion.3), channel_id=1, source_target_pairs={{0,192},{16,208},{32,224},{48,240},{64,128},{80,144},{96,160},{112... | collective-permute-start | bytes 122888 | tf_op jit(solution)/shard_map/ppermute | solution.py:234
  19.5 1.0 %keep.1.residual_ref = bf16[4608,512]{1,0:T(8,128)(2,1)S(1)} custom-call(bf16[4608,512]{1,0:T(8,128)(2,1)S(1)} %bitcast.16), custom_call_target="tpu_custom_call" | custom-call | bytes 4718592 | tf_op jit(solution)/shard_map/keep/pallas_call | solution.py:434
  20.5 1.0 %collective-permute-done.8 = bf16[16,1280]{1,0:T(8,128)(2,1)S(1)} collective-permute-done((bf16[16,1280]{1,0:T(8,128)(2,1)S(1)}, bf16[16,1280]{1,0:T(8,128)(2,1)S(1)}, u32[]{:S(2)}, u32[]{:S(2)}) %collective-permute-start.8) | collective-permute-done | bytes 40992 | tf_op jit(solution)/shard_map/ppermute | solution.py:234
  21.5 0.9 %collective-permute-done.7 = bf16[16,1280]{1,0:T(8,128)(2,1)S(1)} collective-permute-done((bf16[16,1280]{1,0:T(8,128)(2,1)S(1)}, bf16[16,1280]{1,0:T(8,128)(2,1)S(1)}, u32[]{:S(2)}, u32[]{:S(2)}) %collective-permute-start.7) | collective-permute-done | bytes 40992 | tf_op jit(solution)/shard_map/ppermute | solution.py:234
  22.4 1.0 %collective-permute-done.6 = bf16[16,1280]{1,0:T(8,128)(2,1)S(1)} collective-permute-done((bf16[16,1280]{1,0:T(8,128)(2,1)S(1)}, bf16[16,1280]{1,0:T(8,128)(2,1)S(1)}, u32[]{:S(2)}, u32[]{:S(2)}) %collective-permute-start.6) | collective-permute-done | bytes 40992 | tf_op jit(solution)/shard_map/ppermute | solution.py:234
  23.4 2.0 %collective-permute-start.9 = (bf16[16,1280]{1,0:T(8,128)(2,1)S(1)}, bf16[16,1280]{1,0:T(8,128)(2,1)S(1)}, u32[]{:S(2)}, u32[]{:S(2)}) collective-permute-start(bf16[16,1280]{1,0:T(8,128)(2,1)S(1)} %add_convert_fusion.2), channel_id=1, source_target_pairs={{0,2},{1,3},{2,0},{3,1},{4,6},{5,7},{6,4},{7,5},{8,10},{9,11},{10,... | collective-permute-start | bytes 122888 | tf_op jit(solution)/shard_map/ppermute | solution.py:234
  25.4 2.1 %collective-permute-done.9 = bf16[16,1280]{1,0:T(8,128)(2,1)S(1)} collective-permute-done((bf16[16,1280]{1,0:T(8,128)(2,1)S(1)}, bf16[16,1280]{1,0:T(8,128)(2,1)S(1)}, u32[]{:S(2)}, u32[]{:S(2)}) %collective-permute-start.9) | collective-permute-done | bytes 40992 | tf_op jit(solution)/shard_map/ppermute | solution.py:234
  27.5 6.8 %collective-permute-start.12 = (bf16[16,1280]{1,0:T(8,128)(2,1)S(1)}, bf16[16,1280]{1,0:T(8,128)(2,1)S(1)}, u32[]{:S(2)}, u32[]{:S(2)}) collective-permute-start(bf16[16,1280]{1,0:T(8,128)(2,1)S(1)} %add_convert_fusion.1), channel_id=1, source_target_pairs={{0,10},{1,11},{2,8},{3,9},{4,14},{5,15},{6,12},{7,13},{8,2},{9,3},... | collective-permute-start | bytes 122888 | tf_op jit(solution)/shard_map/ppermute | solution.py:234
  34.9 0.9 %collective-permute-start.10 = (bf16[16,1280]{1,0:T(8,128)(2,1)S(1)}, bf16[16,1280]{1,0:T(8,128)(2,1)S(1)}, u32[]{:S(2)}, u32[]{:S(2)}) collective-permute-start(bf16[16,1280]{1,0:T(8,128)(2,1)S(1)} %add_convert_fusion.1), channel_id=1, source_target_pairs={{0,4},{1,5},{2,6},{3,7},{4,0},{5,1},{6,2},{7,3},{8,12},{9,13},{10,... | collective-permute-start | bytes 122888 | tf_op jit(solution)/shard_map/ppermute | solution.py:234
  35.8 0.7 collective-permute-start.5
  36.6 1.6 %phases.1.upscale_ref = bf16[9,512,512]{2,1,0:T(8,128)(2,1)S(1)} custom-call(bf16[9,512,512]{2,1,0:T(8,128)(2,1)S(1)} %bitcast.19), custom_call_target="tpu_custom_call" | custom-call | flops 2621440 | bytes 4718592 | tf_op jit(solution)/shard_map/phases/pallas_call | solution.py:471
  38.2 2.4 %collective-permute-done.11 = bf16[16,1280]{1,0:T(8,128)(2,1)S(1)} collective-permute-done((bf16[16,1280]{1,0:T(8,128)(2,1)S(1)}, bf16[16,1280]{1,0:T(8,128)(2,1)S(1)}, u32[]{:S(2)}, u32[]{:S(2)}) %collective-permute-start.11) | collective-permute-done | bytes 40992 | tf_op jit(solution)/shard_map/ppermute | solution.py:234
  40.7 1.2 %collective-permute-start.15 = (bf16[16,1280]{1,0:T(8,128)(2,1)S(1)}, bf16[16,1280]{1,0:T(8,128)(2,1)S(1)}, u32[]{:S(2)}, u32[]{:S(2)}) collective-permute-start(bf16[16,1280]{1,0:T(8,128)(2,1)S(1)} %add_convert_fusion.rest_0_), channel_id=1, source_target_pairs={{0,48},{16,32},{32,16},{48,0},{64,112},{80,96},{96,80},{112,64},{1... | collective-permute-start | bytes 122888 | tf_op jit(solution)/shard_map/ppermute | solution.py:234
  41.9 1.5 %collective-permute-start.14 = (bf16[16,1280]{1,0:T(8,128)(2,1)S(1)}, bf16[16,1280]{1,0:T(8,128)(2,1)S(1)}, u32[]{:S(2)}, u32[]{:S(2)}) collective-permute-start(bf16[16,1280]{1,0:T(8,128)(2,1)S(1)} %add_convert_fusion.rest_0_), channel_id=1, source_target_pairs={{0,32},{16,48},{32,0},{48,16},{64,96},{80,112},{96,64},{112,80},{1... | collective-permute-start | bytes 122888 | tf_op jit(solution)/shard_map/ppermute | solution.py:234
  43.5 1.4 %collective-permute-start.13 = (bf16[16,1280]{1,0:T(8,128)(2,1)S(1)}, bf16[16,1280]{1,0:T(8,128)(2,1)S(1)}, u32[]{:S(2)}, u32[]{:S(2)}) collective-permute-start(bf16[16,1280]{1,0:T(8,128)(2,1)S(1)} %add_convert_fusion.rest_0_), channel_id=1, source_target_pairs={{0,16},{16,0},{32,48},{48,32},{64,80},{80,64},{96,112},{112,96},{1... | collective-permute-start | bytes 122888 | tf_op jit(solution)/shard_map/ppermute | solution.py:234
  44.9 1.1 %collective-permute-done.15.rest_3_ = bf16[16,1280]{1,0:T(8,128)(2,1)S(1)} collective-permute-done((bf16[16,1280]{1,0:T(8,128)(2,1)S(1)}, bf16[16,1280]{1,0:T(8,128)(2,1)S(1)}, u32[]{:S(2)}, u32[]{:S(2)}) %collective-permute-start.15) | collective-permute-done | bytes 40992 | tf_op jit(solution)/shard_map/ppermute | solution.py:234
  46.0 1.5 %collective-permute-done.14.rest_2_ = bf16[16,1280]{1,0:T(8,128)(2,1)S(1)} collective-permute-done((bf16[16,1280]{1,0:T(8,128)(2,1)S(1)}, bf16[16,1280]{1,0:T(8,128)(2,1)S(1)}, u32[]{:S(2)}, u32[]{:S(2)}) %collective-permute-start.14) | collective-permute-done | bytes 40992 | tf_op jit(solution)/shard_map/ppermute | solution.py:234
  48.0 0.7 collective-permute-done.18.rest_6_
  48.9 3.5 %attend.1 = (f32[32,32,32]{2,1,0:T(8,128)S(1)}, f32[6,32,32]{2,1,0:T(8,128)S(1)}, f32[6,32,32]{2,1,0:T(8,128)S(1)}) custom-call(s32[5]{0:T(128)S(1)} %copy-done, bf16[2,256,2240]{2,1,0:T(8,128)(2,1)S(1)} %bitcast.21, bf16[2,48,2240]{2,1,0:T(8,128)(2,1)S(1)} %collective-permute-done.4.near_ref, bf16[2,48,2240]{2,1,0:T(8,128)(2,1)S(1)} %collective-permute-done.5.far_ref, ...), custom_call_target="tpu_custom_call" | custom-call | flops 1174405120 | bytes 2293760 | tf_op jit(solution)/shard_map/attend/pallas_call | solution.py:208
  52.4 1.3 %collective-permute-start.20 = (f32[6,32,32]{2,1,0:T(8,128)S(1)}, f32[6,32,32]{2,1,0:T(8,128)S(1)}, u32[]{:S(2)}, u32[]{:S(2)}) collective-permute-start(f32[6,32,32]{2,1,0:T(8,128)S(1)} %get-tuple-element.61), channel_id=1, source_target_pairs={{0,16},{16,0},{32,48},{48,32},{64,80},{80,64},{96,112},{112,96},{1... | collective-permute-start | bytes 73736 | tf_op jit(solution)/shard_map/ppermute | solution.py:241
  53.8 2.5 %collective-permute-start.21 = (f32[6,32,32]{2,1,0:T(8,128)S(1)}, f32[6,32,32]{2,1,0:T(8,128)S(1)}, u32[]{:S(2)}, u32[]{:S(2)}) collective-permute-start(f32[6,32,32]{2,1,0:T(8,128)S(1)} %get-tuple-element.62), channel_id=1, source_target_pairs={{16,32},{32,16},{48,64},{64,48},{80,96},{96,80},{112,128},{128,112... | collective-permute-start | bytes 73736 | tf_op jit(solution)/shard_map/ppermute | solution.py:241
  56.3 1.3 %collective-permute-done.20.near_ref = f32[6,32,32]{2,1,0:T(8,128)S(1)} collective-permute-done((f32[6,32,32]{2,1,0:T(8,128)S(1)}, f32[6,32,32]{2,1,0:T(8,128)S(1)}, u32[]{:S(2)}, u32[]{:S(2)}) %collective-permute-start.20) | collective-permute-done | bytes 24608 | tf_op jit(solution)/shard_map/ppermute | solution.py:241
  57.6 4.8 %collective-permute-done.21.far_ref = f32[6,32,32]{2,1,0:T(8,128)S(1)} collective-permute-done((f32[6,32,32]{2,1,0:T(8,128)S(1)}, f32[6,32,32]{2,1,0:T(8,128)S(1)}, u32[]{:S(2)}, u32[]{:S(2)}) %collective-permute-start.21) | collective-permute-done | bytes 24608 | tf_op jit(solution)/shard_map/ppermute | solution.py:241
  62.4 9.1 %decode.1 = bf16[2,16,2,32,512]{4,3,2,1,0:T(8,128)(2,1)} custom-call(s32[5]{0:T(128)S(1)} %copy-done, f32[32,32,32]{2,1,0:T(8,128)S(1)} %get-tuple-element.60.lat_ref, f32[6,32,32]{2,1,0:T(8,128)S(1)} %collective-permute-done.20.near_ref, f32[6,32,32]{2,1,0:T(8,128)S(1)} %collective-permute-done.21.far_ref, bf16[3,96,512]{2,1,0:T(8,128)(2,1)S(1)} %bitcast.22, ...), custom_call_target="tpu_custom_call" | custom-call | flops 8000000000 | bytes 12582912 | tf_op jit(solution)/shard_map/decode/pallas_call | solution.py:494
  (44 shorter events, 2.9 us)
Async XLA Ops:
  0.0 4.7 %copy-start.1 = (bf16[2,16,16,2240]{3,2,1,0:T(8,128)(2,1)S(1)}, bf16[2,16,16,2240]{3,2,1,0:T(8,128)(2,1)}, u32[]{:S(2)}) copy-start(bf16[2,16,16,2240]{3,2,1,0:T(8,128)(2,1)} %param.8) | copy-start | bytes 6881284
  0.0 19.5 %slice-start = ((s8[4718592]{0:T(1024)(128)(4,1)}), s8[524288]{0:T(1024)(128)(4,1)S(1)}, s32[]{:S(2)}) async-start(s8[4718592]{0:T(1024)(128)(4,1)} %bitcast.14), calls=%async_computation | async-start | bytes 1048576
  0.6 4.1 %copy-start = (s32[5]{0:T(128)S(1)}, s32[5]{0:T(128)}, u32[]{:S(2)}) copy-start(s32[5]{0:T(128)} %stack.23.at_ref) | copy-start | bytes 64
  0.6 18.9 %slice-start.1 = ((s8[4718592]{0:T(1024)(128)(4,1)}), s8[4194304]{0:T(1024)(128)(4,1)S(1)}, s32[]{:S(2)}) async-start(s8[4718592]{0:T(1024)(128)(4,1)} %bitcast.14), calls=%async_computation.1 | async-start | bytes 8388608
  4.6 1.5 %collective-permute-start = (bf16[4,16,1280]{2,1,0:T(8,128)(2,1)S(1)}, bf16[4,16,1280]{2,1,0:T(8,128)(2,1)S(1)}, u32[]{:S(2)}, u32[]{:S(2)}) collective-permute-start(bf16[4,16,1280]{2,1,0:T(8,128)(2,1)S(1)} %get-tuple-element.37), channel_id=1, source_target_pairs={{0,1},{1,0},{2,3},{3,2},{4,5},{5,4},{6,7},{7,6},{8,9},{9,8},{10,11... | collective-permute-start | bytes 491528 | tf_op jit(solution)/shard_map/ppermute | solution.py:268
  6.7 4.3 %collective-permute-start.1 = (bf16[16,1280]{1,0:T(8,128)(2,1)S(1)}, bf16[16,1280]{1,0:T(8,128)(2,1)S(1)}, u32[]{:S(2)}, u32[]{:S(2)}) collective-permute-start(bf16[16,1280]{1,0:T(8,128)(2,1)S(1)} %get-tuple-element.43), channel_id=1, source_target_pairs={{0,16},{16,0},{32,48},{48,32},{64,80},{80,64},{96,112},{112,96},{1... | collective-permute-start | bytes 122888 | tf_op jit(solution)/shard_map/ppermute | solution.py:273
  8.2 5.2 %collective-permute-start.2 = (bf16[16,1280]{1,0:T(8,128)(2,1)S(1)}, bf16[16,1280]{1,0:T(8,128)(2,1)S(1)}, u32[]{:S(2)}, u32[]{:S(2)}) collective-permute-start(bf16[16,1280]{1,0:T(8,128)(2,1)S(1)} %get-tuple-element.44), channel_id=1, source_target_pairs={{0,48},{16,32},{32,16},{48,0},{64,112},{80,96},{96,80},{112,64},{1... | collective-permute-start | bytes 122888 | tf_op jit(solution)/shard_map/ppermute | solution.py:273
  10.3 5.5 %collective-permute-start.3 = (bf16[16,1280]{1,0:T(8,128)(2,1)S(1)}, bf16[16,1280]{1,0:T(8,128)(2,1)S(1)}, u32[]{:S(2)}, u32[]{:S(2)}) collective-permute-start(bf16[16,1280]{1,0:T(8,128)(2,1)S(1)} %get-tuple-element.45), channel_id=1, source_target_pairs={{0,32},{16,48},{32,0},{48,16},{64,96},{80,112},{96,64},{112,80},{1... | collective-permute-start | bytes 122888 | tf_op jit(solution)/shard_map/ppermute | solution.py:273
  15.9 20.7 %slice-start.2 = ((s8[4718592]{0:T(1024)(128)(4,1)}), s8[4194304]{0:T(1024)(128)(4,1)S(1)}, s32[]{:S(2)}) async-start(s8[4718592]{0:T(1024)(128)(4,1)} %bitcast.17), calls=%async_computation.2 | async-start | bytes 8388608
  15.9 20.7 %slice-start.3 = ((s8[4718592]{0:T(1024)(128)(4,1)}), s8[524288]{0:T(1024)(128)(4,1)S(1)}, s32[]{:S(2)}) async-start(s8[4718592]{0:T(1024)(128)(4,1)} %bitcast.17), calls=%async_computation.3 | async-start | bytes 1048576
  15.9 5.6 %collective-permute-start.8 = (bf16[16,1280]{1,0:T(8,128)(2,1)S(1)}, bf16[16,1280]{1,0:T(8,128)(2,1)S(1)}, u32[]{:S(2)}, u32[]{:S(2)}) collective-permute-start(bf16[16,1280]{1,0:T(8,128)(2,1)S(1)} %add_convert_fusion.3), channel_id=1, source_target_pairs={{0,128},{16,144},{32,160},{48,176},{64,192},{80,208},{96,224},{112... | collective-permute-start | bytes 122888 | tf_op jit(solution)/shard_map/ppermute | solution.py:234
  17.2 5.2 %collective-permute-start.7 = (bf16[16,1280]{1,0:T(8,128)(2,1)S(1)}, bf16[16,1280]{1,0:T(8,128)(2,1)S(1)}, u32[]{:S(2)}, u32[]{:S(2)}) collective-permute-start(bf16[16,1280]{1,0:T(8,128)(2,1)S(1)} %add_convert_fusion.3), channel_id=1, source_target_pairs={{0,192},{16,208},{32,224},{48,240},{64,128},{80,144},{96,160},{112... | collective-permute-start | bytes 122888 | tf_op jit(solution)/shard_map/ppermute | solution.py:234
  19.4 4.0 %collective-permute-start.6 = (bf16[16,1280]{1,0:T(8,128)(2,1)S(1)}, bf16[16,1280]{1,0:T(8,128)(2,1)S(1)}, u32[]{:S(2)}, u32[]{:S(2)}) collective-permute-start(bf16[16,1280]{1,0:T(8,128)(2,1)S(1)} %add_convert_fusion.3), channel_id=1, source_target_pairs={{0,64},{16,80},{32,96},{48,112},{64,0},{80,16},{96,32},{112,48},{1... | collective-permute-start | bytes 122888 | tf_op jit(solution)/shard_map/ppermute | solution.py:234
  23.4 4.1 %collective-permute-start.9 = (bf16[16,1280]{1,0:T(8,128)(2,1)S(1)}, bf16[16,1280]{1,0:T(8,128)(2,1)S(1)}, u32[]{:S(2)}, u32[]{:S(2)}) collective-permute-start(bf16[16,1280]{1,0:T(8,128)(2,1)S(1)} %add_convert_fusion.2), channel_id=1, source_target_pairs={{0,2},{1,3},{2,0},{3,1},{4,6},{5,7},{6,4},{7,5},{8,10},{9,11},{10,... | collective-permute-start | bytes 122888 | tf_op jit(solution)/shard_map/ppermute | solution.py:234
  27.5 10.6 %collective-permute-start.12 = (bf16[16,1280]{1,0:T(8,128)(2,1)S(1)}, bf16[16,1280]{1,0:T(8,128)(2,1)S(1)}, u32[]{:S(2)}, u32[]{:S(2)}) collective-permute-start(bf16[16,1280]{1,0:T(8,128)(2,1)S(1)} %add_convert_fusion.1), channel_id=1, source_target_pairs={{0,10},{1,11},{2,8},{3,9},{4,14},{5,15},{6,12},{7,13},{8,2},{9,3},... | collective-permute-start | bytes 122888 | tf_op jit(solution)/shard_map/ppermute | solution.py:234
  34.4 6.2 %collective-permute-start.11 = (bf16[16,1280]{1,0:T(8,128)(2,1)S(1)}, bf16[16,1280]{1,0:T(8,128)(2,1)S(1)}, u32[]{:S(2)}, u32[]{:S(2)}) collective-permute-start(bf16[16,1280]{1,0:T(8,128)(2,1)S(1)} %add_convert_fusion.1), channel_id=1, source_target_pairs={{0,12},{1,13},{2,14},{3,15},{4,8},{5,9},{6,10},{7,11},{8,4},{9,5},... | collective-permute-start | bytes 122888 | tf_op jit(solution)/shard_map/ppermute | solution.py:234
  34.9 5.7 %collective-permute-start.10 = (bf16[16,1280]{1,0:T(8,128)(2,1)S(1)}, bf16[16,1280]{1,0:T(8,128)(2,1)S(1)}, u32[]{:S(2)}, u32[]{:S(2)}) collective-permute-start(bf16[16,1280]{1,0:T(8,128)(2,1)S(1)} %add_convert_fusion.1), channel_id=1, source_target_pairs={{0,4},{1,5},{2,6},{3,7},{4,0},{5,1},{6,2},{7,3},{8,12},{9,13},{10,... | collective-permute-start | bytes 122888 | tf_op jit(solution)/shard_map/ppermute | solution.py:234
  35.8 13.1 %collective-permute-start.4 = (bf16[2,48,2240]{2,1,0:T(8,128)(2,1)S(1)}, bf16[2,48,2240]{2,1,0:T(8,128)(2,1)S(1)}, u32[]{:S(2)}, u32[]{:S(2)}) collective-permute-start(bf16[2,48,2240]{2,1,0:T(8,128)(2,1)S(1)} %get-tuple-element.48), channel_id=1, source_target_pairs={{0,1},{1,0},{2,3},{3,2},{4,5},{5,4},{6,7},{7,6},{8,9},{9,8},{10,11... | collective-permute-start | bytes 1290248 | tf_op jit(solution)/shard_map/ppermute | solution.py:241
  35.8 13.1 %collective-permute-start.5 = (bf16[2,48,2240]{2,1,0:T(8,128)(2,1)S(1)}, bf16[2,48,2240]{2,1,0:T(8,128)(2,1)S(1)}, u32[]{:S(2)}, u32[]{:S(2)}) collective-permute-start(bf16[2,48,2240]{2,1,0:T(8,128)(2,1)S(1)} %get-tuple-element.49), channel_id=1, source_target_pairs={{1,2},{2,1},{3,4},{4,3},{5,6},{6,5},{7,8},{8,7},{9,10},{10,9},{11,... | collective-permute-start | bytes 1290248 | tf_op jit(solution)/shard_map/ppermute | solution.py:241
  36.5 12.3 %copy-start.3 = (bf16[2240,32]{0,1:T(8,128)(2,1)S(1)}, bf16[2240,32]{0,1:T(8,128)(2,1)}, u32[]{:S(2)}) copy-start(bf16[2240,32]{0,1:T(8,128)(2,1)} %param.11) | copy-start | bytes 430084
  36.6 25.8 %copy-start.2 = (bf16[3,3,32,512]{3,2,1,0:T(8,128)(2,1)S(1)}, bf16[3,3,32,512]{3,2,1,0:T(8,128)(2,1)}, u32[]{:S(2)}) copy-start(bf16[3,3,32,512]{3,2,1,0:T(8,128)(2,1)} %param.12) | copy-start | bytes 884740
  36.6 25.8 %copy-start.4 = (f32[512]{0:T(512)S(1)}, f32[512]{0:T(512)}, u32[]{:S(2)}) copy-start(f32[512]{0:T(512)} %param.13) | copy-start | bytes 6148
  40.6 2.9 %collective-permute-start.16 = (bf16[16,1280]{1,0:T(8,128)(2,1)S(1)}, bf16[16,1280]{1,0:T(8,128)(2,1)S(1)}, u32[]{:S(2)}, u32[]{:S(2)}) collective-permute-start(bf16[16,1280]{1,0:T(8,128)(2,1)S(1)} %add_convert_fusion.rest_0_), channel_id=1, source_target_pairs={{0,1},{1,0},{2,3},{3,2},{4,5},{5,4},{6,7},{7,6},{8,9},{9,8},{10,11... | collective-permute-start | bytes 122888 | tf_op jit(solution)/shard_map/ppermute | solution.py:290
  40.7 5.3 %collective-permute-start.15 = (bf16[16,1280]{1,0:T(8,128)(2,1)S(1)}, bf16[16,1280]{1,0:T(8,128)(2,1)S(1)}, u32[]{:S(2)}, u32[]{:S(2)}) collective-permute-start(bf16[16,1280]{1,0:T(8,128)(2,1)S(1)} %add_convert_fusion.rest_0_), channel_id=1, source_target_pairs={{0,48},{16,32},{32,16},{48,0},{64,112},{80,96},{96,80},{112,64},{1... | collective-permute-start | bytes 122888 | tf_op jit(solution)/shard_map/ppermute | solution.py:234
  41.9 5.6 %collective-permute-start.14 = (bf16[16,1280]{1,0:T(8,128)(2,1)S(1)}, bf16[16,1280]{1,0:T(8,128)(2,1)S(1)}, u32[]{:S(2)}, u32[]{:S(2)}) collective-permute-start(bf16[16,1280]{1,0:T(8,128)(2,1)S(1)} %add_convert_fusion.rest_0_), channel_id=1, source_target_pairs={{0,32},{16,48},{32,0},{48,16},{64,96},{80,112},{96,64},{112,80},{1... | collective-permute-start | bytes 122888 | tf_op jit(solution)/shard_map/ppermute | solution.py:234
  43.5 4.0 %collective-permute-start.13 = (bf16[16,1280]{1,0:T(8,128)(2,1)S(1)}, bf16[16,1280]{1,0:T(8,128)(2,1)S(1)}, u32[]{:S(2)}, u32[]{:S(2)}) collective-permute-start(bf16[16,1280]{1,0:T(8,128)(2,1)S(1)} %add_convert_fusion.rest_0_), channel_id=1, source_target_pairs={{0,16},{16,0},{32,48},{48,32},{64,80},{80,64},{96,112},{112,96},{1... | collective-permute-start | bytes 122888 | tf_op jit(solution)/shard_map/ppermute | solution.py:234
  46.0 2.0 %collective-permute-start.19 = (bf16[16,1280]{1,0:T(8,128)(2,1)S(1)}, bf16[16,1280]{1,0:T(8,128)(2,1)S(1)}, u32[]{:S(2)}, u32[]{:S(2)}) collective-permute-start(bf16[16,1280]{1,0:T(8,128)(2,1)S(1)} %collective-permute-done.15.rest_3_), channel_id=1, source_target_pairs={{0,1},{1,0},{2,3},{3,2},{4,5},{5,4},{6,7},{7,6},{8,9},{9,8},{10,11... | collective-permute-start | bytes 122888 | tf_op jit(solution)/shard_map/ppermute | solution.py:290
  47.5 1.2 %collective-permute-start.18 = (bf16[16,1280]{1,0:T(8,128)(2,1)S(1)}, bf16[16,1280]{1,0:T(8,128)(2,1)S(1)}, u32[]{:S(2)}, u32[]{:S(2)}) collective-permute-start(bf16[16,1280]{1,0:T(8,128)(2,1)S(1)} %collective-permute-done.14.rest_2_), channel_id=1, source_target_pairs={{0,1},{1,0},{2,3},{3,2},{4,5},{5,4},{6,7},{7,6},{8,9},{9,8},{10,11... | collective-permute-start | bytes 122888 | tf_op jit(solution)/shard_map/ppermute | solution.py:290
  47.5 1.4 %collective-permute-start.17 = (bf16[16,1280]{1,0:T(8,128)(2,1)S(1)}, bf16[16,1280]{1,0:T(8,128)(2,1)S(1)}, u32[]{:S(2)}, u32[]{:S(2)}) collective-permute-start(bf16[16,1280]{1,0:T(8,128)(2,1)S(1)} %collective-permute-done.13.rest_1_), channel_id=1, source_target_pairs={{0,1},{1,0},{2,3},{3,2},{4,5},{5,4},{6,7},{7,6},{8,9},{9,8},{10,11... | collective-permute-start | bytes 122888 | tf_op jit(solution)/shard_map/ppermute | solution.py:290
  52.4 5.1 %collective-permute-start.20 = (f32[6,32,32]{2,1,0:T(8,128)S(1)}, f32[6,32,32]{2,1,0:T(8,128)S(1)}, u32[]{:S(2)}, u32[]{:S(2)}) collective-permute-start(f32[6,32,32]{2,1,0:T(8,128)S(1)} %get-tuple-element.61), channel_id=1, source_target_pairs={{0,16},{16,0},{32,48},{48,32},{64,80},{80,64},{96,112},{112,96},{1... | collective-permute-start | bytes 73736 | tf_op jit(solution)/shard_map/ppermute | solution.py:241
  53.8 8.6 %collective-permute-start.21 = (f32[6,32,32]{2,1,0:T(8,128)S(1)}, f32[6,32,32]{2,1,0:T(8,128)S(1)}, u32[]{:S(2)}, u32[]{:S(2)}) collective-permute-start(f32[6,32,32]{2,1,0:T(8,128)S(1)} %get-tuple-element.62), channel_id=1, source_target_pairs={{16,32},{32,16},{48,64},{64,48},{80,96},{96,80},{112,128},{128,112... | collective-permute-start | bytes 73736 | tf_op jit(solution)/shard_map/ppermute | solution.py:241

commit v5 on v4

--- a/solution.py
+++ b/solution.py
@@ -16,9 +16,14 @@
 SPLIT = (1, 3, 2)
 
 
-def sums_kernel(scale, at_ref, k_hbm, v_hbm, mine_ref, other_ref, k_ref, v_ref, sems):
+def position():
+    row, col = lax.axis_index("row"), lax.axis_index("col")
+    return row, col, lax.rem(row, 4), lax.rem(col, 2), lax.rem(row, 2)
+
+
+def sums_kernel(scale, k_hbm, v_hbm, mine_ref, other_ref, k_ref, v_ref, sems):
     images, tokens, width = k_ref.shape
-    core = at_ref[3]
+    core = position()[3]
     half = tokens // 2
     copies = []
     for n in range(images):
@@ -61,7 +66,7 @@
                 out_ref[2 * r + c] = total[16 * r : 16 * r + 16, wide * c : wide * (c + 1)]
 
 
-def image_sums(keys, values, at, scale):
+def image_sums(keys, values, scale):
     images, tokens, width = keys.shape
     out = pltpu.VMEM((4, 16, PACK // 2), jnp.bfloat16)
     vmem = pl.BlockSpec(memory_space=pltpu.VMEM)
@@ -69,7 +74,7 @@
     return pl.pallas_call(
         functools.partial(sums_kernel, scale),
         out_shape=[out, out],
-        in_specs=[pl.BlockSpec(memory_space=pltpu.SMEM), hbm, hbm],
+        in_specs=[hbm, hbm],
         out_specs=[vmem, vmem],
         scratch_shapes=[
             pltpu.VMEM(keys.shape, keys.dtype),
@@ -79,10 +84,11 @@
         compiler_params=pltpu.CompilerParams(vmem_limit_bytes=56 << 20),
         cost_estimate=pl.CostEstimate(flops=4 * tokens * width * 256, bytes_accessed=8 * tokens * width, transcendentals=0),
         name="image_sums",
-    )(at, keys, values)
-
-
-def sides_kernel(at_ref, q_ref, near_ref, far_ref):
+    )(keys, values)
+
+
+def sides_kernel(q_ref, near_ref, far_ref):
+    at_ref = position()
     tokens = q_ref.shape[1]
     edge = near_ref.shape[1]
     odd = at_ref[3] == 1
@@ -97,7 +103,7 @@
     far_ref[0] = jnp.where(odd, picked[edge:], picked[:edge])
 
 
-def sides(at, queries):
+def sides(queries):
     images, tokens, width = queries.shape
     edge = 16 * WIDE
     out = jax.ShapeDtypeStruct((images, edge, width), queries.dtype)
@@ -106,20 +112,18 @@
         sides_kernel,
         out_shape=[out, out],
         grid=(images,),
-        in_specs=[
-            pl.BlockSpec(memory_space=pltpu.SMEM),
-            pl.BlockSpec((1, tokens, width), lambda i: (i, 0, 0)),
-        ],
+        in_specs=[pl.BlockSpec((1, tokens, width), lambda i: (i, 0, 0))],
         out_specs=[block, block],
         compiler_params=pltpu.CompilerParams(vmem_limit_bytes=48 << 20),
         cost_estimate=pl.CostEstimate(flops=10**9, bytes_accessed=3 * images * tokens * width, transcendentals=0),
         name="sides",
-    )(at, queries)
+    )(queries)
 
 
 def attend_kernel(
-    at_ref, q_ref, near_ref, far_ref, *rest,
+    q_ref, near_ref, far_ref, *rest,
 ):
+    at_ref = position()
     pieces, (weight_ref, out_ref, near_out_ref, far_out_ref, sums) = rest[:8], rest[8:]
     f32, bf16 = jnp.float32, jnp.bfloat16
     images, inner, width = q_ref.shape
@@ -201,7 +205,7 @@
     far_out_ref[...] = jnp.where(odd_row, last, first)
 
 
-def attend(at, queries, sides, pieces, weight):
+def attend(queries, sides, pieces, weight):
     images, tokens, width = queries.shape
     channels = weight.shape[1]
     vmem = pl.BlockSpec(memory_space=pltpu.VMEM)
@@ -210,13 +214,13 @@
         out_shape=[
             jax.ShapeDtypeStruct((images * lines, 32, channels), jnp.float32) for lines in (16, WIDE, WIDE)
         ],
-        in_specs=[pl.BlockSpec(memory_space=pltpu.SMEM)] + [vmem] * 12,
+        in_specs=[vmem] * 12,
         out_specs=[vmem] * 3,
         scratch_shapes=[pltpu.VMEM((4, images, 16, PACK // 2), jnp.bfloat16)],
         compiler_params=pltpu.CompilerParams(vmem_limit_bytes=32 << 20),
         cost_estimate=pl.CostEstimate(flops=2 * images * tokens * width * 512, bytes_accessed=2 * images * tokens * width, transcendentals=0),
         name="attend",
-    )(at, queries, *sides, *pieces, weight.T)
+    )(queries, *sides, *pieces, weight.T)
 
 
 def xor_pairs(distance):
@@ -241,7 +245,8 @@
     return lax.ppermute(even, axis, near), lax.ppermute(odd, axis, far)
 
 
-def split_kernel(at_ref, mine_ref, arrived_ref, own_ref, *parts_ref):
+def split_kernel(mine_ref, arrived_ref, own_ref, *parts_ref):
+    at_ref = position()
     f32 = jnp.float32
     for d, out_ref in zip((0,) + SPLIT, (own_ref,) + parts_ref):
         chunk = at_ref[2] ^ d
@@ -249,27 +254,27 @@
         out_ref[...] = total.astype(out_ref.dtype)
 
 
-def split(at, mine, arrived):
+def split(mine, arrived):
     shape = mine.shape[1:]
     vmem = pl.BlockSpec(memory_space=pltpu.VMEM)
     return pl.pallas_call(
         split_kernel,
         out_shape=[jax.ShapeDtypeStruct(shape, jnp.float32)]
         + [jax.ShapeDtypeStruct(shape, jnp.bfloat16)] * len(SPLIT),
-        in_specs=[pl.BlockSpec(memory_space=pltpu.SMEM), vmem, vmem],
+        in_specs=[vmem, vmem],
         out_specs=[vmem] * (1 + len(SPLIT)),
         compiler_params=pltpu.CompilerParams(vmem_limit_bytes=8 << 20),
         name="split",
-    )(at, mine, arrived)
-
-
-def gather_all(at, mine, other, queries, residual, upscale):
+    )(mine, arrived)
+
+
+def gather_all(mine, other, queries, residual, upscale):
     hold = lax.optimization_barrier
     arrived = lax.ppermute(other, "col", xor_pairs(1))
     near, mine = hold((queries, mine))
-    start, end = sides(at, near)
+    start, end = sides(near)
     arrived, start, end = hold((arrived, start, end))
-    own, *parts = split(at, mine, arrived)
+    own, *parts = split(mine, arrived)
     parts = [lax.ppermute(part, "row", xor_pairs(d)) for part, d in zip(parts, SPLIT)]
     chunk = added(own, parts)
 
@@ -301,9 +306,10 @@
 
 
 def decode_kernel(
-    tiles, at_ref, lat_ref, near_ref, far_ref, entry_ref, gain_ref, residual_ref, upscale_ref, out_hbm,
+    tiles, lat_ref, near_ref, far_ref, entry_ref, gain_ref, residual_ref, upscale_ref, out_hbm,
     wide, dec, hid, taps, ref, centre, slope, mix, out_ref, sems,
 ):
+    at_ref = position()
     tile = 16
     channels = out_hbm.shape[-1]
     pitch = 24
@@ -480,7 +486,7 @@
     )(upscale.reshape(shape))
 
 
-def decode(at, latent, entry, gain, residual, combined, tiles):
+def decode(latent, entry, gain, residual, combined, tiles):
     images, tile = 2, 16
     latents = latent[0].shape[-1]
     channels = entry.shape[-1]
@@ -494,7 +500,7 @@
     out = pl.pallas_call(
         functools.partial(decode_kernel, tiles),
         out_shape=jax.ShapeDtypeStruct((images, tile, 2, 2 * tile, channels), bf16),
-        in_specs=[pl.BlockSpec(memory_space=pltpu.SMEM)] + [vmem] * 7,
+        in_specs=[vmem] * 7,
         out_specs=hbm,
         scratch_shapes=[
             pltpu.VMEM((images * (tile + 6) * pitch, 3 * latents), bf16),
@@ -512,7 +518,6 @@
         cost_estimate=pl.CostEstimate(flops=8 * 10**9, bytes_accessed=12 << 20, transcendentals=0),
         name="decode",
     )(
-        at,
         *latent,
         entry.reshape(3, 3 * entry.shape[2], channels),
         gain.reshape(1, channels),
@@ -536,19 +541,16 @@
     scale = 1.0 / (tile * lax.axis_size("row") * tile * lax.axis_size("col"))
     flat = (images, tile * tile, width)
     keys, values = key_rows_per_head.reshape(flat), value_rows_per_head.reshape(flat)
-    row, col = lax.axis_index("row"), lax.axis_index("col")
-    at = jnp.stack([row, col, row % 4, col % 2, row % 2]).astype(jnp.int32)
-    mine, other = image_sums(keys, values, at, scale)
+    mine, other = image_sums(keys, values, scale)
     channels = residual_conv_weight.shape[-1]
     residual = residual_conv_weight.reshape(9 * channels, channels)
     queries = queries.reshape(flat)
     pieces, beside, residual, combined = gather_all(
-        at, mine, other, queries, residual, upscale_conv_weight
+        mine, other, queries, residual, upscale_conv_weight
     )
-    latent, near, far = attend(at, queries, beside, pieces, latent_projection_weight)
+    latent, near, far = attend(queries, beside, pieces, latent_projection_weight)
     near, far = swapped(near, far, "row")
     return decode(
-        at,
         (latent, near, far),
         entry_conv_weight,
         residual_norm_gain,

time: 71.8 us -> 68.5 us (0.954)
  Pallas kernels: 21.1 us -> 17.9 us
    pallas_call x1, Pallas kernels: 3.96 us -> 3.1 us  [image_sums(): pl.pallas_call(functools.partial(sums_kernel, scale), out_shape=[out, out...]
where the time goes in v5:
time: 68.5 us; the launch traced here: 68.3 us
  starting transfers between devices  27.6 us (40%)
  waiting for transfers between devices  22.3 us (33%)
  Pallas kernels  17.9 us (26%)
    ppermute x10, starting transfers between devices, sent(): return [lax.ppermute(value, axis, xor_pairs(d)) for d in distances]  18 us
    ppermute x10, waiting for transfers between devices, sent(): return [lax.ppermute(value, axis, xor_pairs(d)) for d in distances]  9.91 us
    pallas_call x1, Pallas kernels, decode(): pl.pallas_call(functools.partial(decode_kernel, tiles), out_shape=jax.Sha...  8.46 us
    ppermute x4, waiting for transfers between devices, swapped(): return (lax.ppermute(even, axis, near), lax.ppermute(odd, axis, far))  6.06 us
    ppermute x3, waiting for transfers between devices, gather_all(): lax.ppermute(part, 'row', xor_pairs(d))  4.87 us
    ppermute x4, starting transfers between devices, swapped(): return (lax.ppermute(even, axis, near), lax.ppermute(odd, axis, far))  4.55 us
    ppermute x3, starting transfers between devices, gather_all(): lax.ppermute(part, 'row', xor_pairs(d))  4.31 us
    pallas_call x1, Pallas kernels, image_sums(): pl.pallas_call(functools.partial(sums_kernel, scale), out_shape=[out, out...  3.1 us
  transfers between devices with their start and end apart: 22, of which 14 were waited for; matrix products, arithmetic and copies ran while one was open for 0% of the time, Pallas kernels for 5%

profile of v5, /device:TPU:24, one launch (start us, length us, event | category | flops | bytes accessed | tf_op | source)
XLA Modules:
  0.0 68.3 jit_solution(5306819407337464197)
XLA Ops:
  0.0 3.1 %image_sums.1 = (bf16[4,16,1280]{2,1,0:T(8,128)(2,1)S(1)}, bf16[4,16,1280]{2,1,0:T(8,128)(2,1)S(1)}) custom-call(bf16[2,256,2240]{2,1,0:T(8,128)(2,1)} %bitcast.20, bf16[2,256,2240]{2,1,0:T(8,128)(2,1)} %bitcast.21), custom_call_target="tpu_custom_call" | custom-call | flops 587202560 | bytes 4587520 | tf_op jit(solution)/shard_map/image_sums/pallas_call | solution.py:74
  3.2 0.7 %sides.1 = (bf16[2,48,2240]{2,1,0:T(8,128)(2,1)S(1)}, bf16[2,48,2240]{2,1,0:T(8,128)(2,1)S(1)}) custom-call(bf16[2,256,2240]{2,1,0:T(8,128)(2,1)S(1)} %bitcast.15), custom_call_target="tpu_custom_call" | custom-call | flops 1000000000 | bytes 3440640 | tf_op jit(solution)/shard_map/sides/pallas_call | solution.py:111
  4.6 1.6 %collective-permute-start.1 = (bf16[16,1280]{1,0:T(8,128)(2,1)S(1)}, bf16[16,1280]{1,0:T(8,128)(2,1)S(1)}, u32[]{:S(2)}, u32[]{:S(2)}) collective-permute-start(bf16[16,1280]{1,0:T(8,128)(2,1)S(1)} %get-tuple-element.43), channel_id=1, source_target_pairs={{0,16},{16,0},{32,48},{48,32},{64,80},{80,64},{96,112},{112,96},{1... | collective-permute-start | bytes 122888 | tf_op jit(solution)/shard_map/ppermute | solution.py:278
  6.2 2.1 %collective-permute-start.2 = (bf16[16,1280]{1,0:T(8,128)(2,1)S(1)}, bf16[16,1280]{1,0:T(8,128)(2,1)S(1)}, u32[]{:S(2)}, u32[]{:S(2)}) collective-permute-start(bf16[16,1280]{1,0:T(8,128)(2,1)S(1)} %get-tuple-element.44), channel_id=1, source_target_pairs={{0,48},{16,32},{32,16},{48,0},{64,112},{80,96},{96,80},{112,64},{1... | collective-permute-start | bytes 122888 | tf_op jit(solution)/shard_map/ppermute | solution.py:278
  8.3 0.6 collective-permute-start.3
  9.0 2.5 %collective-permute-done.2 = bf16[16,1280]{1,0:T(8,128)(2,1)S(1)} collective-permute-done((bf16[16,1280]{1,0:T(8,128)(2,1)S(1)}, bf16[16,1280]{1,0:T(8,128)(2,1)S(1)}, u32[]{:S(2)}, u32[]{:S(2)}) %collective-permute-start.2) | collective-permute-done | bytes 40992 | tf_op jit(solution)/shard_map/ppermute | solution.py:278
  11.4 2.4 %collective-permute-done.3 = bf16[16,1280]{1,0:T(8,128)(2,1)S(1)} collective-permute-done((bf16[16,1280]{1,0:T(8,128)(2,1)S(1)}, bf16[16,1280]{1,0:T(8,128)(2,1)S(1)}, u32[]{:S(2)}, u32[]{:S(2)}) %collective-permute-start.3) | collective-permute-done | bytes 40992 | tf_op jit(solution)/shard_map/ppermute | solution.py:278
  13.9 1.3 %collective-permute-start.8 = (bf16[16,1280]{1,0:T(8,128)(2,1)S(1)}, bf16[16,1280]{1,0:T(8,128)(2,1)S(1)}, u32[]{:S(2)}, u32[]{:S(2)}) collective-permute-start(bf16[16,1280]{1,0:T(8,128)(2,1)S(1)} %add_convert_fusion.3), channel_id=1, source_target_pairs={{0,128},{16,144},{32,160},{48,176},{64,192},{80,208},{96,224},{112... | collective-permute-start | bytes 122888 | tf_op jit(solution)/shard_map/ppermute | solution.py:238
  15.2 2.2 %collective-permute-start.7 = (bf16[16,1280]{1,0:T(8,128)(2,1)S(1)}, bf16[16,1280]{1,0:T(8,128)(2,1)S(1)}, u32[]{:S(2)}, u32[]{:S(2)}) collective-permute-start(bf16[16,1280]{1,0:T(8,128)(2,1)S(1)} %add_convert_fusion.3), channel_id=1, source_target_pairs={{0,192},{16,208},{32,224},{48,240},{64,128},{80,144},{96,160},{112... | collective-permute-start | bytes 122888 | tf_op jit(solution)/shard_map/ppermute | solution.py:238
  17.5 1.0 %keep.1.residual_ref = bf16[4608,512]{1,0:T(8,128)(2,1)S(1)} custom-call(bf16[4608,512]{1,0:T(8,128)(2,1)S(1)} %bitcast.11), custom_call_target="tpu_custom_call" | custom-call | bytes 4718592 | tf_op jit(solution)/shard_map/keep/pallas_call | solution.py:440
  18.5 1.0 %collective-permute-done.8 = bf16[16,1280]{1,0:T(8,128)(2,1)S(1)} collective-permute-done((bf16[16,1280]{1,0:T(8,128)(2,1)S(1)}, bf16[16,1280]{1,0:T(8,128)(2,1)S(1)}, u32[]{:S(2)}, u32[]{:S(2)}) %collective-permute-start.8) | collective-permute-done | bytes 40992 | tf_op jit(solution)/shard_map/ppermute | solution.py:238
  19.5 0.9 %collective-permute-done.7 = bf16[16,1280]{1,0:T(8,128)(2,1)S(1)} collective-permute-done((bf16[16,1280]{1,0:T(8,128)(2,1)S(1)}, bf16[16,1280]{1,0:T(8,128)(2,1)S(1)}, u32[]{:S(2)}, u32[]{:S(2)}) %collective-permute-start.7) | collective-permute-done | bytes 40992 | tf_op jit(solution)/shard_map/ppermute | solution.py:238
  20.4 1.0 %collective-permute-done.6 = bf16[16,1280]{1,0:T(8,128)(2,1)S(1)} collective-permute-done((bf16[16,1280]{1,0:T(8,128)(2,1)S(1)}, bf16[16,1280]{1,0:T(8,128)(2,1)S(1)}, u32[]{:S(2)}, u32[]{:S(2)}) %collective-permute-start.6) | collective-permute-done | bytes 40992 | tf_op jit(solution)/shard_map/ppermute | solution.py:238
  21.4 2.0 %collective-permute-start.9 = (bf16[16,1280]{1,0:T(8,128)(2,1)S(1)}, bf16[16,1280]{1,0:T(8,128)(2,1)S(1)}, u32[]{:S(2)}, u32[]{:S(2)}) collective-permute-start(bf16[16,1280]{1,0:T(8,128)(2,1)S(1)} %add_convert_fusion.2), channel_id=1, source_target_pairs={{0,2},{1,3},{2,0},{3,1},{4,6},{5,7},{6,4},{7,5},{8,10},{9,11},{10,... | collective-permute-start | bytes 122888 | tf_op jit(solution)/shard_map/ppermute | solution.py:238
  23.4 2.1 %collective-permute-done.9 = bf16[16,1280]{1,0:T(8,128)(2,1)S(1)} collective-permute-done((bf16[16,1280]{1,0:T(8,128)(2,1)S(1)}, bf16[16,1280]{1,0:T(8,128)(2,1)S(1)}, u32[]{:S(2)}, u32[]{:S(2)}) %collective-permute-start.9) | collective-permute-done | bytes 40992 | tf_op jit(solution)/shard_map/ppermute | solution.py:238
  25.5 6.8 %collective-permute-start.12 = (bf16[16,1280]{1,0:T(8,128)(2,1)S(1)}, bf16[16,1280]{1,0:T(8,128)(2,1)S(1)}, u32[]{:S(2)}, u32[]{:S(2)}) collective-permute-start(bf16[16,1280]{1,0:T(8,128)(2,1)S(1)} %add_convert_fusion.1), channel_id=1, source_target_pairs={{0,10},{1,11},{2,8},{3,9},{4,14},{5,15},{6,12},{7,13},{8,2},{9,3},... | collective-permute-start | bytes 122888 | tf_op jit(solution)/shard_map/ppermute | solution.py:238
  32.9 0.9 %collective-permute-start.10 = (bf16[16,1280]{1,0:T(8,128)(2,1)S(1)}, bf16[16,1280]{1,0:T(8,128)(2,1)S(1)}, u32[]{:S(2)}, u32[]{:S(2)}) collective-permute-start(bf16[16,1280]{1,0:T(8,128)(2,1)S(1)} %add_convert_fusion.1), channel_id=1, source_target_pairs={{0,4},{1,5},{2,6},{3,7},{4,0},{5,1},{6,2},{7,3},{8,12},{9,13},{10,... | collective-permute-start | bytes 122888 | tf_op jit(solution)/shard_map/ppermute | solution.py:238
  33.8 0.7 collective-permute-start.5
  34.6 1.6 %phases.1.upscale_ref = bf16[9,512,512]{2,1,0:T(8,128)(2,1)S(1)} custom-call(bf16[9,512,512]{2,1,0:T(8,128)(2,1)S(1)} %bitcast.14), custom_call_target="tpu_custom_call" | custom-call | flops 2621440 | bytes 4718592 | tf_op jit(solution)/shard_map/phases/pallas_call | solution.py:477
  36.2 2.3 %collective-permute-done.11 = bf16[16,1280]{1,0:T(8,128)(2,1)S(1)} collective-permute-done((bf16[16,1280]{1,0:T(8,128)(2,1)S(1)}, bf16[16,1280]{1,0:T(8,128)(2,1)S(1)}, u32[]{:S(2)}, u32[]{:S(2)}) %collective-permute-start.11) | collective-permute-done | bytes 40992 | tf_op jit(solution)/shard_map/ppermute | solution.py:238
  38.6 1.2 %collective-permute-start.15 = (bf16[16,1280]{1,0:T(8,128)(2,1)S(1)}, bf16[16,1280]{1,0:T(8,128)(2,1)S(1)}, u32[]{:S(2)}, u32[]{:S(2)}) collective-permute-start(bf16[16,1280]{1,0:T(8,128)(2,1)S(1)} %add_convert_fusion.rest_0_), channel_id=1, source_target_pairs={{0,48},{16,32},{32,16},{48,0},{64,112},{80,96},{96,80},{112,64},{1... | collective-permute-start | bytes 122888 | tf_op jit(solution)/shard_map/ppermute | solution.py:238
  39.8 1.5 %collective-permute-start.14 = (bf16[16,1280]{1,0:T(8,128)(2,1)S(1)}, bf16[16,1280]{1,0:T(8,128)(2,1)S(1)}, u32[]{:S(2)}, u32[]{:S(2)}) collective-permute-start(bf16[16,1280]{1,0:T(8,128)(2,1)S(1)} %add_convert_fusion.rest_0_), channel_id=1, source_target_pairs={{0,32},{16,48},{32,0},{48,16},{64,96},{80,112},{96,64},{112,80},{1... | collective-permute-start | bytes 122888 | tf_op jit(solution)/shard_map/ppermute | solution.py:238
  41.3 1.4 %collective-permute-start.13 = (bf16[16,1280]{1,0:T(8,128)(2,1)S(1)}, bf16[16,1280]{1,0:T(8,128)(2,1)S(1)}, u32[]{:S(2)}, u32[]{:S(2)}) collective-permute-start(bf16[16,1280]{1,0:T(8,128)(2,1)S(1)} %add_convert_fusion.rest_0_), channel_id=1, source_target_pairs={{0,16},{16,0},{32,48},{48,32},{64,80},{80,64},{96,112},{112,96},{1... | collective-permute-start | bytes 122888 | tf_op jit(solution)/shard_map/ppermute | solution.py:238
  42.8 1.1 %collective-permute-done.15.rest_3_ = bf16[16,1280]{1,0:T(8,128)(2,1)S(1)} collective-permute-done((bf16[16,1280]{1,0:T(8,128)(2,1)S(1)}, bf16[16,1280]{1,0:T(8,128)(2,1)S(1)}, u32[]{:S(2)}, u32[]{:S(2)}) %collective-permute-start.15) | collective-permute-done | bytes 40992 | tf_op jit(solution)/shard_map/ppermute | solution.py:238
  43.9 1.5 %collective-permute-done.14.rest_2_ = bf16[16,1280]{1,0:T(8,128)(2,1)S(1)} collective-permute-done((bf16[16,1280]{1,0:T(8,128)(2,1)S(1)}, bf16[16,1280]{1,0:T(8,128)(2,1)S(1)}, u32[]{:S(2)}, u32[]{:S(2)}) %collective-permute-start.14) | collective-permute-done | bytes 40992 | tf_op jit(solution)/shard_map/ppermute | solution.py:238
  45.9 0.7 %collective-permute-done.18.rest_6_ = bf16[16,1280]{1,0:T(8,128)(2,1)S(1)} collective-permute-done((bf16[16,1280]{1,0:T(8,128)(2,1)S(1)}, bf16[16,1280]{1,0:T(8,128)(2,1)S(1)}, u32[]{:S(2)}, u32[]{:S(2)}) %collective-permute-start.18) | collective-permute-done | bytes 40992 | tf_op jit(solution)/shard_map/ppermute | solution.py:295
  46.8 3.0 %attend.1 = (f32[32,32,32]{2,1,0:T(8,128)S(1)}, f32[6,32,32]{2,1,0:T(8,128)S(1)}, f32[6,32,32]{2,1,0:T(8,128)S(1)}) custom-call(bf16[2,256,2240]{2,1,0:T(8,128)(2,1)S(1)} %bitcast.16, bf16[2,48,2240]{2,1,0:T(8,128)(2,1)S(1)} %collective-permute-done.4.near_ref, bf16[2,48,2240]{2,1,0:T(8,128)(2,1)S(1)} %collective-permute-done.5.far_ref, ...), custom_call_target="tpu_custom_call" | custom-call | flops 1174405120 | bytes 2293760 | tf_op jit(solution)/shard_map/attend/pallas_call | solution.py:212
  49.8 1.3 %collective-permute-start.20 = (f32[6,32,32]{2,1,0:T(8,128)S(1)}, f32[6,32,32]{2,1,0:T(8,128)S(1)}, u32[]{:S(2)}, u32[]{:S(2)}) collective-permute-start(f32[6,32,32]{2,1,0:T(8,128)S(1)} %get-tuple-element.61), channel_id=1, source_target_pairs={{0,16},{16,0},{32,48},{48,32},{64,80},{80,64},{96,112},{112,96},{1... | collective-permute-start | bytes 73736 | tf_op jit(solution)/shard_map/ppermute | solution.py:245
  51.1 2.5 %collective-permute-start.21 = (f32[6,32,32]{2,1,0:T(8,128)S(1)}, f32[6,32,32]{2,1,0:T(8,128)S(1)}, u32[]{:S(2)}, u32[]{:S(2)}) collective-permute-start(f32[6,32,32]{2,1,0:T(8,128)S(1)} %get-tuple-element.62), channel_id=1, source_target_pairs={{16,32},{32,16},{48,64},{64,48},{80,96},{96,80},{112,128},{128,112... | collective-permute-start | bytes 73736 | tf_op jit(solution)/shard_map/ppermute | solution.py:245
  53.7 1.3 %collective-permute-done.20.near_ref = f32[6,32,32]{2,1,0:T(8,128)S(1)} collective-permute-done((f32[6,32,32]{2,1,0:T(8,128)S(1)}, f32[6,32,32]{2,1,0:T(8,128)S(1)}, u32[]{:S(2)}, u32[]{:S(2)}) %collective-permute-start.20) | collective-permute-done | bytes 24608 | tf_op jit(solution)/shard_map/ppermute | solution.py:245
  54.9 4.8 %collective-permute-done.21.far_ref = f32[6,32,32]{2,1,0:T(8,128)S(1)} collective-permute-done((f32[6,32,32]{2,1,0:T(8,128)S(1)}, f32[6,32,32]{2,1,0:T(8,128)S(1)}, u32[]{:S(2)}, u32[]{:S(2)}) %collective-permute-start.21) | collective-permute-done | bytes 24608 | tf_op jit(solution)/shard_map/ppermute | solution.py:245
  59.7 8.5 %decode.1 = bf16[2,16,2,32,512]{4,3,2,1,0:T(8,128)(2,1)} custom-call(f32[32,32,32]{2,1,0:T(8,128)S(1)} %get-tuple-element.60.lat_ref, f32[6,32,32]{2,1,0:T(8,128)S(1)} %collective-permute-done.20.near_ref, f32[6,32,32]{2,1,0:T(8,128)S(1)} %collective-permute-done.21.far_ref, bf16[3,96,512]{2,1,0:T(8,128)(2,1)S(1)} %bitcast.17, f32[1,512]{1,0:T(1,128)S(1)} %bitcast.19, ...), custom_call_target="tpu_custom_call" | custom-call | flops 8000000000 | bytes 12582912 | tf_op jit(solution)/shard_map/decode/pallas_call | solution.py:500
  (41 shorter events, 2.4 us)
Async XLA Ops:
  0.0 3.2 %copy-start = (bf16[2,16,16,2240]{3,2,1,0:T(8,128)(2,1)S(1)}, bf16[2,16,16,2240]{3,2,1,0:T(8,128)(2,1)}, u32[]{:S(2)}) copy-start(bf16[2,16,16,2240]{3,2,1,0:T(8,128)(2,1)} %param.8) | copy-start | bytes 6881284
  0.0 17.4 %slice-start = ((s8[4718592]{0:T(1024)(128)(4,1)}), s8[4194304]{0:T(1024)(128)(4,1)S(1)}, s32[]{:S(2)}) async-start(s8[4718592]{0:T(1024)(128)(4,1)} %bitcast.9), calls=%async_computation | async-start | bytes 8388608
  0.0 17.4 %slice-start.1 = ((s8[4718592]{0:T(1024)(128)(4,1)}), s8[524288]{0:T(1024)(128)(4,1)S(1)}, s32[]{:S(2)}) async-start(s8[4718592]{0:T(1024)(128)(4,1)} %bitcast.9), calls=%async_computation.1 | async-start | bytes 1048576
  3.1 1.5 %collective-permute-start = (bf16[4,16,1280]{2,1,0:T(8,128)(2,1)S(1)}, bf16[4,16,1280]{2,1,0:T(8,128)(2,1)S(1)}, u32[]{:S(2)}, u32[]{:S(2)}) collective-permute-start(bf16[4,16,1280]{2,1,0:T(8,128)(2,1)S(1)} %get-tuple-element.37), channel_id=1, source_target_pairs={{0,1},{1,0},{2,3},{3,2},{4,5},{5,4},{6,7},{7,6},{8,9},{9,8},{10,11... | collective-permute-start | bytes 491528 | tf_op jit(solution)/shard_map/ppermute | solution.py:273
  4.6 4.3 %collective-permute-start.1 = (bf16[16,1280]{1,0:T(8,128)(2,1)S(1)}, bf16[16,1280]{1,0:T(8,128)(2,1)S(1)}, u32[]{:S(2)}, u32[]{:S(2)}) collective-permute-start(bf16[16,1280]{1,0:T(8,128)(2,1)S(1)} %get-tuple-element.43), channel_id=1, source_target_pairs={{0,16},{16,0},{32,48},{48,32},{64,80},{80,64},{96,112},{112,96},{1... | collective-permute-start | bytes 122888 | tf_op jit(solution)/shard_map/ppermute | solution.py:278
  6.2 5.2 %collective-permute-start.2 = (bf16[16,1280]{1,0:T(8,128)(2,1)S(1)}, bf16[16,1280]{1,0:T(8,128)(2,1)S(1)}, u32[]{:S(2)}, u32[]{:S(2)}) collective-permute-start(bf16[16,1280]{1,0:T(8,128)(2,1)S(1)} %get-tuple-element.44), channel_id=1, source_target_pairs={{0,48},{16,32},{32,16},{48,0},{64,112},{80,96},{96,80},{112,64},{1... | collective-permute-start | bytes 122888 | tf_op jit(solution)/shard_map/ppermute | solution.py:278
  8.3 5.5 %collective-permute-start.3 = (bf16[16,1280]{1,0:T(8,128)(2,1)S(1)}, bf16[16,1280]{1,0:T(8,128)(2,1)S(1)}, u32[]{:S(2)}, u32[]{:S(2)}) collective-permute-start(bf16[16,1280]{1,0:T(8,128)(2,1)S(1)} %get-tuple-element.45), channel_id=1, source_target_pairs={{0,32},{16,48},{32,0},{48,16},{64,96},{80,112},{96,64},{112,80},{1... | collective-permute-start | bytes 122888 | tf_op jit(solution)/shard_map/ppermute | solution.py:278
  13.8 20.7 %slice-start.2 = ((s8[4718592]{0:T(1024)(128)(4,1)}), s8[4194304]{0:T(1024)(128)(4,1)S(1)}, s32[]{:S(2)}) async-start(s8[4718592]{0:T(1024)(128)(4,1)} %bitcast.12), calls=%async_computation.2 | async-start | bytes 8388608
  13.9 20.7 %slice-start.3 = ((s8[4718592]{0:T(1024)(128)(4,1)}), s8[524288]{0:T(1024)(128)(4,1)S(1)}, s32[]{:S(2)}) async-start(s8[4718592]{0:T(1024)(128)(4,1)} %bitcast.12), calls=%async_computation.3 | async-start | bytes 1048576
  13.9 5.6 %collective-permute-start.8 = (bf16[16,1280]{1,0:T(8,128)(2,1)S(1)}, bf16[16,1280]{1,0:T(8,128)(2,1)S(1)}, u32[]{:S(2)}, u32[]{:S(2)}) collective-permute-start(bf16[16,1280]{1,0:T(8,128)(2,1)S(1)} %add_convert_fusion.3), channel_id=1, source_target_pairs={{0,128},{16,144},{32,160},{48,176},{64,192},{80,208},{96,224},{112... | collective-permute-start | bytes 122888 | tf_op jit(solution)/shard_map/ppermute | solution.py:238
  15.2 5.2 %collective-permute-start.7 = (bf16[16,1280]{1,0:T(8,128)(2,1)S(1)}, bf16[16,1280]{1,0:T(8,128)(2,1)S(1)}, u32[]{:S(2)}, u32[]{:S(2)}) collective-permute-start(bf16[16,1280]{1,0:T(8,128)(2,1)S(1)} %add_convert_fusion.3), channel_id=1, source_target_pairs={{0,192},{16,208},{32,224},{48,240},{64,128},{80,144},{96,160},{112... | collective-permute-start | bytes 122888 | tf_op jit(solution)/shard_map/ppermute | solution.py:238
  17.4 4.0 %collective-permute-start.6 = (bf16[16,1280]{1,0:T(8,128)(2,1)S(1)}, bf16[16,1280]{1,0:T(8,128)(2,1)S(1)}, u32[]{:S(2)}, u32[]{:S(2)}) collective-permute-start(bf16[16,1280]{1,0:T(8,128)(2,1)S(1)} %add_convert_fusion.3), channel_id=1, source_target_pairs={{0,64},{16,80},{32,96},{48,112},{64,0},{80,16},{96,32},{112,48},{1... | collective-permute-start | bytes 122888 | tf_op jit(solution)/shard_map/ppermute | solution.py:238
  21.4 4.1 %collective-permute-start.9 = (bf16[16,1280]{1,0:T(8,128)(2,1)S(1)}, bf16[16,1280]{1,0:T(8,128)(2,1)S(1)}, u32[]{:S(2)}, u32[]{:S(2)}) collective-permute-start(bf16[16,1280]{1,0:T(8,128)(2,1)S(1)} %add_convert_fusion.2), channel_id=1, source_target_pairs={{0,2},{1,3},{2,0},{3,1},{4,6},{5,7},{6,4},{7,5},{8,10},{9,11},{10,... | collective-permute-start | bytes 122888 | tf_op jit(solution)/shard_map/ppermute | solution.py:238
  25.5 10.6 %collective-permute-start.12 = (bf16[16,1280]{1,0:T(8,128)(2,1)S(1)}, bf16[16,1280]{1,0:T(8,128)(2,1)S(1)}, u32[]{:S(2)}, u32[]{:S(2)}) collective-permute-start(bf16[16,1280]{1,0:T(8,128)(2,1)S(1)} %add_convert_fusion.1), channel_id=1, source_target_pairs={{0,10},{1,11},{2,8},{3,9},{4,14},{5,15},{6,12},{7,13},{8,2},{9,3},... | collective-permute-start | bytes 122888 | tf_op jit(solution)/shard_map/ppermute | solution.py:238
  32.3 6.1 %collective-permute-start.11 = (bf16[16,1280]{1,0:T(8,128)(2,1)S(1)}, bf16[16,1280]{1,0:T(8,128)(2,1)S(1)}, u32[]{:S(2)}, u32[]{:S(2)}) collective-permute-start(bf16[16,1280]{1,0:T(8,128)(2,1)S(1)} %add_convert_fusion.1), channel_id=1, source_target_pairs={{0,12},{1,13},{2,14},{3,15},{4,8},{5,9},{6,10},{7,11},{8,4},{9,5},... | collective-permute-start | bytes 122888 | tf_op jit(solution)/shard_map/ppermute | solution.py:238
  32.9 5.6 %collective-permute-start.10 = (bf16[16,1280]{1,0:T(8,128)(2,1)S(1)}, bf16[16,1280]{1,0:T(8,128)(2,1)S(1)}, u32[]{:S(2)}, u32[]{:S(2)}) collective-permute-start(bf16[16,1280]{1,0:T(8,128)(2,1)S(1)} %add_convert_fusion.1), channel_id=1, source_target_pairs={{0,4},{1,5},{2,6},{3,7},{4,0},{5,1},{6,2},{7,3},{8,12},{9,13},{10,... | collective-permute-start | bytes 122888 | tf_op jit(solution)/shard_map/ppermute | solution.py:238
  33.8 12.9 %collective-permute-start.4 = (bf16[2,48,2240]{2,1,0:T(8,128)(2,1)S(1)}, bf16[2,48,2240]{2,1,0:T(8,128)(2,1)S(1)}, u32[]{:S(2)}, u32[]{:S(2)}) collective-permute-start(bf16[2,48,2240]{2,1,0:T(8,128)(2,1)S(1)} %get-tuple-element.48), channel_id=1, source_target_pairs={{0,1},{1,0},{2,3},{3,2},{4,5},{5,4},{6,7},{7,6},{8,9},{9,8},{10,11... | collective-permute-start | bytes 1290248 | tf_op jit(solution)/shard_map/ppermute | solution.py:245
  33.8 12.9 %collective-permute-start.5 = (bf16[2,48,2240]{2,1,0:T(8,128)(2,1)S(1)}, bf16[2,48,2240]{2,1,0:T(8,128)(2,1)S(1)}, u32[]{:S(2)}, u32[]{:S(2)}) collective-permute-start(bf16[2,48,2240]{2,1,0:T(8,128)(2,1)S(1)} %get-tuple-element.49), channel_id=1, source_target_pairs={{1,2},{2,1},{3,4},{4,3},{5,6},{6,5},{7,8},{8,7},{9,10},{10,9},{11,... | collective-permute-start | bytes 1290248 | tf_op jit(solution)/shard_map/ppermute | solution.py:245
  34.5 12.2 %copy-start.2 = (bf16[2240,32]{0,1:T(8,128)(2,1)S(1)}, bf16[2240,32]{0,1:T(8,128)(2,1)}, u32[]{:S(2)}) copy-start(bf16[2240,32]{0,1:T(8,128)(2,1)} %param.11) | copy-start | bytes 430084
  34.5 25.2 %copy-start.1 = (bf16[3,3,32,512]{3,2,1,0:T(8,128)(2,1)S(1)}, bf16[3,3,32,512]{3,2,1,0:T(8,128)(2,1)}, u32[]{:S(2)}) copy-start(bf16[3,3,32,512]{3,2,1,0:T(8,128)(2,1)} %param.12) | copy-start | bytes 884740
  34.6 25.2 %copy-start.3 = (f32[512]{0:T(512)S(1)}, f32[512]{0:T(512)}, u32[]{:S(2)}) copy-start(f32[512]{0:T(512)} %param.13) | copy-start | bytes 6148
  38.5 2.8 %collective-permute-start.16 = (bf16[16,1280]{1,0:T(8,128)(2,1)S(1)}, bf16[16,1280]{1,0:T(8,128)(2,1)S(1)}, u32[]{:S(2)}, u32[]{:S(2)}) collective-permute-start(bf16[16,1280]{1,0:T(8,128)(2,1)S(1)} %add_convert_fusion.rest_0_), channel_id=1, source_target_pairs={{0,1},{1,0},{2,3},{3,2},{4,5},{5,4},{6,7},{7,6},{8,9},{9,8},{10,11... | collective-permute-start | bytes 122888 | tf_op jit(solution)/shard_map/ppermute | solution.py:295
  38.6 5.2 %collective-permute-start.15 = (bf16[16,1280]{1,0:T(8,128)(2,1)S(1)}, bf16[16,1280]{1,0:T(8,128)(2,1)S(1)}, u32[]{:S(2)}, u32[]{:S(2)}) collective-permute-start(bf16[16,1280]{1,0:T(8,128)(2,1)S(1)} %add_convert_fusion.rest_0_), channel_id=1, source_target_pairs={{0,48},{16,32},{32,16},{48,0},{64,112},{80,96},{96,80},{112,64},{1... | collective-permute-start | bytes 122888 | tf_op jit(solution)/shard_map/ppermute | solution.py:238
  39.8 5.6 %collective-permute-start.14 = (bf16[16,1280]{1,0:T(8,128)(2,1)S(1)}, bf16[16,1280]{1,0:T(8,128)(2,1)S(1)}, u32[]{:S(2)}, u32[]{:S(2)}) collective-permute-start(bf16[16,1280]{1,0:T(8,128)(2,1)S(1)} %add_convert_fusion.rest_0_), channel_id=1, source_target_pairs={{0,32},{16,48},{32,0},{48,16},{64,96},{80,112},{96,64},{112,80},{1... | collective-permute-start | bytes 122888 | tf_op jit(solution)/shard_map/ppermute | solution.py:238
  41.3 4.0 %collective-permute-start.13 = (bf16[16,1280]{1,0:T(8,128)(2,1)S(1)}, bf16[16,1280]{1,0:T(8,128)(2,1)S(1)}, u32[]{:S(2)}, u32[]{:S(2)}) collective-permute-start(bf16[16,1280]{1,0:T(8,128)(2,1)S(1)} %add_convert_fusion.rest_0_), channel_id=1, source_target_pairs={{0,16},{16,0},{32,48},{48,32},{64,80},{80,64},{96,112},{112,96},{1... | collective-permute-start | bytes 122888 | tf_op jit(solution)/shard_map/ppermute | solution.py:238
  43.9 2.0 %collective-permute-start.19 = (bf16[16,1280]{1,0:T(8,128)(2,1)S(1)}, bf16[16,1280]{1,0:T(8,128)(2,1)S(1)}, u32[]{:S(2)}, u32[]{:S(2)}) collective-permute-start(bf16[16,1280]{1,0:T(8,128)(2,1)S(1)} %collective-permute-done.15.rest_3_), channel_id=1, source_target_pairs={{0,1},{1,0},{2,3},{3,2},{4,5},{5,4},{6,7},{7,6},{8,9},{9,8},{10,11... | collective-permute-start | bytes 122888 | tf_op jit(solution)/shard_map/ppermute | solution.py:295
  45.4 1.2 %collective-permute-start.18 = (bf16[16,1280]{1,0:T(8,128)(2,1)S(1)}, bf16[16,1280]{1,0:T(8,128)(2,1)S(1)}, u32[]{:S(2)}, u32[]{:S(2)}) collective-permute-start(bf16[16,1280]{1,0:T(8,128)(2,1)S(1)} %collective-permute-done.14.rest_2_), channel_id=1, source_target_pairs={{0,1},{1,0},{2,3},{3,2},{4,5},{5,4},{6,7},{7,6},{8,9},{9,8},{10,11... | collective-permute-start | bytes 122888 | tf_op jit(solution)/shard_map/ppermute | solution.py:295
  45.4 1.4 %collective-permute-start.17 = (bf16[16,1280]{1,0:T(8,128)(2,1)S(1)}, bf16[16,1280]{1,0:T(8,128)(2,1)S(1)}, u32[]{:S(2)}, u32[]{:S(2)}) collective-permute-start(bf16[16,1280]{1,0:T(8,128)(2,1)S(1)} %collective-permute-done.13.rest_1_), channel_id=1, source_target_pairs={{0,1},{1,0},{2,3},{3,2},{4,5},{5,4},{6,7},{7,6},{8,9},{9,8},{10,11... | collective-permute-start | bytes 122888 | tf_op jit(solution)/shard_map/ppermute | solution.py:295
  49.8 5.1 %collective-permute-start.20 = (f32[6,32,32]{2,1,0:T(8,128)S(1)}, f32[6,32,32]{2,1,0:T(8,128)S(1)}, u32[]{:S(2)}, u32[]{:S(2)}) collective-permute-start(f32[6,32,32]{2,1,0:T(8,128)S(1)} %get-tuple-element.61), channel_id=1, source_target_pairs={{0,16},{16,0},{32,48},{48,32},{64,80},{80,64},{96,112},{112,96},{1... | collective-permute-start | bytes 73736 | tf_op jit(solution)/shard_map/ppermute | solution.py:245
  51.1 8.6 %collective-permute-start.21 = (f32[6,32,32]{2,1,0:T(8,128)S(1)}, f32[6,32,32]{2,1,0:T(8,128)S(1)}, u32[]{:S(2)}, u32[]{:S(2)}) collective-permute-start(f32[6,32,32]{2,1,0:T(8,128)S(1)} %get-tuple-element.62), channel_id=1, source_target_pairs={{16,32},{32,16},{48,64},{64,48},{80,96},{96,80},{112,128},{128,112... | collective-permute-start | bytes 73736 | tf_op jit(solution)/shard_map/ppermute | solution.py:245

commit v6 on v5

--- a/solution.py
+++ b/solution.py
@@ -199,8 +199,8 @@
             at += edge
             out_ref[line, WIDE + tile : 2 * WIDE + tile] = normed[at : at + WIDE]
     out_ref[:, 2 * WIDE + tile :] = jnp.zeros((images * tile, 10, weight_ref.shape[0]), f32)
-    first = out_ref[: images * WIDE]
-    last = out_ref[images * (tile - WIDE) :]
+    first = out_ref[: images * WIDE].astype(bf16)
+    last = out_ref[images * (tile - WIDE) :].astype(bf16)
     near_out_ref[...] = jnp.where(odd_row, first, last)
     far_out_ref[...] = jnp.where(odd_row, last, first)
 
@@ -212,7 +212,8 @@
     return pl.pallas_call(
         attend_kernel,
         out_shape=[
-            jax.ShapeDtypeStruct((images * lines, 32, channels), jnp.float32) for lines in (16, WIDE, WIDE)
+            jax.ShapeDtypeStruct((images * lines, 32, channels), kind)
+            for lines, kind in ((16, jnp.float32), (WIDE, jnp.bfloat16), (WIDE, jnp.bfloat16))
         ],
         in_specs=[vmem] * 12,
         out_specs=[vmem] * 3,
@@ -323,12 +324,12 @@
 
     for i in range(2 * (tile + 6)):
         if i < 2 * WIDE:
-            line = jnp.where(odd, near_ref[i], far_ref[i])
+            line = jnp.where(odd, near_ref[i], far_ref[i]).astype(f32)
         elif i < 2 * (tile + WIDE):
             line = lat_ref[i - 2 * WIDE]
         else:
             line = i - 2 * (tile + WIDE)
-            line = jnp.where(odd, far_ref[line], near_ref[line])
+            line = jnp.where(odd, far_ref[line], near_ref[line]).astype(f32)
         block = [line[dx : dx + pitch] for dx in range(3)]
         wide[pitch * i : pitch * (i + 1)] = jnp.concatenate(block, axis=1).astype(bf16)
 

time: 68.5 us -> 68 us (level)
  no operation moved by 1% of the time
where the time goes in v6:
time: 68 us; the launch traced here: 67.8 us
  starting transfers between devices  27.6 us (41%)
  waiting for transfers between devices  21.8 us (32%)
  Pallas kernels  17.9 us (26%)
    ppermute x10, starting transfers between devices, sent(): return [lax.ppermute(value, axis, xor_pairs(d)) for d in distances]  18 us
    ppermute x10, waiting for transfers between devices, sent(): return [lax.ppermute(value, axis, xor_pairs(d)) for d in distances]  9.91 us
    pallas_call x1, Pallas kernels, decode(): pl.pallas_call(functools.partial(decode_kernel, tiles), out_shape=jax.Sha...  8.47 us
    ppermute x4, waiting for transfers between devices, swapped(): return (lax.ppermute(even, axis, near), lax.ppermute(odd, axis, far))  5.54 us
    ppermute x3, waiting for transfers between devices, gather_all(): lax.ppermute(part, 'row', xor_pairs(d))  4.87 us
    ppermute x4, starting transfers between devices, swapped(): return (lax.ppermute(even, axis, near), lax.ppermute(odd, axis, far))  4.55 us
    ppermute x3, starting transfers between devices, gather_all(): lax.ppermute(part, 'row', xor_pairs(d))  4.31 us
    pallas_call x1, Pallas kernels, image_sums(): pl.pallas_call(functools.partial(sums_kernel, scale), out_shape=[out, out...  3.1 us
  transfers between devices with their start and end apart: 22, of which 14 were waited for; matrix products, arithmetic and copies ran while one was open for 0% of the time, Pallas kernels for 5%

profile of v6, /device:TPU:24, one launch (start us, length us, event | category | flops | bytes accessed | tf_op | source)
XLA Modules:
  0.0 67.8 jit_solution(6073618911335883689)
XLA Ops:
  0.0 3.1 %image_sums.1 = (bf16[4,16,1280]{2,1,0:T(8,128)(2,1)S(1)}, bf16[4,16,1280]{2,1,0:T(8,128)(2,1)S(1)}) custom-call(bf16[2,256,2240]{2,1,0:T(8,128)(2,1)} %bitcast.20, bf16[2,256,2240]{2,1,0:T(8,128)(2,1)} %bitcast.21), custom_call_target="tpu_custom_call" | custom-call | flops 587202560 | bytes 4587520 | tf_op jit(solution)/shard_map/image_sums/pallas_call | solution.py:74
  3.2 0.7 %sides.1 = (bf16[2,48,2240]{2,1,0:T(8,128)(2,1)S(1)}, bf16[2,48,2240]{2,1,0:T(8,128)(2,1)S(1)}) custom-call(bf16[2,256,2240]{2,1,0:T(8,128)(2,1)S(1)} %bitcast.15), custom_call_target="tpu_custom_call" | custom-call | flops 1000000000 | bytes 3440640 | tf_op jit(solution)/shard_map/sides/pallas_call | solution.py:111
  4.0 0.6 collective-permute-done.arrived_ref
  4.6 1.6 %collective-permute-start.1 = (bf16[16,1280]{1,0:T(8,128)(2,1)S(1)}, bf16[16,1280]{1,0:T(8,128)(2,1)S(1)}, u32[]{:S(2)}, u32[]{:S(2)}) collective-permute-start(bf16[16,1280]{1,0:T(8,128)(2,1)S(1)} %get-tuple-element.43), channel_id=1, source_target_pairs={{0,16},{16,0},{32,48},{48,32},{64,80},{80,64},{96,112},{112,96},{1... | collective-permute-start | bytes 122888 | tf_op jit(solution)/shard_map/ppermute | solution.py:279
  6.2 2.1 %collective-permute-start.2 = (bf16[16,1280]{1,0:T(8,128)(2,1)S(1)}, bf16[16,1280]{1,0:T(8,128)(2,1)S(1)}, u32[]{:S(2)}, u32[]{:S(2)}) collective-permute-start(bf16[16,1280]{1,0:T(8,128)(2,1)S(1)} %get-tuple-element.44), channel_id=1, source_target_pairs={{0,48},{16,32},{32,16},{48,0},{64,112},{80,96},{96,80},{112,64},{1... | collective-permute-start | bytes 122888 | tf_op jit(solution)/shard_map/ppermute | solution.py:279
  8.3 0.6 collective-permute-start.3
  9.0 2.5 %collective-permute-done.2 = bf16[16,1280]{1,0:T(8,128)(2,1)S(1)} collective-permute-done((bf16[16,1280]{1,0:T(8,128)(2,1)S(1)}, bf16[16,1280]{1,0:T(8,128)(2,1)S(1)}, u32[]{:S(2)}, u32[]{:S(2)}) %collective-permute-start.2) | collective-permute-done | bytes 40992 | tf_op jit(solution)/shard_map/ppermute | solution.py:279
  11.4 2.4 %collective-permute-done.3 = bf16[16,1280]{1,0:T(8,128)(2,1)S(1)} collective-permute-done((bf16[16,1280]{1,0:T(8,128)(2,1)S(1)}, bf16[16,1280]{1,0:T(8,128)(2,1)S(1)}, u32[]{:S(2)}, u32[]{:S(2)}) %collective-permute-start.3) | collective-permute-done | bytes 40992 | tf_op jit(solution)/shard_map/ppermute | solution.py:279
  13.9 1.3 %collective-permute-start.8 = (bf16[16,1280]{1,0:T(8,128)(2,1)S(1)}, bf16[16,1280]{1,0:T(8,128)(2,1)S(1)}, u32[]{:S(2)}, u32[]{:S(2)}) collective-permute-start(bf16[16,1280]{1,0:T(8,128)(2,1)S(1)} %add_convert_fusion.3), channel_id=1, source_target_pairs={{0,128},{16,144},{32,160},{48,176},{64,192},{80,208},{96,224},{112... | collective-permute-start | bytes 122888 | tf_op jit(solution)/shard_map/ppermute | solution.py:239
  15.2 2.2 %collective-permute-start.7 = (bf16[16,1280]{1,0:T(8,128)(2,1)S(1)}, bf16[16,1280]{1,0:T(8,128)(2,1)S(1)}, u32[]{:S(2)}, u32[]{:S(2)}) collective-permute-start(bf16[16,1280]{1,0:T(8,128)(2,1)S(1)} %add_convert_fusion.3), channel_id=1, source_target_pairs={{0,192},{16,208},{32,224},{48,240},{64,128},{80,144},{96,160},{112... | collective-permute-start | bytes 122888 | tf_op jit(solution)/shard_map/ppermute | solution.py:239
  17.5 1.0 %keep.1.residual_ref = bf16[4608,512]{1,0:T(8,128)(2,1)S(1)} custom-call(bf16[4608,512]{1,0:T(8,128)(2,1)S(1)} %bitcast.11), custom_call_target="tpu_custom_call" | custom-call | bytes 4718592 | tf_op jit(solution)/shard_map/keep/pallas_call | solution.py:441
  18.5 1.0 %collective-permute-done.8 = bf16[16,1280]{1,0:T(8,128)(2,1)S(1)} collective-permute-done((bf16[16,1280]{1,0:T(8,128)(2,1)S(1)}, bf16[16,1280]{1,0:T(8,128)(2,1)S(1)}, u32[]{:S(2)}, u32[]{:S(2)}) %collective-permute-start.8) | collective-permute-done | bytes 40992 | tf_op jit(solution)/shard_map/ppermute | solution.py:239
  19.5 0.9 %collective-permute-done.7 = bf16[16,1280]{1,0:T(8,128)(2,1)S(1)} collective-permute-done((bf16[16,1280]{1,0:T(8,128)(2,1)S(1)}, bf16[16,1280]{1,0:T(8,128)(2,1)S(1)}, u32[]{:S(2)}, u32[]{:S(2)}) %collective-permute-start.7) | collective-permute-done | bytes 40992 | tf_op jit(solution)/shard_map/ppermute | solution.py:239
  20.4 1.0 %collective-permute-done.6 = bf16[16,1280]{1,0:T(8,128)(2,1)S(1)} collective-permute-done((bf16[16,1280]{1,0:T(8,128)(2,1)S(1)}, bf16[16,1280]{1,0:T(8,128)(2,1)S(1)}, u32[]{:S(2)}, u32[]{:S(2)}) %collective-permute-start.6) | collective-permute-done | bytes 40992 | tf_op jit(solution)/shard_map/ppermute | solution.py:239
  21.4 2.0 %collective-permute-start.9 = (bf16[16,1280]{1,0:T(8,128)(2,1)S(1)}, bf16[16,1280]{1,0:T(8,128)(2,1)S(1)}, u32[]{:S(2)}, u32[]{:S(2)}) collective-permute-start(bf16[16,1280]{1,0:T(8,128)(2,1)S(1)} %add_convert_fusion.2), channel_id=1, source_target_pairs={{0,2},{1,3},{2,0},{3,1},{4,6},{5,7},{6,4},{7,5},{8,10},{9,11},{10,... | collective-permute-start | bytes 122888 | tf_op jit(solution)/shard_map/ppermute | solution.py:239
  23.4 2.1 %collective-permute-done.9 = bf16[16,1280]{1,0:T(8,128)(2,1)S(1)} collective-permute-done((bf16[16,1280]{1,0:T(8,128)(2,1)S(1)}, bf16[16,1280]{1,0:T(8,128)(2,1)S(1)}, u32[]{:S(2)}, u32[]{:S(2)}) %collective-permute-start.9) | collective-permute-done | bytes 40992 | tf_op jit(solution)/shard_map/ppermute | solution.py:239
  25.5 6.8 %collective-permute-start.12 = (bf16[16,1280]{1,0:T(8,128)(2,1)S(1)}, bf16[16,1280]{1,0:T(8,128)(2,1)S(1)}, u32[]{:S(2)}, u32[]{:S(2)}) collective-permute-start(bf16[16,1280]{1,0:T(8,128)(2,1)S(1)} %add_convert_fusion.1), channel_id=1, source_target_pairs={{0,10},{1,11},{2,8},{3,9},{4,14},{5,15},{6,12},{7,13},{8,2},{9,3},... | collective-permute-start | bytes 122888 | tf_op jit(solution)/shard_map/ppermute | solution.py:239
  32.9 0.9 %collective-permute-start.10 = (bf16[16,1280]{1,0:T(8,128)(2,1)S(1)}, bf16[16,1280]{1,0:T(8,128)(2,1)S(1)}, u32[]{:S(2)}, u32[]{:S(2)}) collective-permute-start(bf16[16,1280]{1,0:T(8,128)(2,1)S(1)} %add_convert_fusion.1), channel_id=1, source_target_pairs={{0,4},{1,5},{2,6},{3,7},{4,0},{5,1},{6,2},{7,3},{8,12},{9,13},{10,... | collective-permute-start | bytes 122888 | tf_op jit(solution)/shard_map/ppermute | solution.py:239
  33.8 0.7 collective-permute-start.5
  34.6 1.6 %phases.1.upscale_ref = bf16[9,512,512]{2,1,0:T(8,128)(2,1)S(1)} custom-call(bf16[9,512,512]{2,1,0:T(8,128)(2,1)S(1)} %bitcast.14), custom_call_target="tpu_custom_call" | custom-call | flops 2621440 | bytes 4718592 | tf_op jit(solution)/shard_map/phases/pallas_call | solution.py:478
  36.2 2.3 %collective-permute-done.11 = bf16[16,1280]{1,0:T(8,128)(2,1)S(1)} collective-permute-done((bf16[16,1280]{1,0:T(8,128)(2,1)S(1)}, bf16[16,1280]{1,0:T(8,128)(2,1)S(1)}, u32[]{:S(2)}, u32[]{:S(2)}) %collective-permute-start.11) | collective-permute-done | bytes 40992 | tf_op jit(solution)/shard_map/ppermute | solution.py:239
  38.6 1.2 %collective-permute-start.15 = (bf16[16,1280]{1,0:T(8,128)(2,1)S(1)}, bf16[16,1280]{1,0:T(8,128)(2,1)S(1)}, u32[]{:S(2)}, u32[]{:S(2)}) collective-permute-start(bf16[16,1280]{1,0:T(8,128)(2,1)S(1)} %add_convert_fusion.rest_0_), channel_id=1, source_target_pairs={{0,48},{16,32},{32,16},{48,0},{64,112},{80,96},{96,80},{112,64},{1... | collective-permute-start | bytes 122888 | tf_op jit(solution)/shard_map/ppermute | solution.py:239
  39.8 1.5 %collective-permute-start.14 = (bf16[16,1280]{1,0:T(8,128)(2,1)S(1)}, bf16[16,1280]{1,0:T(8,128)(2,1)S(1)}, u32[]{:S(2)}, u32[]{:S(2)}) collective-permute-start(bf16[16,1280]{1,0:T(8,128)(2,1)S(1)} %add_convert_fusion.rest_0_), channel_id=1, source_target_pairs={{0,32},{16,48},{32,0},{48,16},{64,96},{80,112},{96,64},{112,80},{1... | collective-permute-start | bytes 122888 | tf_op jit(solution)/shard_map/ppermute | solution.py:239
  41.3 1.4 %collective-permute-start.13 = (bf16[16,1280]{1,0:T(8,128)(2,1)S(1)}, bf16[16,1280]{1,0:T(8,128)(2,1)S(1)}, u32[]{:S(2)}, u32[]{:S(2)}) collective-permute-start(bf16[16,1280]{1,0:T(8,128)(2,1)S(1)} %add_convert_fusion.rest_0_), channel_id=1, source_target_pairs={{0,16},{16,0},{32,48},{48,32},{64,80},{80,64},{96,112},{112,96},{1... | collective-permute-start | bytes 122888 | tf_op jit(solution)/shard_map/ppermute | solution.py:239
  42.8 1.1 %collective-permute-done.15.rest_3_ = bf16[16,1280]{1,0:T(8,128)(2,1)S(1)} collective-permute-done((bf16[16,1280]{1,0:T(8,128)(2,1)S(1)}, bf16[16,1280]{1,0:T(8,128)(2,1)S(1)}, u32[]{:S(2)}, u32[]{:S(2)}) %collective-permute-start.15) | collective-permute-done | bytes 40992 | tf_op jit(solution)/shard_map/ppermute | solution.py:239
  43.9 1.5 %collective-permute-done.14.rest_2_ = bf16[16,1280]{1,0:T(8,128)(2,1)S(1)} collective-permute-done((bf16[16,1280]{1,0:T(8,128)(2,1)S(1)}, bf16[16,1280]{1,0:T(8,128)(2,1)S(1)}, u32[]{:S(2)}, u32[]{:S(2)}) %collective-permute-start.14) | collective-permute-done | bytes 40992 | tf_op jit(solution)/shard_map/ppermute | solution.py:239
  45.9 0.7 %collective-permute-done.18.rest_6_ = bf16[16,1280]{1,0:T(8,128)(2,1)S(1)} collective-permute-done((bf16[16,1280]{1,0:T(8,128)(2,1)S(1)}, bf16[16,1280]{1,0:T(8,128)(2,1)S(1)}, u32[]{:S(2)}, u32[]{:S(2)}) %collective-permute-start.18) | collective-permute-done | bytes 40992 | tf_op jit(solution)/shard_map/ppermute | solution.py:296
  46.8 3.0 %attend.1 = (f32[32,32,32]{2,1,0:T(8,128)S(1)}, bf16[6,32,32]{2,1,0:T(8,128)(2,1)S(1)}, bf16[6,32,32]{2,1,0:T(8,128)(2,1)S(1)}) custom-call(bf16[2,256,2240]{2,1,0:T(8,128)(2,1)S(1)} %bitcast.16, bf16[2,48,2240]{2,1,0:T(8,128)(2,1)S(1)} %collective-permute-done.4.near_ref, bf16[2,48,2240]{2,1,0:T(8,128)(2,1)S(1)} %collective-permute-done.5.far_ref, ...), custom_call_target="tpu_custom_call" | custom-call | flops 1174405120 | bytes 2293760 | tf_op jit(solution)/shard_map/attend/pallas_call | solution.py:212
  49.8 1.3 %collective-permute-start.20 = (bf16[6,32,32]{2,1,0:T(8,128)(2,1)S(1)}, bf16[6,32,32]{2,1,0:T(8,128)(2,1)S(1)}, u32[]{:S(2)}, u32[]{:S(2)}) collective-permute-start(bf16[6,32,32]{2,1,0:T(8,128)(2,1)S(1)} %get-tuple-element.61), channel_id=1, source_target_pairs={{0,16},{16,0},{32,48},{48,32},{64,80},{80,64},{96,112},{112,96},{1... | collective-permute-start | bytes 36872 | tf_op jit(solution)/shard_map/ppermute | solution.py:246
  51.1 2.5 %collective-permute-start.21 = (bf16[6,32,32]{2,1,0:T(8,128)(2,1)S(1)}, bf16[6,32,32]{2,1,0:T(8,128)(2,1)S(1)}, u32[]{:S(2)}, u32[]{:S(2)}) collective-permute-start(bf16[6,32,32]{2,1,0:T(8,128)(2,1)S(1)} %get-tuple-element.62), channel_id=1, source_target_pairs={{16,32},{32,16},{48,64},{64,48},{80,96},{96,80},{112,128},{128,112... | collective-permute-start | bytes 36872 | tf_op jit(solution)/shard_map/ppermute | solution.py:246
  54.0 5.2 %collective-permute-done.21.far_ref = bf16[6,32,32]{2,1,0:T(8,128)(2,1)S(1)} collective-permute-done((bf16[6,32,32]{2,1,0:T(8,128)(2,1)S(1)}, bf16[6,32,32]{2,1,0:T(8,128)(2,1)S(1)}, u32[]{:S(2)}, u32[]{:S(2)}) %collective-permute-start.21) | collective-permute-done | bytes 12320 | tf_op jit(solution)/shard_map/ppermute | solution.py:246
  59.2 8.5 %decode.1 = bf16[2,16,2,32,512]{4,3,2,1,0:T(8,128)(2,1)} custom-call(f32[32,32,32]{2,1,0:T(8,128)S(1)} %get-tuple-element.60.lat_ref, bf16[6,32,32]{2,1,0:T(8,128)(2,1)S(1)} %collective-permute-done.20.near_ref, bf16[6,32,32]{2,1,0:T(8,128)(2,1)S(1)} %collective-permute-done.21.far_ref, bf16[3,96,512]{2,1,0:T(8,128)(2,1)S(1)} %bitcast.17, ...), custom_call_target="tpu_custom_call" | custom-call | flops 8000000000 | bytes 12582912 | tf_op jit(solution)/shard_map/decode/pallas_call | solution.py:501
  (41 shorter events, 2.0 us)
Async XLA Ops:
  0.0 3.2 %copy-start = (bf16[2,16,16,2240]{3,2,1,0:T(8,128)(2,1)S(1)}, bf16[2,16,16,2240]{3,2,1,0:T(8,128)(2,1)}, u32[]{:S(2)}) copy-start(bf16[2,16,16,2240]{3,2,1,0:T(8,128)(2,1)} %param.8) | copy-start | bytes 6881284
  0.0 17.4 %slice-start = ((s8[4718592]{0:T(1024)(128)(4,1)}), s8[4194304]{0:T(1024)(128)(4,1)S(1)}, s32[]{:S(2)}) async-start(s8[4718592]{0:T(1024)(128)(4,1)} %bitcast.9), calls=%async_computation | async-start | bytes 8388608
  0.0 17.4 %slice-start.1 = ((s8[4718592]{0:T(1024)(128)(4,1)}), s8[524288]{0:T(1024)(128)(4,1)S(1)}, s32[]{:S(2)}) async-start(s8[4718592]{0:T(1024)(128)(4,1)} %bitcast.9), calls=%async_computation.1 | async-start | bytes 1048576
  3.1 1.5 %collective-permute-start = (bf16[4,16,1280]{2,1,0:T(8,128)(2,1)S(1)}, bf16[4,16,1280]{2,1,0:T(8,128)(2,1)S(1)}, u32[]{:S(2)}, u32[]{:S(2)}) collective-permute-start(bf16[4,16,1280]{2,1,0:T(8,128)(2,1)S(1)} %get-tuple-element.37), channel_id=1, source_target_pairs={{0,1},{1,0},{2,3},{3,2},{4,5},{5,4},{6,7},{7,6},{8,9},{9,8},{10,11... | collective-permute-start | bytes 491528 | tf_op jit(solution)/shard_map/ppermute | solution.py:274
  4.6 4.3 %collective-permute-start.1 = (bf16[16,1280]{1,0:T(8,128)(2,1)S(1)}, bf16[16,1280]{1,0:T(8,128)(2,1)S(1)}, u32[]{:S(2)}, u32[]{:S(2)}) collective-permute-start(bf16[16,1280]{1,0:T(8,128)(2,1)S(1)} %get-tuple-element.43), channel_id=1, source_target_pairs={{0,16},{16,0},{32,48},{48,32},{64,80},{80,64},{96,112},{112,96},{1... | collective-permute-start | bytes 122888 | tf_op jit(solution)/shard_map/ppermute | solution.py:279
  6.2 5.2 %collective-permute-start.2 = (bf16[16,1280]{1,0:T(8,128)(2,1)S(1)}, bf16[16,1280]{1,0:T(8,128)(2,1)S(1)}, u32[]{:S(2)}, u32[]{:S(2)}) collective-permute-start(bf16[16,1280]{1,0:T(8,128)(2,1)S(1)} %get-tuple-element.44), channel_id=1, source_target_pairs={{0,48},{16,32},{32,16},{48,0},{64,112},{80,96},{96,80},{112,64},{1... | collective-permute-start | bytes 122888 | tf_op jit(solution)/shard_map/ppermute | solution.py:279
  8.3 5.5 %collective-permute-start.3 = (bf16[16,1280]{1,0:T(8,128)(2,1)S(1)}, bf16[16,1280]{1,0:T(8,128)(2,1)S(1)}, u32[]{:S(2)}, u32[]{:S(2)}) collective-permute-start(bf16[16,1280]{1,0:T(8,128)(2,1)S(1)} %get-tuple-element.45), channel_id=1, source_target_pairs={{0,32},{16,48},{32,0},{48,16},{64,96},{80,112},{96,64},{112,80},{1... | collective-permute-start | bytes 122888 | tf_op jit(solution)/shard_map/ppermute | solution.py:279
  13.8 20.7 %slice-start.2 = ((s8[4718592]{0:T(1024)(128)(4,1)}), s8[4194304]{0:T(1024)(128)(4,1)S(1)}, s32[]{:S(2)}) async-start(s8[4718592]{0:T(1024)(128)(4,1)} %bitcast.12), calls=%async_computation.2 | async-start | bytes 8388608
  13.9 20.7 %slice-start.3 = ((s8[4718592]{0:T(1024)(128)(4,1)}), s8[524288]{0:T(1024)(128)(4,1)S(1)}, s32[]{:S(2)}) async-start(s8[4718592]{0:T(1024)(128)(4,1)} %bitcast.12), calls=%async_computation.3 | async-start | bytes 1048576
  13.9 5.6 %collective-permute-start.8 = (bf16[16,1280]{1,0:T(8,128)(2,1)S(1)}, bf16[16,1280]{1,0:T(8,128)(2,1)S(1)}, u32[]{:S(2)}, u32[]{:S(2)}) collective-permute-start(bf16[16,1280]{1,0:T(8,128)(2,1)S(1)} %add_convert_fusion.3), channel_id=1, source_target_pairs={{0,128},{16,144},{32,160},{48,176},{64,192},{80,208},{96,224},{112... | collective-permute-start | bytes 122888 | tf_op jit(solution)/shard_map/ppermute | solution.py:239
  15.2 5.2 %collective-permute-start.7 = (bf16[16,1280]{1,0:T(8,128)(2,1)S(1)}, bf16[16,1280]{1,0:T(8,128)(2,1)S(1)}, u32[]{:S(2)}, u32[]{:S(2)}) collective-permute-start(bf16[16,1280]{1,0:T(8,128)(2,1)S(1)} %add_convert_fusion.3), channel_id=1, source_target_pairs={{0,192},{16,208},{32,224},{48,240},{64,128},{80,144},{96,160},{112... | collective-permute-start | bytes 122888 | tf_op jit(solution)/shard_map/ppermute | solution.py:239
  17.4 4.0 %collective-permute-start.6 = (bf16[16,1280]{1,0:T(8,128)(2,1)S(1)}, bf16[16,1280]{1,0:T(8,128)(2,1)S(1)}, u32[]{:S(2)}, u32[]{:S(2)}) collective-permute-start(bf16[16,1280]{1,0:T(8,128)(2,1)S(1)} %add_convert_fusion.3), channel_id=1, source_target_pairs={{0,64},{16,80},{32,96},{48,112},{64,0},{80,16},{96,32},{112,48},{1... | collective-permute-start | bytes 122888 | tf_op jit(solution)/shard_map/ppermute | solution.py:239
  21.4 4.1 %collective-permute-start.9 = (bf16[16,1280]{1,0:T(8,128)(2,1)S(1)}, bf16[16,1280]{1,0:T(8,128)(2,1)S(1)}, u32[]{:S(2)}, u32[]{:S(2)}) collective-permute-start(bf16[16,1280]{1,0:T(8,128)(2,1)S(1)} %add_convert_fusion.2), channel_id=1, source_target_pairs={{0,2},{1,3},{2,0},{3,1},{4,6},{5,7},{6,4},{7,5},{8,10},{9,11},{10,... | collective-permute-start | bytes 122888 | tf_op jit(solution)/shard_map/ppermute | solution.py:239
  25.5 10.6 %collective-permute-start.12 = (bf16[16,1280]{1,0:T(8,128)(2,1)S(1)}, bf16[16,1280]{1,0:T(8,128)(2,1)S(1)}, u32[]{:S(2)}, u32[]{:S(2)}) collective-permute-start(bf16[16,1280]{1,0:T(8,128)(2,1)S(1)} %add_convert_fusion.1), channel_id=1, source_target_pairs={{0,10},{1,11},{2,8},{3,9},{4,14},{5,15},{6,12},{7,13},{8,2},{9,3},... | collective-permute-start | bytes 122888 | tf_op jit(solution)/shard_map/ppermute | solution.py:239
  32.3 6.1 %collective-permute-start.11 = (bf16[16,1280]{1,0:T(8,128)(2,1)S(1)}, bf16[16,1280]{1,0:T(8,128)(2,1)S(1)}, u32[]{:S(2)}, u32[]{:S(2)}) collective-permute-start(bf16[16,1280]{1,0:T(8,128)(2,1)S(1)} %add_convert_fusion.1), channel_id=1, source_target_pairs={{0,12},{1,13},{2,14},{3,15},{4,8},{5,9},{6,10},{7,11},{8,4},{9,5},... | collective-permute-start | bytes 122888 | tf_op jit(solution)/shard_map/ppermute | solution.py:239
  32.9 5.6 %collective-permute-start.10 = (bf16[16,1280]{1,0:T(8,128)(2,1)S(1)}, bf16[16,1280]{1,0:T(8,128)(2,1)S(1)}, u32[]{:S(2)}, u32[]{:S(2)}) collective-permute-start(bf16[16,1280]{1,0:T(8,128)(2,1)S(1)} %add_convert_fusion.1), channel_id=1, source_target_pairs={{0,4},{1,5},{2,6},{3,7},{4,0},{5,1},{6,2},{7,3},{8,12},{9,13},{10,... | collective-permute-start | bytes 122888 | tf_op jit(solution)/shard_map/ppermute | solution.py:239
  33.8 12.9 %collective-permute-start.4 = (bf16[2,48,2240]{2,1,0:T(8,128)(2,1)S(1)}, bf16[2,48,2240]{2,1,0:T(8,128)(2,1)S(1)}, u32[]{:S(2)}, u32[]{:S(2)}) collective-permute-start(bf16[2,48,2240]{2,1,0:T(8,128)(2,1)S(1)} %get-tuple-element.48), channel_id=1, source_target_pairs={{0,1},{1,0},{2,3},{3,2},{4,5},{5,4},{6,7},{7,6},{8,9},{9,8},{10,11... | collective-permute-start | bytes 1290248 | tf_op jit(solution)/shard_map/ppermute | solution.py:246
  33.8 12.9 %collective-permute-start.5 = (bf16[2,48,2240]{2,1,0:T(8,128)(2,1)S(1)}, bf16[2,48,2240]{2,1,0:T(8,128)(2,1)S(1)}, u32[]{:S(2)}, u32[]{:S(2)}) collective-permute-start(bf16[2,48,2240]{2,1,0:T(8,128)(2,1)S(1)} %get-tuple-element.49), channel_id=1, source_target_pairs={{1,2},{2,1},{3,4},{4,3},{5,6},{6,5},{7,8},{8,7},{9,10},{10,9},{11,... | collective-permute-start | bytes 1290248 | tf_op jit(solution)/shard_map/ppermute | solution.py:246
  34.5 12.2 %copy-start.2 = (bf16[2240,32]{0,1:T(8,128)(2,1)S(1)}, bf16[2240,32]{0,1:T(8,128)(2,1)}, u32[]{:S(2)}) copy-start(bf16[2240,32]{0,1:T(8,128)(2,1)} %param.11) | copy-start | bytes 430084
  34.5 24.7 %copy-start.1 = (bf16[3,3,32,512]{3,2,1,0:T(8,128)(2,1)S(1)}, bf16[3,3,32,512]{3,2,1,0:T(8,128)(2,1)}, u32[]{:S(2)}) copy-start(bf16[3,3,32,512]{3,2,1,0:T(8,128)(2,1)} %param.12) | copy-start | bytes 884740
  34.6 24.6 %copy-start.3 = (f32[512]{0:T(512)S(1)}, f32[512]{0:T(512)}, u32[]{:S(2)}) copy-start(f32[512]{0:T(512)} %param.13) | copy-start | bytes 6148
  38.5 2.8 %collective-permute-start.16 = (bf16[16,1280]{1,0:T(8,128)(2,1)S(1)}, bf16[16,1280]{1,0:T(8,128)(2,1)S(1)}, u32[]{:S(2)}, u32[]{:S(2)}) collective-permute-start(bf16[16,1280]{1,0:T(8,128)(2,1)S(1)} %add_convert_fusion.rest_0_), channel_id=1, source_target_pairs={{0,1},{1,0},{2,3},{3,2},{4,5},{5,4},{6,7},{7,6},{8,9},{9,8},{10,11... | collective-permute-start | bytes 122888 | tf_op jit(solution)/shard_map/ppermute | solution.py:296
  38.6 5.2 %collective-permute-start.15 = (bf16[16,1280]{1,0:T(8,128)(2,1)S(1)}, bf16[16,1280]{1,0:T(8,128)(2,1)S(1)}, u32[]{:S(2)}, u32[]{:S(2)}) collective-permute-start(bf16[16,1280]{1,0:T(8,128)(2,1)S(1)} %add_convert_fusion.rest_0_), channel_id=1, source_target_pairs={{0,48},{16,32},{32,16},{48,0},{64,112},{80,96},{96,80},{112,64},{1... | collective-permute-start | bytes 122888 | tf_op jit(solution)/shard_map/ppermute | solution.py:239
  39.8 5.6 %collective-permute-start.14 = (bf16[16,1280]{1,0:T(8,128)(2,1)S(1)}, bf16[16,1280]{1,0:T(8,128)(2,1)S(1)}, u32[]{:S(2)}, u32[]{:S(2)}) collective-permute-start(bf16[16,1280]{1,0:T(8,128)(2,1)S(1)} %add_convert_fusion.rest_0_), channel_id=1, source_target_pairs={{0,32},{16,48},{32,0},{48,16},{64,96},{80,112},{96,64},{112,80},{1... | collective-permute-start | bytes 122888 | tf_op jit(solution)/shard_map/ppermute | solution.py:239
  41.3 4.0 %collective-permute-start.13 = (bf16[16,1280]{1,0:T(8,128)(2,1)S(1)}, bf16[16,1280]{1,0:T(8,128)(2,1)S(1)}, u32[]{:S(2)}, u32[]{:S(2)}) collective-permute-start(bf16[16,1280]{1,0:T(8,128)(2,1)S(1)} %add_convert_fusion.rest_0_), channel_id=1, source_target_pairs={{0,16},{16,0},{32,48},{48,32},{64,80},{80,64},{96,112},{112,96},{1... | collective-permute-start | bytes 122888 | tf_op jit(solution)/shard_map/ppermute | solution.py:239
  43.9 2.0 %collective-permute-start.19 = (bf16[16,1280]{1,0:T(8,128)(2,1)S(1)}, bf16[16,1280]{1,0:T(8,128)(2,1)S(1)}, u32[]{:S(2)}, u32[]{:S(2)}) collective-permute-start(bf16[16,1280]{1,0:T(8,128)(2,1)S(1)} %collective-permute-done.15.rest_3_), channel_id=1, source_target_pairs={{0,1},{1,0},{2,3},{3,2},{4,5},{5,4},{6,7},{7,6},{8,9},{9,8},{10,11... | collective-permute-start | bytes 122888 | tf_op jit(solution)/shard_map/ppermute | solution.py:296
  45.4 1.2 %collective-permute-start.18 = (bf16[16,1280]{1,0:T(8,128)(2,1)S(1)}, bf16[16,1280]{1,0:T(8,128)(2,1)S(1)}, u32[]{:S(2)}, u32[]{:S(2)}) collective-permute-start(bf16[16,1280]{1,0:T(8,128)(2,1)S(1)} %collective-permute-done.14.rest_2_), channel_id=1, source_target_pairs={{0,1},{1,0},{2,3},{3,2},{4,5},{5,4},{6,7},{7,6},{8,9},{9,8},{10,11... | collective-permute-start | bytes 122888 | tf_op jit(solution)/shard_map/ppermute | solution.py:296
  45.4 1.4 %collective-permute-start.17 = (bf16[16,1280]{1,0:T(8,128)(2,1)S(1)}, bf16[16,1280]{1,0:T(8,128)(2,1)S(1)}, u32[]{:S(2)}, u32[]{:S(2)}) collective-permute-start(bf16[16,1280]{1,0:T(8,128)(2,1)S(1)} %collective-permute-done.13.rest_1_), channel_id=1, source_target_pairs={{0,1},{1,0},{2,3},{3,2},{4,5},{5,4},{6,7},{7,6},{8,9},{9,8},{10,11... | collective-permute-start | bytes 122888 | tf_op jit(solution)/shard_map/ppermute | solution.py:296
  49.8 4.2 %collective-permute-start.20 = (bf16[6,32,32]{2,1,0:T(8,128)(2,1)S(1)}, bf16[6,32,32]{2,1,0:T(8,128)(2,1)S(1)}, u32[]{:S(2)}, u32[]{:S(2)}) collective-permute-start(bf16[6,32,32]{2,1,0:T(8,128)(2,1)S(1)} %get-tuple-element.61), channel_id=1, source_target_pairs={{0,16},{16,0},{32,48},{48,32},{64,80},{80,64},{96,112},{112,96},{1... | collective-permute-start | bytes 36872 | tf_op jit(solution)/shard_map/ppermute | solution.py:246
  51.1 8.1 %collective-permute-start.21 = (bf16[6,32,32]{2,1,0:T(8,128)(2,1)S(1)}, bf16[6,32,32]{2,1,0:T(8,128)(2,1)S(1)}, u32[]{:S(2)}, u32[]{:S(2)}) collective-permute-start(bf16[6,32,32]{2,1,0:T(8,128)(2,1)S(1)} %get-tuple-element.62), channel_id=1, source_target_pairs={{16,32},{32,16},{48,64},{64,48},{80,96},{96,80},{112,128},{128,112... | collective-permute-start | bytes 36872 | tf_op jit(solution)/shard_map/ppermute | solution.py:246
